TPU v7x, 512 devices: a whole 4x8x8 slice. The times are simulated.
512 devices in a mesh: dp: 32 (over x, z), table: 16 (over y, core).
Axes of the slice: x: 4, y: 8, z: 8, core: 2. Of those that a mesh axis runs over, the one named last changes fastest.
Arguments:
- dense_feats: bfloat16 [65536, 13], P(('dp', 'table')), may hold values from -6 to 6
- lookup_ids: int32 [32, 8, 65536], P('table', None, 'dp'), may hold values from 0 to 2047
- lookup_counts: int32 [32, 65536], P('table', 'dp'), may hold values from 0 to 8
- shard_table: int32 [32], replicated, may hold values from 0 to 25, as said below
- embed_tables: bfloat16 [32, 2048, 128], P('table'), may hold values from -6 to 6
- first_layer: bfloat16 [13, 512], replicated, may hold values from -1.75 to 1.75
- first_offset: float32 [512], replicated, may hold values from -3 to 3
- second_layer: bfloat16 [512, 256], replicated, may hold values from -0.25 to 0.25
- second_offset: float32 [256], replicated, may hold values from -3 to 3
- third_layer: bfloat16 [256, 128], replicated, may hold values from -0.375 to 0.375
- third_offset: float32 [128], replicated, may hold values from -3 to 3
- cross_down: bfloat16 [3456, 512], P(None, 'table'), may hold values from -0.109375 to 0.109375
- cross_up: bfloat16 [512, 3456], P('table'), may hold values from -0.25 to 0.25
- cross_bias: float32 [3456], replicated, may hold values from -3 to 3
- cotangent: bfloat16 [65536, 3456], P(('dp', 'table')), may hold values from -0.059814453 to 0.059814453
Outputs:
- table_grad: float32 [32, 2048, 128], P('table', 'dp')
- first_layer_grad: float32 [13, 512], replicated
- first_offset_grad: float32 [512], replicated
- second_layer_grad: float32 [512, 256], replicated
- second_offset_grad: float32 [256], replicated
- third_layer_grad: float32 [256, 128], replicated
- third_offset_grad: float32 [128], replicated
- cross_bias_grad: float32 [3456], replicated
Inputs may be any that keep to these rules, and one draw needn't show every extreme that they name: `shard_table`: every table has at least one shard.
All inputs are finite; a program needn't handle non-finite values.
Results may differ from a plain program's by a relative error of at most 0.0085.
Values may be sent and summed in bfloat16 or wider, within the bound.
No kernel may reach another device: no remote copies, remote signals or barrier semaphores. Data moves between devices by JAX's collectives and lax.ppermute only.
A program may use at most 64 MiB of HBM per device.

v0:
```python
import math

import jax
import jax.numpy as jnp
from jax import lax
from jax.sharding import PartitionSpec as P

TABLES = 26


def silu_slope(value):
    sigmoid = 1.0 / (1.0 + jnp.exp(-value))
    return sigmoid * (1.0 + value * (1.0 - sigmoid))


def hit_counts(index_block, count_block, row_total):
    iota_rows = lax.broadcasted_iota(jnp.int32, (index_block.shape[1], row_total), 1)
    totals = jnp.zeros((index_block.shape[1], row_total), jnp.bfloat16)
    for slot_index in range(index_block.shape[0]):
        matched = (index_block[slot_index][:, None] == iota_rows) & (
            count_block[:, None] > slot_index
        )
        totals = totals + matched.astype(jnp.bfloat16)
    return totals


def split_blocks(shard_index, shard_count, block_size):
    hot_total, batch_total = shard_index.shape
    blocks = batch_total // block_size
    index_blocks = shard_index.reshape(hot_total, blocks, block_size).transpose(1, 0, 2)
    count_blocks = shard_count.reshape(blocks, block_size)
    return (index_blocks, count_blocks, blocks)


def pool_shard(table_rows, shard_index, shard_count, block_size):
    index_blocks, count_blocks, blocks = split_blocks(shard_index, shard_count, block_size)

    def pool_one_block(inputs):
        hit_table = hit_counts(inputs[0], inputs[1], table_rows.shape[0])
        return jnp.dot(hit_table, table_rows, preferred_element_type=jnp.float32)

    pooled = lax.map(pool_one_block, (index_blocks, count_blocks))
    return pooled.reshape(shard_index.shape[1], table_rows.shape[1])


def shard_gradient(shard_index, shard_count, grad_rows, row_total, block_size):
    index_blocks, count_blocks, blocks = split_blocks(shard_index, shard_count, block_size)
    grad_blocks = grad_rows.reshape(blocks, block_size, grad_rows.shape[1])

    def shard_one_block(running, inputs):
        hit_table = hit_counts(inputs[0], inputs[1], row_total)
        update = lax.dot_general(
            hit_table, inputs[2], (((0,), (0,)), ((), ())), preferred_element_type=jnp.float32
        )
        return (running + update, None)

    result, unused = lax.scan(
        shard_one_block,
        jnp.zeros((row_total, grad_rows.shape[1]), jnp.float32),
        (index_blocks, count_blocks, grad_blocks),
    )
    return result


def bottom_pass(
    dense_rows, first_layer, first_offset, second_layer, second_offset, third_layer, third_offset
):
    first_pre = jnp.dot(dense_rows, first_layer, preferred_element_type=jnp.float32) + first_offset
    first_act = jax.nn.silu(first_pre).astype(jnp.bfloat16)
    second_pre = (
        jnp.dot(first_act, second_layer, preferred_element_type=jnp.float32) + second_offset
    )
    second_act = jax.nn.silu(second_pre).astype(jnp.bfloat16)
    third_pre = jnp.dot(second_act, third_layer, preferred_element_type=jnp.float32) + third_offset
    bottom_out = jax.nn.silu(third_pre).astype(jnp.bfloat16)
    return (bottom_out, (first_pre, first_act, second_pre, second_act, third_pre))


def bottom_back(dense_rows, saved, second_layer, third_layer, bottom_grad):
    first_pre, first_act, second_pre, second_act, third_pre = saved
    contract = (((0,), (0,)), ((), ()))
    back_dims = (((1,), (1,)), ((), ()))
    third_delta = (silu_slope(third_pre) * bottom_grad.astype(jnp.float32)).astype(jnp.bfloat16)
    third_grad = lax.dot_general(
        second_act, third_delta, contract, preferred_element_type=jnp.float32
    )
    third_bias = jnp.sum(third_delta.astype(jnp.float32), axis=0)
    second_back = lax.dot_general(
        third_delta, third_layer, back_dims, preferred_element_type=jnp.float32
    )
    second_delta = (silu_slope(second_pre) * second_back).astype(jnp.bfloat16)
    second_grad = lax.dot_general(
        first_act, second_delta, contract, preferred_element_type=jnp.float32
    )
    second_bias = jnp.sum(second_delta.astype(jnp.float32), axis=0)
    first_back = lax.dot_general(
        second_delta, second_layer, back_dims, preferred_element_type=jnp.float32
    )
    first_delta = (silu_slope(first_pre) * first_back).astype(jnp.bfloat16)
    first_grad = lax.dot_general(
        dense_rows, first_delta, contract, preferred_element_type=jnp.float32
    )
    first_bias = jnp.sum(first_delta.astype(jnp.float32), axis=0)
    return (first_grad, first_bias, second_grad, second_bias, third_grad, third_bias)


def local(
    dense_feats,
    lookup_ids,
    lookup_counts,
    shard_table,
    embed_tables,
    first_layer,
    first_offset,
    second_layer,
    second_offset,
    third_layer,
    third_offset,
    cross_down,
    cross_up,
    cross_bias,
    cotangent,
):
    local_shards, row_total, width = embed_tables.shape
    batch_group = lookup_ids.shape[2]
    block_size = math.gcd(batch_group, 1024)
    examples = dense_feats.shape[0]
    back_dims = (((1,), (1,)), ((), ()))
    pooled = jnp.stack(
        [
            pool_shard(
                embed_tables[shard_pos], lookup_ids[shard_pos], lookup_counts[shard_pos], block_size
            )
            for shard_pos in range(local_shards)
        ],
        axis=1,
    ).astype(jnp.bfloat16)
    arrived = lax.all_to_all(pooled, "table", split_axis=0, concat_axis=1, tiled=True)
    table_onehot = (
        shard_table[:, None] == lax.broadcasted_iota(jnp.int32, (shard_table.shape[0], TABLES), 1)
    ).astype(jnp.bfloat16)
    table_pooled = jnp.einsum(
        "bse,st->bte", arrived, table_onehot, preferred_element_type=jnp.float32
    ).astype(jnp.bfloat16)
    bottom_out, saved = bottom_pass(
        dense_feats,
        first_layer,
        first_offset,
        second_layer,
        second_offset,
        third_layer,
        third_offset,
    )
    cross_input = jnp.concatenate([bottom_out[:, None, :], table_pooled], axis=1).reshape(
        examples, -1
    )
    down_whole = lax.all_gather(cross_down, "table", axis=1, tiled=True)
    up_whole = lax.all_gather(cross_up, "table", axis=0, tiled=True)
    low_rank = jnp.dot(cross_input, down_whole, preferred_element_type=jnp.float32).astype(
        jnp.bfloat16
    )
    mixing = jnp.dot(low_rank, up_whole, preferred_element_type=jnp.float32) + cross_bias
    cot_float = cotangent.astype(jnp.float32)
    mix_grad = cot_float * cross_input.astype(jnp.float32)
    bias_part = jnp.sum(mix_grad, axis=0)
    rank_grad = lax.dot_general(
        mix_grad.astype(jnp.bfloat16), up_whole, back_dims, preferred_element_type=jnp.float32
    ).astype(jnp.bfloat16)
    input_grad = (
        cot_float * (mixing + 1.0)
        + lax.dot_general(rank_grad, down_whole, back_dims, preferred_element_type=jnp.float32)
    ).astype(jnp.bfloat16)
    input_grad = input_grad.reshape(examples, TABLES + 1, width)
    bottom_grad = input_grad[:, 0, :]
    shard_grads = jnp.einsum(
        "bte,st->bse", input_grad[:, 1:, :], table_onehot, preferred_element_type=jnp.float32
    ).astype(jnp.bfloat16)
    returned = lax.all_to_all(shard_grads, "table", split_axis=1, concat_axis=0, tiled=True)
    local_grad = jnp.stack(
        [
            shard_gradient(
                lookup_ids[shard_pos],
                lookup_counts[shard_pos],
                returned[:, shard_pos, :],
                row_total,
                block_size,
            )
            for shard_pos in range(local_shards)
        ],
        axis=0,
    )
    table_grad = lax.psum_scatter(local_grad, "dp", scatter_dimension=1, tiled=True)
    partial_grads = bottom_back(dense_feats, saved, second_layer, third_layer, bottom_grad)
    summed = lax.psum(
        (
            partial_grads[0],
            partial_grads[1],
            partial_grads[2],
            partial_grads[3],
            partial_grads[4],
            partial_grads[5],
            bias_part,
        ),
        ("dp", "table"),
    )
    return (table_grad, summed[0], summed[1], summed[2], summed[3], summed[4], summed[5], summed[6])


def solution(mesh):
    placed = (
        P(("dp", "table"), None),
        P("table", None, "dp"),
        P("table", "dp"),
        P(),
        P("table", None, None),
        P(),
        P(),
        P(),
        P(),
        P(),
        P(),
        P(None, "table"),
        P("table", None),
        P(),
        P(("dp", "table"), None),
    )
    return jax.shard_map(
        local,
        mesh=mesh,
        in_specs=placed,
        out_specs=(P("table", "dp", None), P(), P(), P(), P(), P(), P(), P()),
        check_vma=False,
    )
```

profile of v0, /device:TPU:1, one launch (start us, length us, event | category | flops | bytes accessed | tf_op | source)
XLA Modules:
  0.0 663.4 jit_solution(7342675556975713716)
XLA Ops:
  11.8 33.8 %while.42 = (s32[]{:T(128)}, bf16[2,1024,128]{2,1,0:T(8,128)(2,1)S(1)}, s32[2,8,1024]{2,1,0:T(8,128)S(1)}, s32[2,1024]{1,0:T(2,128)S(1)}, bf16[2048,128]{1,0:T(8...) while((s32[]{:T(128)}, ...), condition=%wide.region_1.2_spmd, body=%wide.region_0.1_spmd.sunk | while | flops 620765184 | bytes 1167617 | solution.py:42
  11.9 16.7 %fusion.244 = bf16[2,1024,128]{2,1,0:T(8,128)(2,1)S(1)} fusion(bf16[2,1024,128]{2,1,0:T(8,128)(2,1)S(1)} %get-tuple-element.590, s32[]{:T(128)} %get-tuple-element.589, bf16[2048,128]{1,0:T(8,128)(2,1)S(1)} %get-tuple-element.607, s32[1024]{0:T(1024)S(1)} %bitcast.227, s32[1024]{0:T(1024)S(1)} %bitcast.221, s32[1024]{0:T(1024)S(1)} %bitcast.222, ...), kind=kOutput, calls=%fused_computation.41.clone.1 | convolution fusion | flops 620756992 | bytes 1089540 | tf_op jit(solution)/shard_map/while/body/eval_jaxpr/dot_general | solution.py:40
  28.8 16.7 %fusion.244 = bf16[2,1024,128]{2,1,0:T(8,128)(2,1)S(1)} fusion(bf16[2,1024,128]{2,1,0:T(8,128)(2,1)S(1)} %get-tuple-element.590, s32[]{:T(128)} %get-tuple-element.589, bf16[2048,128]{1,0:T(8,128)(2,1)S(1)} %get-tuple-element.607, s32[1024]{0:T(1024)S(1)} %bitcast.227, s32[1024]{0:T(1024)S(1)} %bitcast.221, s32[1024]{0:T(1024)S(1)} %bitcast.222, ...), kind=kOutput, calls=%fused_computation.41.clone.1 | convolution fusion | flops 620756992 | bytes 1089540 | tf_op jit(solution)/shard_map/while/body/eval_jaxpr/dot_general | solution.py:40
  45.7 33.8 %while.43 = (s32[]{:T(128)}, bf16[2,1024,128]{2,1,0:T(8,128)(2,1)S(1)}, s32[2,8,1024]{2,1,0:T(8,128)S(1)}, s32[2,1024]{1,0:T(2,128)S(1)}, bf16[2048,128]{1,0:T(8...) while((s32[]{:T(128)}, ...), condition=%wide.region_3.4_spmd, body=%wide.region_2.3_spmd.sunk | while | flops 620765184 | bytes 1167617 | solution.py:42
  45.8 16.7 %fusion.247 = bf16[2,1024,128]{2,1,0:T(8,128)(2,1)S(1)} fusion(bf16[2,1024,128]{2,1,0:T(8,128)(2,1)S(1)} %get-tuple-element.548, s32[]{:T(128)} %get-tuple-element.547, bf16[2048,128]{1,0:T(8,128)(2,1)S(1)} %get-tuple-element.565, s32[1024]{0:T(1024)S(1)} %bitcast.235, s32[1024]{0:T(1024)S(1)} %bitcast.229, s32[1024]{0:T(1024)S(1)} %bitcast.230, ...), kind=kOutput, calls=%fused_computation.100.clone.1 | convolution fusion | flops 620756992 | bytes 1089540 | tf_op jit(solution)/shard_map/while/body/eval_jaxpr/dot_general | solution.py:40
  62.7 16.7 %fusion.247 = bf16[2,1024,128]{2,1,0:T(8,128)(2,1)S(1)} fusion(bf16[2,1024,128]{2,1,0:T(8,128)(2,1)S(1)} %get-tuple-element.548, s32[]{:T(128)} %get-tuple-element.547, bf16[2048,128]{1,0:T(8,128)(2,1)S(1)} %get-tuple-element.565, s32[1024]{0:T(1024)S(1)} %bitcast.235, s32[1024]{0:T(1024)S(1)} %bitcast.229, s32[1024]{0:T(1024)S(1)} %bitcast.230, ...), kind=kOutput, calls=%fused_computation.100.clone.1 | convolution fusion | flops 620756992 | bytes 1089540 | tf_op jit(solution)/shard_map/while/body/eval_jaxpr/dot_general | solution.py:40
  79.6 9.5 %copy.44 = bf16[2048,2,128]{2,1,0:T(2,128)(2,1)} copy(bf16[2048,2,128]{2,0,1:T(8,128)(2,1)S(1)} %pad_maximum_fusion.1) | data formatting | bytes 2097152 | tf_op jit(solution)/shard_map/stack | solution.py:129
  89.1 10.9 %all-to-all-start = ((bf16[2048,2,128]{2,1,0:T(2,128)(2,1)}), bf16[2048,2,128]{2,1,0:T(2,128)(2,1)S(1)}, u32[]{:S(2)}, u32[]{:S(2)}) async-start(bf16[2048,2,128]{2,1,0:T(2,128)(2,1)} %copy.44), calls=%async_computation | async-start | bytes 2097152 | tf_op jit(solution)/shard_map/all_to_all | solution.py:138
  100.9 26.8 %all-to-all-done = bf16[2048,2,128]{2,1,0:T(2,128)(2,1)S(1)} async-done(((bf16[2048,2,128]{2,1,0:T(2,128)(2,1)}), bf16[2048,2,128]{2,1,0:T(2,128)(2,1)S(1)}, u32[]{:S(2)}, u32[]{:S(2)}) %all-to-all-start) | async-done | bytes 1048608 | tf_op jit(solution)/shard_map/all_to_all | solution.py:138
  132.5 6.5 fusion.187
  139.0 5.4 fusion.188
  146.4 1.9 copy.52
  150.3 3.6 all-to-all-start.1
  157.5 24.4 %all-to-all-done.1 = bf16[128,32,128]{2,0,1:T(8,128)(2,1)S(1)} async-done(((bf16[128,32,128]{2,0,1:T(8,128)(2,1)}), bf16[128,32,128]{2,0,1:T(8,128)(2,1)S(1)}, u32[]{:S(2)}, u32[]{:S(2)}) %all-to-all-start.1) | async-done | bytes 1048608 | tf_op jit(solution)/shard_map/all_to_all | solution.py:178
  182.1 30.7 %while.44 = (s32[]{:T(128)}, f32[2048,128]{1,0:T(8,128)}, s32[2,8,1024]{2,1,0:T(8,128)S(1)}, s32[2,1024]{1,0:T(2,128)S(1)}, bf16[2,1024,128]{2,1,0:T(8,128)(2,1)...) while((s32[]{:T(128)}, f32[2048,128]{1,0:T(8,128)}, ...), condition=%wide.region_5.6_spmd.clone, body=%wide.region_4.5_spmd.clone.sunk | while | flops 621289472 | bytes 2478347 | solution.py:57
  182.5 14.5 %fusion.250 = f32[2048,128]{1,0:T(8,128)} fusion(s32[1024]{0:T(1024)S(1)} %bitcast.211, s32[1024]{0:T(1024)S(1)} %bitcast.205, s32[1024]{0:T(1024)S(1)} %bitcast.206, s32[1024]{0:T(1024)S(1)} %bitcast.207, s32[1024]{0:T(1024)S(1)} %bitcast.208, s32[1024]{0:T(1024)S(1)} %bitcast.209, s32[1024]{0:T(1024)S(1)} %bitcast.210, s32[1024]{0:T(1024)S(1)} %bitcast.204, ...), kind=kOutput, calls=%fused_computation.166.clone.1 | convolution fusion | flops 621281280 | bytes 2400261 | tf_op jit(solution)/shard_map/while/body/eval_jaxpr/dot_general | solution.py:52
  197.1 15.7 %fusion.250 = f32[2048,128]{1,0:T(8,128)} fusion(s32[1024]{0:T(1024)S(1)} %bitcast.211, s32[1024]{0:T(1024)S(1)} %bitcast.205, s32[1024]{0:T(1024)S(1)} %bitcast.206, s32[1024]{0:T(1024)S(1)} %bitcast.207, s32[1024]{0:T(1024)S(1)} %bitcast.208, s32[1024]{0:T(1024)S(1)} %bitcast.209, s32[1024]{0:T(1024)S(1)} %bitcast.210, s32[1024]{0:T(1024)S(1)} %bitcast.204, ...), kind=kOutput, calls=%fused_computation.166.clone.1 | convolution fusion | flops 621281280 | bytes 2400261 | tf_op jit(solution)/shard_map/while/body/eval_jaxpr/dot_general | solution.py:52
  212.8 27.9 %while.45 = (s32[]{:T(128)}, f32[2048,128]{1,0:T(8,128)S(1)}, s32[2,8,1024]{2,1,0:T(8,128)S(1)}, s32[2,1024]{1,0:T(2,128)S(1)}, bf16[2,1024,128]{2,1,0:T(8,128)(...) while((s32[]{:T(128)}, f32[2048,128]{1,0:T(8,128)S(1)}, ...), condition=%wide.region_7.8_spmd.clone, body=%wide.region_6.7_spmd.clone.sunk | while | flops 621289472 | bytes 2478347 | solution.py:57
  213.2 13.7 %fusion.253 = f32[2048,128]{1,0:T(8,128)S(1)} fusion(s32[1024]{0:T(1024)S(1)} %bitcast.219, s32[1024]{0:T(1024)S(1)} %bitcast.213, s32[1024]{0:T(1024)S(1)} %bitcast.214, s32[1024]{0:T(1024)S(1)} %bitcast.215, s32[1024]{0:T(1024)S(1)} %bitcast.216, s32[1024]{0:T(1024)S(1)} %bitcast.217, s32[1024]{0:T(1024)S(1)} %bitcast.218, ...), kind=kOutput, calls=%fused_computation.235.clone.1 | convolution fusion | flops 621281280 | bytes 2400261 | tf_op jit(solution)/shard_map/while/body/eval_jaxpr/dot_general | solution.py:52
  227.0 13.7 %fusion.253 = f32[2048,128]{1,0:T(8,128)S(1)} fusion(s32[1024]{0:T(1024)S(1)} %bitcast.219, s32[1024]{0:T(1024)S(1)} %bitcast.213, s32[1024]{0:T(1024)S(1)} %bitcast.214, s32[1024]{0:T(1024)S(1)} %bitcast.215, s32[1024]{0:T(1024)S(1)} %bitcast.216, s32[1024]{0:T(1024)S(1)} %bitcast.217, s32[1024]{0:T(1024)S(1)} %bitcast.218, ...), kind=kOutput, calls=%fused_computation.235.clone.1 | convolution fusion | flops 621281280 | bytes 2400261 | tf_op jit(solution)/shard_map/while/body/eval_jaxpr/dot_general | solution.py:52
  240.8 2.9 pad_maximum_fusion
  244.5 101.2 %all-reduce = (f32[13,512]{1,0:T(8,128)}, f32[512]{0:T(512)}, f32[256]{0:T(256)}, f32[128]{0:T(128)}, f32[3456]{0:T(1024)}) all-reduce(f32[13,512]{1,0:T(8,128)S(1)} %convolution_bitcast_fusion, f32[512]{0:T(512)S(1)} %get-tuple-element.277, f32[256]{0:T(256)S(1)} %copy-done.15, ...), channel_id=1, replica_groups=mesh['dp'=32,'table'=16] {'dp','table'}, use_global_device_ids=true, to_apply=%region_9.10 | all-reduce | flops 11008 | bytes 88064 | tf_op jit(solution)/shard_map/psum | solution.py:194
  345.6 88.4 %all-reduce.4.cloned.1.call-done = (f32[512,256]{1,0:T(8,128)}, f32[256,128]{1,0:T(8,128)}) async-done(((f32[512,256]{1,0:T(8,128)}, f32[256,128]{1,0:T(8,128)}), (f32[512,256]{1,0:T(8,128)}, f32[256,128]{1,0:T(8,128)})) %all-reduce.4.cloned.1.call-update) | async-done | bytes 655376 | tf_op jit(solution)/shard_map/psum | solution.py:194
  434.1 219.0 %reduce-scatter.2.cloned.1.call-done = f32[2,64,128]{2,1,0:T(8,128)} async-done(((f32[2,2048,128]{2,1,0:T(8,128)}), f32[2,64,128]{2,1,0:T(8,128)}) %reduce-scatter.2.cloned.1.call-update) | async-done | bytes 65552 | tf_op jit(solution)/shard_map/reduce_scatter | solution.py:192
  (110 shorter events, 23.2 us)
Async XLA Ops:
  7.2 93.1 %copy-start = (bf16[512,256]{1,0:T(8,128)(2,1)S(1)}, bf16[512,256]{1,0:T(8,128)(2,1)}, u32[]{:S(2)}) copy-start(bf16[512,256]{1,0:T(8,128)(2,1)} %param.30) | copy-start | bytes 786436
  7.2 125.3 %all-gather.3.cloned.1.call-start = ((), (), s32[]{:S(2)}) async-start(), calls=%async_computation.3 | async-start | bytes 3760128 | tf_op jit(solution)/shard_map/all_gather | solution.py:157
  7.9 124.6 %all-gather.5.cloned.1.call-start = ((), (), s32[]{:S(2)}) async-start(), calls=%async_computation.4 | async-start | bytes 3760128 | tf_op jit(solution)/shard_map/all_gather | solution.py:158
  79.5 20.5 %copy-start.8 = (bf16[13,512]{1,0:T(8,128)(2,1)S(1)}, bf16[13,512]{1,0:T(8,128)(2,1)}, u32[]{:S(2)}) copy-start(bf16[13,512]{1,0:T(8,128)(2,1)} %param.28) | copy-start | bytes 39940
  79.5 20.5 %copy-start.9 = (bf16[128,13]{0,1:T(8,128)(2,1)S(1)}, bf16[128,13]{0,1:T(8,128)(2,1)}, u32[]{:S(2)}) copy-start(bf16[128,13]{0,1:T(8,128)(2,1)} %param.23) | copy-start | bytes 9988
  79.5 20.5 %copy-start.11 = (f32[512]{0:T(512)S(1)}, f32[512]{0:T(512)}, u32[]{:S(2)}) copy-start(f32[512]{0:T(512)} %param.29) | copy-start | bytes 6148
  79.5 20.8 %copy-start.18 = (f32[256]{0:T(256)S(1)}, f32[256]{0:T(256)}, u32[]{:S(2)}) copy-start(f32[256]{0:T(256)} %param.31) | copy-start | bytes 3076
  79.5 21.0 %copy-start.16 = (bf16[256,128]{1,0:T(8,128)(2,1)S(1)}, bf16[256,128]{1,0:T(8,128)(2,1)}, u32[]{:S(2)}) copy-start(bf16[256,128]{1,0:T(8,128)(2,1)} %param.32) | copy-start | bytes 196612
  79.5 21.0 %copy-start.19 = (f32[128]{0:T(128)S(1)}, f32[128]{0:T(128)}, u32[]{:S(2)}) copy-start(f32[128]{0:T(128)} %param.33) | copy-start | bytes 1540
  89.1 38.6 %all-to-all-start = ((bf16[2048,2,128]{2,1,0:T(2,128)(2,1)}), bf16[2048,2,128]{2,1,0:T(2,128)(2,1)S(1)}, u32[]{:S(2)}, u32[]{:S(2)}) async-start(bf16[2048,2,128]{2,1,0:T(2,128)(2,1)} %copy.44), calls=%async_computation | async-start | bytes 2097152 | tf_op jit(solution)/shard_map/all_to_all | solution.py:138
  100.0 29.0 %copy-start.12 = (s32[32]{0:T(128)S(1)}, s32[32]{0:T(128)}, u32[]{:S(2)}) copy-start(s32[32]{0:T(128)} %param.26) | copy-start | bytes 388
  100.3 56.1 %copy-start.6 = (f32[128,512]{1,0:T(8,128)}, f32[128,512]{1,0:T(8,128)S(1)}, u32[]{:S(2)}) copy-start(f32[128,512]{1,0:T(8,128)S(1)} %convolution_add_fusion.2) | copy-start | bytes 786436
  100.5 29.0 %copy-start.20 = (f32[128,256]{1,0:T(8,128)}, f32[128,256]{1,0:T(8,128)S(1)}, u32[]{:S(2)}) copy-start(f32[128,256]{1,0:T(8,128)S(1)} %convolution_add_fusion.3) | copy-start | bytes 393220
  129.0 3.5 copy-start.3
  132.4 6.6 copy-start.1
  144.4 3.9 copy-start.13
  148.4 6.3 copy-start.17
  148.4 6.3 copy-start.21
  150.3 31.6 %all-to-all-start.1 = ((bf16[128,32,128]{2,0,1:T(8,128)(2,1)}), bf16[128,32,128]{2,0,1:T(8,128)(2,1)S(1)}, u32[]{:S(2)}, u32[]{:S(2)}) async-start(bf16[128,32,128]{2,0,1:T(8,128)(2,1)} %copy.53), calls=%async_computation.1 | async-start | bytes 2097152 | tf_op jit(solution)/shard_map/all_to_all | solution.py:178
  154.0 280.1 %all-reduce.4.cloned.1.call-start = ((), (), s32[]{:S(2)}) async-start(), calls=%async_computation.6 | async-start | bytes 1310720 | tf_op jit(solution)/shard_map/psum | solution.py:194
  155.5 26.6 %copy-start.22 = (bf16[128,256]{1,0:T(8,128)(2,1)}, bf16[128,256]{1,0:T(8,128)(2,1)S(1)}, u32[]{:S(2)}) copy-start(bf16[128,256]{1,0:T(8,128)(2,1)S(1)} %get-tuple-element.280) | copy-start | bytes 196612
  157.5 495.6 %reduce-scatter.2.cloned.1.call-start = ((), (), s32[]{:S(2)}) async-start(), calls=%async_computation.5 | async-start | bytes 2162688 | tf_op jit(solution)/shard_map/reduce_scatter | solution.py:192
  182.1 30.7 %copy-start.5 = (f32[2048,128]{1,0:T(8,128)S(1)}, f32[2048,128]{1,0:T(8,128)}, u32[]{:S(2)}) copy-start(f32[2048,128]{1,0:T(8,128)} %custom-call.1) | copy-start | bytes 3145732
  240.8 3.2 copy-start.7
  (6 other events, 11.4 us)
Sparse Core Ops, SparseCore 0:
  10.1 49.8 all-gather.2
  62.2 42.8 all-gather.4
  160.4 273.6 all-reduce.3
  439.5 213.4 reduce-scatter.1
where the time goes:
time: 674 us; the launch traced here: 663 us
  waiting for transfers between devices  360 us (53%)
  matrix products  141 us (21%)
  blocking collectives  101 us (15%)
  local copies, waits for them, and re-layouts  25.8 us (4%)
  starting transfers between devices  14.7 us (2%)
  between operations  14.7 us (2%)
    reduce_scatter x1, waiting for transfers between devices, local(): lax.psum_scatter(local_grad, 'dp', scatter_dimension=1, tiled=True)  219 us
    psum x1, blocking collectives, local(): lax.psum((partial_grads[0], partial_grads[1], partial_grads[2], partial_g...  101 us
    psum x1, waiting for transfers between devices, local(): lax.psum((partial_grads[0], partial_grads[1], partial_grads[2], partial_g...  88.4 us
    dot_general x4, matrix products, pool_one_block(): return jnp.dot(hit_table, table_rows, preferred_element_type=jnp.float32)  66.9 us
    dot_general x4, matrix products, shard_one_block(): lax.dot_general(hit_table, inputs[2], (((0,), (0,)), ((), ())), preferred...  57.5 us
    all_to_all x1, waiting for transfers between devices, local(): lax.all_to_all(pooled, 'table', split_axis=0, concat_axis=1, tiled=True)  26.8 us
    all_to_all x1, waiting for transfers between devices, local(): lax.all_to_all(shard_grads, 'table', split_axis=1, concat_axis=0, tiled=T...  24.4 us
  transfers between devices with their start and end apart: 6, of which 4 were waited for; matrix products, arithmetic and copies ran while one was open for 23% of the time, Pallas kernels for 0%

commit v1 on v0

v1 whole, which is shorter than its diff:
```python
import functools

import jax
import jax.numpy as jnp
import numpy as np
from jax import lax
from jax.experimental import pallas as pl
from jax.experimental.pallas import tpu as pltpu
from jax.sharding import Mesh
from jax.sharding import PartitionSpec as P

TABLES = 26
WIDTH = 128
GROUP = 32
BLOCK = 256
LOW = 256
TABLE = ("y", "c")
DP = ("x", "z")
EVERY = ("x", "z", "y", "c")
CHUNK = 96

NT = (((1,), (1,)), ((), ()))
TN = (((0,), (0,)), ((), ()))


def dot(a, b, dims=(((1,), (0,)), ((), ()))):
    return lax.dot_general(a, b, dims, preferred_element_type=jnp.float32)


def params(megabytes=48):
    return pltpu.CompilerParams(vmem_limit_bytes=megabytes * 1024 * 1024)


def pool_kernel(code_ref, table_ref, hits_ref, pooled_ref):
    slots = code_ref.shape[2]
    rows = table_ref.shape[1]
    lane = lax.broadcasted_iota(jnp.int32, (GROUP, slots), 1)
    own = (lane & (GROUP - 1)) == lax.broadcasted_iota(jnp.int32, (GROUP, slots), 0)
    low_iota = lax.broadcasted_iota(jnp.int32, (LOW, slots), 0).astype(jnp.float32).astype(jnp.bfloat16)
    one = jnp.ones((), jnp.bfloat16)
    zero = jnp.zeros((), jnp.bfloat16)
    for group in range(BLOCK // GROUP):
        code = code_ref[0, pl.ds(group, 1), :]
        high = jnp.broadcast_to(code >> 8, (GROUP, slots))
        high = jnp.where(own, high, -1).astype(jnp.float32).astype(jnp.bfloat16)
        low = (code & (LOW - 1)).astype(jnp.float32).astype(jnp.bfloat16)
        right = jnp.where(low_iota == jnp.broadcast_to(low, (LOW, slots)), one, zero)
        left = jnp.concatenate(
            [jnp.where(high == jnp.full((), part, jnp.bfloat16), one, zero) for part in range(rows // LOW)], axis=0
        )
        hits = dot(left, right, NT).astype(jnp.bfloat16)
        for part in range(rows // LOW):
            hits_ref[0, pl.ds(group * GROUP, GROUP), pl.ds(part * LOW, LOW)] = hits[
                part * GROUP : (part + 1) * GROUP
            ]
    pooled_ref[...] = dot(hits_ref[0], table_ref[0]).astype(jnp.bfloat16)


def pool(lookup_ids, lookup_counts, embed_tables):
    shards, hot, batch = lookup_ids.shape
    rows = embed_tables.shape[1]
    slot = lax.broadcasted_iota(jnp.int32, lookup_ids.shape, 1)
    code = jnp.where(lookup_counts[:, None, :] > slot, lookup_ids, -1)
    code = code.reshape(shards, hot, batch // GROUP, GROUP).transpose(0, 2, 1, 3)
    code = code.reshape(shards, batch // GROUP, hot * GROUP)
    return pl.pallas_call(
        pool_kernel,
        grid=(shards, batch // BLOCK),
        in_specs=[
            pl.BlockSpec((1, BLOCK // GROUP, hot * GROUP), lambda s, b: (s, b, 0)),
            pl.BlockSpec((1, rows, WIDTH), lambda s, b: (s, 0, 0)),
        ],
        out_specs=[
            pl.BlockSpec((1, BLOCK, rows), lambda s, b: (s, b, 0)),
            pl.BlockSpec((BLOCK, WIDTH), lambda s, b: (b, s)),
        ],
        out_shape=[
            jax.ShapeDtypeStruct((shards, batch, rows), jnp.bfloat16),
            jax.ShapeDtypeStruct((batch, shards * WIDTH), jnp.bfloat16),
        ],
        compiler_params=params(),
        name="pool",
    )(code, embed_tables)


def table_grad_kernel(hits_ref, grad_ref, out_ref):
    total = dot(hits_ref[0], grad_ref[...], TN).astype(jnp.bfloat16)
    out_ref[...] = total.reshape(out_ref.shape)


def table_grads(hits, grads, parts):
    shards, batch, rows = hits.shape
    each = rows // parts
    step = BLOCK // each
    return pl.pallas_call(
        table_grad_kernel,
        grid=(shards, rows // BLOCK),
        in_specs=[
            pl.BlockSpec((1, batch, BLOCK), lambda s, r: (s, 0, r)),
            pl.BlockSpec((batch, WIDTH), lambda s, r: (0, s)),
        ],
        out_specs=pl.BlockSpec((step, 1, each, WIDTH), lambda s, r: (r, s, 0, 0)),
        out_shape=jax.ShapeDtypeStruct((parts, shards, each, WIDTH), jnp.bfloat16),
        compiler_params=params(),
        name="table_grads",
    )(hits, grads)


def silu(value):
    return value / (1.0 + jnp.exp(-value))


def silu_slope(value):
    sigmoid = 1.0 / (1.0 + jnp.exp(-value))
    return sigmoid * (1.0 + value * (1.0 - sigmoid))


def bottom_pre(dense, w1, b1, w2, b2, w3, b3):
    first_pre = dot(dense[...], w1[...]) + b1[...]
    first_act = silu(first_pre).astype(jnp.bfloat16)
    second_pre = dot(first_act, w2[...]) + b2[...]
    second_act = silu(second_pre).astype(jnp.bfloat16)
    third_pre = dot(second_act, w3[...]) + b3[...]
    return first_pre, first_act, second_pre, second_act, third_pre


def bottom_kernel(dense, w1, b1, w2, b2, w3, b3, out_ref):
    out_ref[...] = silu(bottom_pre(dense, w1, b1, w2, b2, w3, b3)[4]).astype(jnp.bfloat16)


def bottom_back_kernel(dense, w1, b1, w2, b2, w3, b3, grad_ref, bias_ref, out_ref):
    first_pre, first_act, second_pre, second_act, third_pre = bottom_pre(dense, w1, b1, w2, b2, w3, b3)
    third_delta = silu_slope(third_pre) * grad_ref[...].astype(jnp.float32)
    third_delta = third_delta.astype(jnp.bfloat16)
    out_ref[1024:1280, :] = dot(second_act, third_delta, TN).astype(jnp.bfloat16)
    second_delta = (silu_slope(second_pre) * dot(third_delta, w3[...], NT)).astype(jnp.bfloat16)
    second_grad = dot(first_act, second_delta, TN).astype(jnp.bfloat16)
    out_ref[0:512, :] = second_grad[:, :128]
    out_ref[512:1024, :] = second_grad[:, 128:]
    first_delta = (silu_slope(first_pre) * dot(second_delta, w2[...], NT)).astype(jnp.bfloat16)
    first_grad = dot(dense[...], first_delta, TN)
    first_grad = jnp.concatenate([first_grad, jnp.zeros((3, first_grad.shape[1]), jnp.float32)], axis=0)
    for part in range(4):
        out_ref[1280 + 16 * part : 1296 + 16 * part, :] = first_grad[:, part * 128 : part * 128 + 128].astype(
            jnp.bfloat16
        )
    first_sum = jnp.sum(first_delta.astype(jnp.float32), axis=0, keepdims=True)
    second_sum = jnp.sum(second_delta.astype(jnp.float32), axis=0, keepdims=True)
    third_sum = jnp.sum(third_delta.astype(jnp.float32), axis=0, keepdims=True)
    rows = [first_sum[:, part * 128 : part * 128 + 128] for part in range(4)]
    rows += [second_sum[:, part * 128 : part * 128 + 128] for part in range(2)]
    rows += [third_sum, jnp.zeros((9, 128), jnp.float32)]
    out_ref[1344:1360, :] = jnp.concatenate(rows, axis=0).astype(jnp.bfloat16)
    out_ref[1360:1392, :] = bias_ref[...].astype(jnp.bfloat16)
    out_ref[1392:1536, :] = jnp.zeros((144, 128), jnp.bfloat16)


def cross_kernel(
    owner_ref, arrived_ref, bottom_ref, weights_ref, bias_ref, cot_ref,
    send_ref, bottom_grad_ref, bias_grad_ref, total, inputs, mixed, grads,
):
    blocks = total.shape[0]
    wide = blocks * WIDTH
    shards = owner_ref.shape[0]
    total[1:] = jnp.zeros_like(total[1:])
    total[0] = bottom_ref[...].astype(jnp.float32)
    for shard in range(shards):
        place = owner_ref[shard] + 1
        piece = arrived_ref[shard // 2, :, (shard % 2) * WIDTH : (shard % 2) * WIDTH + WIDTH]
        total[place] = total[place] + piece.astype(jnp.float32)
    bias_grad_ref[...] = jnp.zeros_like(bias_grad_ref)
    for block in range(blocks):
        columns = slice(block * WIDTH, block * WIDTH + WIDTH)
        piece = total[block].astype(jnp.bfloat16)
        inputs[:, columns] = piece
        mix_grad = cot_ref[:, columns].astype(jnp.float32) * piece.astype(jnp.float32)
        mixed[:, columns] = mix_grad.astype(jnp.bfloat16)
        bias_grad_ref[block : block + 1, :] = jnp.sum(mix_grad, axis=0, keepdims=True)
    low_rank = dot(inputs[...], weights_ref[:, wide:], NT).astype(jnp.bfloat16)
    rank_grad = dot(mixed[...], weights_ref[:, :wide], NT).astype(jnp.bfloat16)
    step = 3 * WIDTH
    for part in range(wide // step):
        columns = slice(part * step, part * step + step)
        mixing = dot(low_rank, weights_ref[:, columns]) + bias_ref[:, columns]
        back = dot(rank_grad, weights_ref[:, wide + part * step : wide + part * step + step])
        grad = (cot_ref[:, columns].astype(jnp.float32) * (mixing + 1.0) + back).astype(jnp.bfloat16)
        for inner in range(3):
            grads[part * 3 + inner] = grad[:, inner * WIDTH : inner * WIDTH + WIDTH]
    bottom_grad_ref[...] = grads[0]
    for shard in range(shards):
        send_ref[shard // 2, :, (shard % 2) * WIDTH : (shard % 2) * WIDTH + WIDTH] = grads[owner_ref[shard] + 1]


def cross(shard_table, arrived, bottom_out, weights, cross_bias, cotangent):
    examples, wide = cotangent.shape
    blocks = wide // WIDTH
    vmem = pl.BlockSpec(memory_space=pltpu.VMEM)
    return pl.pallas_call(
        cross_kernel,
        in_specs=[pl.BlockSpec(memory_space=pltpu.SMEM)] + [vmem] * 5,
        out_specs=[vmem] * 3,
        out_shape=[
            jax.ShapeDtypeStruct(arrived.shape, jnp.bfloat16),
            jax.ShapeDtypeStruct((examples, WIDTH), jnp.bfloat16),
            jax.ShapeDtypeStruct((32, WIDTH), jnp.float32),
        ],
        scratch_shapes=[
            pltpu.VMEM((blocks, examples, WIDTH), jnp.float32),
            pltpu.VMEM((examples, wide), jnp.bfloat16),
            pltpu.VMEM((examples, wide), jnp.bfloat16),
            pltpu.VMEM((blocks, examples, WIDTH), jnp.bfloat16),
        ],
        compiler_params=params(),
        name="cross",
    )(shard_table, arrived, bottom_out, weights, cross_bias, cotangent)


def local(
    dense_feats, lookup_ids, lookup_counts, shard_table, embed_tables, first_layer, first_offset, second_layer,
    second_offset, third_layer, third_offset, cross_down, cross_up, cross_bias, cotangent,
):
    examples = dense_feats.shape[0]
    devices = lookup_ids.shape[2] // examples
    weights = lax.all_gather(jnp.concatenate([cross_up, cross_down.T], axis=1), TABLE, axis=0, tiled=True)
    hits, pooled = pool(lookup_ids, lookup_counts, embed_tables)
    pooled = pooled.reshape(devices, examples, pooled.shape[1])
    arrived = lax.all_to_all(pooled, TABLE, split_axis=0, concat_axis=0, tiled=True)
    vmem = pl.BlockSpec(memory_space=pltpu.VMEM)
    bottom_args = (
        dense_feats, first_layer, first_offset[None], second_layer, second_offset[None], third_layer,
        third_offset[None],
    )
    bottom_out = pl.pallas_call(
        bottom_kernel,
        in_specs=[vmem] * 7,
        out_specs=vmem,
        out_shape=jax.ShapeDtypeStruct((examples, WIDTH), jnp.bfloat16),
        compiler_params=params(),
        name="bottom",
    )(*bottom_args)
    send, bottom_grad, bias_part = cross(shard_table, arrived, bottom_out, weights, cross_bias[None], cotangent)
    returned = lax.all_to_all(send, TABLE, split_axis=0, concat_axis=0, tiled=True)
    parts = lax.axis_size("x") * lax.axis_size("z")
    table_parts = table_grads(hits, returned.reshape(-1, returned.shape[2]), parts)
    table_parts = lax.all_to_all(table_parts, DP, split_axis=0, concat_axis=0, tiled=True)
    table_grad = jnp.sum(table_parts.astype(jnp.float32), axis=0)

    packed = pl.pallas_call(
        bottom_back_kernel,
        in_specs=[vmem] * 9,
        out_specs=vmem,
        out_shape=jax.ShapeDtypeStruct((devices * CHUNK, 128), jnp.bfloat16),
        compiler_params=params(),
        name="bottom_back",
    )(*bottom_args, bottom_grad, bias_part)
    packed = lax.all_to_all(packed.reshape(devices, CHUNK, 128), TABLE, split_axis=0, concat_axis=0, tiled=True)
    summed = jnp.sum(packed.astype(jnp.float32), axis=0)
    summed = lax.psum(lax.psum(summed, "x"), "z").astype(jnp.bfloat16)
    summed = lax.all_gather(summed, TABLE, axis=0, tiled=True)
    whole = summed.astype(jnp.float32)
    second_grad = jnp.concatenate([whole[0:512], whole[512:1024]], axis=1)
    first_grad = jnp.concatenate([whole[1280 + 16 * part : 1293 + 16 * part] for part in range(4)], axis=1)
    return (
        table_grad,
        first_grad,
        whole[1344:1348].reshape(-1),
        second_grad,
        whole[1348:1350].reshape(-1),
        whole[1024:1280],
        whole[1350],
        whole[1360:1387].reshape(-1),
    )


def solution(mesh):
    fine = Mesh(mesh.devices.reshape(4, 8, 8, 2), EVERY)
    placed = (
        P(EVERY, None),
        P(TABLE, None, DP),
        P(TABLE, DP),
        P(),
        P(TABLE, None, None),
        P(),
        P(),
        P(),
        P(),
        P(),
        P(),
        P(None, TABLE),
        P(TABLE, None),
        P(),
        P(EVERY, None),
    )
    return jax.shard_map(
        local,
        mesh=fine,
        in_specs=placed,
        out_specs=(P(TABLE, DP, None), P(), P(), P(), P(), P(), P(), P()),
        check_vma=False,
    )
```

time: 674 us -> 242 us (0.36); the launches traced: 663 us -> 241 us
  waiting for transfers between devices: 360 us -> 75.1 us
  matrix products: 141 us -> 0 us
  Pallas kernels: 0 us -> 39.5 us
  blocking collectives: 101 us -> 67.5 us
  local copies, waits for them, and re-layouts: 25.8 us -> 10.8 us
  starting transfers between devices: 14.7 us -> 28.7 us
    reduce_scatter x1 -> x0, waiting for transfers between devices: 219 us -> none  [local(): lax.psum_scatter(local_grad, 'dp', scatter_dimension=1, tiled=True)]
    dot_general x20 -> x0, matrix products: 141 us -> none  [the longest x4 66.9 us: pool_one_block(): return jnp.dot(hit_table, table_rows, preferred_element_type=jnp.float32)]
    psum x1 -> x0, waiting for transfers between devices: 88.4 us -> none  [local(): lax.psum((partial_grads[0], partial_grads[1], partial_grads[2], partial_g...]
    psum x1 -> x2, blocking collectives: 101 us -> 42.3 us  [local(): summed = lax.psum(lax.psum(summed, 'x'), 'z').astype(jnp.bfloat16)]
    pallas_call x0 -> x5, Pallas kernels: none -> 39.5 us  [the longest x1 15.7 us: table_grads(): pl.pallas_call(table_grad_kernel, grid=(shards, rows // BLOCK), in_specs=...]
    all_gather x0 -> x1, blocking collectives: none -> 25.2 us  [local(): summed = lax.all_gather(summed, TABLE, axis=0, tiled=True)]
    all_gather x2 -> x1, waiting for transfers between devices: 0.04 us -> 17.8 us  [local(): lax.all_gather(jnp.concatenate([cross_up, cross_down.T], axis=1), TABLE,...]
    all_to_all x2 -> x4, starting transfers between devices: 14.5 us -> 28.6 us  [the longest x1 10.5 us: local(): lax.all_to_all(pooled, TABLE, split_axis=0, concat_axis=0, tiled=True)]
  transfers between devices with their start and end apart: 6 -> 5, of which waited for: 4 -> 3; matrix products, arithmetic and copies ran while one was open for 23% -> 3% of each run, Pallas kernels for 0% -> 13%
where the time goes in v1:
time: 242 us; the launch traced here: 241 us
  waiting for transfers between devices  75.1 us (31%)
  blocking collectives  67.5 us (28%)
  Pallas kernels  39.5 us (16%)
  starting transfers between devices  28.7 us (12%)
  between operations  14.2 us (6%)
  local copies, waits for them, and re-layouts  10.8 us (4%)
  other arithmetic  5.18 us (2%)
    psum x2, blocking collectives, local(): summed = lax.psum(lax.psum(summed, 'x'), 'z').astype(jnp.bfloat16)  42.3 us
    all_to_all x1, waiting for transfers between devices, local(): lax.all_to_all(pooled, TABLE, split_axis=0, concat_axis=0, tiled=True)  31.1 us
    all_to_all x1, waiting for transfers between devices, local(): lax.all_to_all(send, TABLE, split_axis=0, concat_axis=0, tiled=True)  26.2 us
    all_gather x1, blocking collectives, local(): summed = lax.all_gather(summed, TABLE, axis=0, tiled=True)  25.2 us
    all_gather x1, waiting for transfers between devices, local(): lax.all_gather(jnp.concatenate([cross_up, cross_down.T], axis=1), TABLE,...  17.8 us
    pallas_call x1, Pallas kernels, table_grads(): pl.pallas_call(table_grad_kernel, grid=(shards, rows // BLOCK), in_specs=...  15.7 us
    pallas_call x1, Pallas kernels, pool(): pl.pallas_call(pool_kernel, grid=(shards, batch // BLOCK), in_specs=[pl.B...  13.4 us
    all_to_all x1, starting transfers between devices, local(): lax.all_to_all(pooled, TABLE, split_axis=0, concat_axis=0, tiled=True)  10.5 us
  transfers between devices with their start and end apart: 5, of which 3 were waited for; matrix products, arithmetic and copies ran while one was open for 3% of the time, Pallas kernels for 13%

profile of v1, /device:TPU:1, one launch (start us, length us, event | category | flops | bytes accessed | tf_op | source)
XLA Modules:
  0.0 241.0 jit_solution(7942663961033721196)
XLA Ops:
  7.2 1.9 pad_maximum_fusion.1
  9.2 0.9 fusion
  10.6 1.2 copy-done
  11.8 13.4 %pool.1 = (bf16[2,2048,2048]{2,1,0:T(8,128)(2,1)}, bf16[2048,256]{1,0:T(8,128)(2,1)}) custom-call(s32[2,64,256]{2,1,0:T(8,128)S(1)} %copy.27.code_ref, bf16[2,2048,128]{2,1,0:T(8,128)(2,1)S(1)} %copy-done), custom_call_target="tpu_custom_call" | custom-call | tf_op jit(solution)/shard_map/pool/pallas_call | solution.py:66
  25.2 10.5 %all-to-all-start = ((bf16[16,128,256]{2,1,0:T(8,128)(2,1)}), bf16[16,128,256]{2,1,0:T(8,128)(2,1)S(1)}, u32[]{:S(2)}, u32[]{:S(2)}) async-start(bf16[16,128,256]{2,1,0:T(8,128)(2,1)} %bitcast.2), calls=%async_computation | async-start | bytes 2097152 | tf_op jit(solution)/shard_map/all_to_all | solution.py:227
  35.7 0.7 broadcast_in_dim.21.bias_ref
  36.4 0.8 copy.28.dense
  37.2 0.9 copy-done.1
  38.2 0.8 copy-done.4
  39.0 0.7 copy-done.6
  42.3 31.1 %all-to-all-done.arrived_ref = bf16[16,128,256]{2,1,0:T(8,128)(2,1)S(1)} async-done(((bf16[16,128,256]{2,1,0:T(8,128)(2,1)}), bf16[16,128,256]{2,1,0:T(8,128)(2,1)S(1)}, u32[]{:S(2)}, u32[]{:S(2)}) %all-to-all-start) | async-done | bytes 1048608 | tf_op jit(solution)/shard_map/all_to_all | solution.py:227
  73.4 17.8 %all-gather.2.cloned.1.call-done.weights_ref = bf16[512,6912]{1,0:T(8,128)(2,1)} async-done(((bf16[32,6912]{1,0:T(8,128)(2,1)}), bf16[512,6912]{1,0:T(8,128)(2,1)}) %all-gather.2.cloned.1.call-update) | async-done | bytes 7077904 | tf_op jit(solution)/shard_map/all_gather | solution.py:224
  91.2 8.2 %cross.1 = (bf16[16,128,256]{2,1,0:T(8,128)(2,1)}, bf16[128,128]{1,0:T(8,128)(2,1)S(1)}, f32[32,128]{1,0:T(8,128)S(1)}) custom-call(s32[32]{0:T(128)S(1)} %copy-done.14, bf16[16,128,256]{2,1,0:T(8,128)(2,1)S(1)} %all-to-all-done.arrived_ref, bf16[128,128]{1,0:T(8,128)(2,1)S(1)} %bottom.1.bottom_ref, ...), custom_call_target="tpu_custom_call" | custom-call | tf_op jit(solution)/shard_map/cross/pallas_call | solution.py:198
  99.4 4.7 %all-to-all-start.1 = ((bf16[16,128,256]{2,1,0:T(8,128)(2,1)}), bf16[16,128,256]{2,1,0:T(8,128)(2,1)S(1)}, u32[]{:S(2)}, u32[]{:S(2)}) async-start(bf16[16,128,256]{2,1,0:T(8,128)(2,1)} %get-tuple-element.15), calls=%async_computation.1 | async-start | bytes 2097152 | tf_op jit(solution)/shard_map/all_to_all | solution.py:242
  104.2 1.7 bottom_back.1
  105.9 26.2 %all-to-all-done.1 = bf16[16,128,256]{2,1,0:T(8,128)(2,1)S(1)} async-done(((bf16[16,128,256]{2,1,0:T(8,128)(2,1)}), bf16[16,128,256]{2,1,0:T(8,128)(2,1)S(1)}, u32[]{:S(2)}, u32[]{:S(2)}) %all-to-all-start.1) | async-done | bytes 1048608 | tf_op jit(solution)/shard_map/all_to_all | solution.py:242
  132.1 3.5 %all-to-all-start.3 = ((bf16[16,96,128]{2,1,0:T(8,128)(2,1)}), bf16[16,96,128]{2,1,0:T(8,128)(2,1)S(1)}, u32[]{:S(2)}, u32[]{:S(2)}) async-start(bf16[16,96,128]{2,1,0:T(8,128)(2,1)} %bitcast.8), calls=%async_computation.3 | async-start | bytes 786432 | tf_op jit(solution)/shard_map/all_to_all | solution.py:256
  135.6 15.7 %table_grads.1 = bf16[32,2,64,128]{3,2,1,0:T(8,128)(2,1)} custom-call(bf16[2,2048,2048]{2,1,0:T(8,128)(2,1)} %get-tuple-element.13.hits_ref, bf16[2048,256]{1,0:T(8,128)(2,1)S(1)} %bitcast.17), custom_call_target="tpu_custom_call" | custom-call | tf_op jit(solution)/shard_map/table_grads/pallas_call | solution.py:95
  151.3 9.9 %all-to-all-start.2 = ((bf16[32,2,64,128]{3,2,1,0:T(8,128)(2,1)}), bf16[32,2,64,128]{3,2,1,0:T(8,128)(2,1)S(1)}, u32[]{:S(2)}, u32[]{:S(2)}) async-start(bf16[32,2,64,128]{3,2,1,0:T(8,128)(2,1)} %table_grads.1), calls=%async_computation.2 | async-start | bytes 2097152 | tf_op jit(solution)/shard_map/all_to_all | solution.py:245
  161.3 15.0 %psum.14 = f32[96,128]{1,0:T(8,128)S(1)} all-reduce(f32[96,128]{1,0:T(8,128)S(1)} %convert_reduce_fusion.1), channel_id=1, replica_groups=mesh['x'=4,'z'=8,'y'=8,'c'=2] {'x'}, use_global_device_ids=true, to_apply=%region_2.3 | all-reduce | flops 12288 | bytes 98304 | tf_op jit(solution)/shard_map/psum | solution.py:258
  176.3 27.3 %psum.15 = bf16[96,128]{1,0:T(8,128)(2,1)S(1)} all-reduce(f32[96,128]{1,0:T(8,128)S(1)} %psum.14), channel_id=1, replica_groups=mesh['x'=4,'z'=8,'y'=8,'c'=2] {'z'}, use_global_device_ids=true, to_apply=%region_3.4 | all-reduce | flops 12288 | bytes 73728 | tf_op jit(solution)/shard_map/psum | solution.py:258
  203.6 25.2 %all_gather.7 = bf16[1536,128]{1,0:T(8,128)(2,1)S(1)} all-gather(bf16[96,128]{1,0:T(8,128)(2,1)S(1)} %psum.15), channel_id=1, replica_groups=mesh['x'=4,'z'=8,'y'=8,'c'=2] {'y','c'}, dimensions={0}, use_global_device_ids=true | all-gather | bytes 417792 | tf_op jit(solution)/shard_map/all_gather | solution.py:259
  230.3 0.8 pad_maximum_fusion
  233.4 0.8 convert_reduce_fusion
  (44 shorter events, 6.8 us)
Async XLA Ops:
  7.2 84.0 %copy-start.3 = (bf16[128,3456]{1,0:T(8,128)(2,1)S(1)}, bf16[128,3456]{1,0:T(8,128)(2,1)}, u32[]{:S(2)}) copy-start(bf16[128,3456]{1,0:T(8,128)(2,1)} %cot_ref.1) | copy-start | bytes 2654212
  7.2 84.0 %copy-start.14 = (s32[32]{0:T(128)S(1)}, s32[32]{0:T(128)}, u32[]{:S(2)}) copy-start(s32[32]{0:T(128)} %owner_ref.1) | copy-start | bytes 388
  7.2 84.0 %all-gather.2.cloned.1.call-start = ((), (), s32[]{:S(2)}) async-start(), calls=%async_computation.4 | async-start | bytes 7520256 | tf_op jit(solution)/shard_map/all_gather | solution.py:224
  10.6 1.2 copy-start
  25.2 79.0 %copy-start.2 = (bf16[512,256]{1,0:T(8,128)(2,1)S(1)}, bf16[512,256]{1,0:T(8,128)(2,1)}, u32[]{:S(2)}) copy-start(bf16[512,256]{1,0:T(8,128)(2,1)} %w2.3) | copy-start | bytes 786436
  25.2 79.0 %copy-start.5 = (bf16[256,128]{1,0:T(8,128)(2,1)S(1)}, bf16[256,128]{1,0:T(8,128)(2,1)}, u32[]{:S(2)}) copy-start(bf16[256,128]{1,0:T(8,128)(2,1)} %w3.3) | copy-start | bytes 196612
  25.2 79.0 %copy-start.7 = (bf16[13,512]{1,0:T(8,128)(2,1)S(1)}, bf16[13,512]{1,0:T(8,128)(2,1)}, u32[]{:S(2)}) copy-start(bf16[13,512]{1,0:T(8,128)(2,1)} %w1.3) | copy-start | bytes 39940
  25.2 79.0 %copy-start.9 = (f32[512]{0:T(512)S(1)}, f32[512]{0:T(512)}, u32[]{:S(2)}) copy-start(f32[512]{0:T(512)} %param.21) | copy-start | bytes 6148
  25.2 79.0 %copy-start.11 = (f32[256]{0:T(256)S(1)}, f32[256]{0:T(256)}, u32[]{:S(2)}) copy-start(f32[256]{0:T(256)} %param.23) | copy-start | bytes 3076
  25.2 79.0 %copy-start.13 = (f32[128]{0:T(128)S(1)}, f32[128]{0:T(128)}, u32[]{:S(2)}) copy-start(f32[128]{0:T(128)} %param.25) | copy-start | bytes 1540
  25.2 48.2 %all-to-all-start = ((bf16[16,128,256]{2,1,0:T(8,128)(2,1)}), bf16[16,128,256]{2,1,0:T(8,128)(2,1)S(1)}, u32[]{:S(2)}, u32[]{:S(2)}) async-start(bf16[16,128,256]{2,1,0:T(8,128)(2,1)} %bitcast.2), calls=%async_computation | async-start | bytes 2097152 | tf_op jit(solution)/shard_map/all_to_all | solution.py:227
  37.2 1.0 copy-start.1
  38.2 0.8 copy-start.4
  39.0 0.7 copy-start.6
  39.8 0.7 copy-start.8
  40.4 0.7 copy-start.10
  41.1 0.7 copy-start.12
  99.4 32.7 %all-to-all-start.1 = ((bf16[16,128,256]{2,1,0:T(8,128)(2,1)}), bf16[16,128,256]{2,1,0:T(8,128)(2,1)S(1)}, u32[]{:S(2)}, u32[]{:S(2)}) async-start(bf16[16,128,256]{2,1,0:T(8,128)(2,1)} %get-tuple-element.15), calls=%async_computation.1 | async-start | bytes 2097152 | tf_op jit(solution)/shard_map/all_to_all | solution.py:242
  132.1 19.2 %all-to-all-start.3 = ((bf16[16,96,128]{2,1,0:T(8,128)(2,1)}), bf16[16,96,128]{2,1,0:T(8,128)(2,1)S(1)}, u32[]{:S(2)}, u32[]{:S(2)}) async-start(bf16[16,96,128]{2,1,0:T(8,128)(2,1)} %bitcast.8), calls=%async_computation.3 | async-start | bytes 786432 | tf_op jit(solution)/shard_map/all_to_all | solution.py:256
  151.3 82.0 %all-to-all-start.2 = ((bf16[32,2,64,128]{3,2,1,0:T(8,128)(2,1)}), bf16[32,2,64,128]{3,2,1,0:T(8,128)(2,1)S(1)}, u32[]{:S(2)}, u32[]{:S(2)}) async-start(bf16[32,2,64,128]{3,2,1,0:T(8,128)(2,1)} %table_grads.1), calls=%async_computation.2 | async-start | bytes 2097152 | tf_op jit(solution)/shard_map/all_to_all | solution.py:245
Sparse Core Ops, SparseCore 0:
  10.7 80.4 all-gather.1

commit v2 on v1

--- a/solution.py
+++ b/solution.py
@@ -17,7 +17,7 @@
 TABLE = ("y", "c")
 DP = ("x", "z")
 EVERY = ("x", "z", "y", "c")
-CHUNK = 96
+CHUNK = 192
 
 NT = (((1,), (1,)), ((), ()))
 TN = (((0,), (0,)), ((), ()))
@@ -27,7 +27,7 @@
     return lax.dot_general(a, b, dims, preferred_element_type=jnp.float32)
 
 
-def params(megabytes=48):
+def params(megabytes):
     return pltpu.CompilerParams(vmem_limit_bytes=megabytes * 1024 * 1024)
 
 
@@ -50,10 +50,11 @@
         )
         hits = dot(left, right, NT).astype(jnp.bfloat16)
         for part in range(rows // LOW):
-            hits_ref[0, pl.ds(group * GROUP, GROUP), pl.ds(part * LOW, LOW)] = hits[
-                part * GROUP : (part + 1) * GROUP
-            ]
-    pooled_ref[...] = dot(hits_ref[0], table_ref[0]).astype(jnp.bfloat16)
+            hits_ref[0, part, pl.ds(group * GROUP, GROUP), :] = hits[part * GROUP : (part + 1) * GROUP]
+    total = dot(hits_ref[0, 0], table_ref[0, 0:LOW])
+    for part in range(1, rows // LOW):
+        total = total + dot(hits_ref[0, part], table_ref[0, part * LOW : part * LOW + LOW])
+    pooled_ref[...] = total.astype(jnp.bfloat16)
 
 
 def pool(lookup_ids, lookup_counts, embed_tables):
@@ -71,39 +72,54 @@
             pl.BlockSpec((1, rows, WIDTH), lambda s, b: (s, 0, 0)),
         ],
         out_specs=[
-            pl.BlockSpec((1, BLOCK, rows), lambda s, b: (s, b, 0)),
+            pl.BlockSpec((1, rows // LOW, BLOCK, LOW), lambda s, b: (s, 0, b, 0)),
             pl.BlockSpec((BLOCK, WIDTH), lambda s, b: (b, s)),
         ],
         out_shape=[
-            jax.ShapeDtypeStruct((shards, batch, rows), jnp.bfloat16),
+            pltpu.HBM((shards, rows // LOW, batch, LOW), jnp.bfloat16),
             jax.ShapeDtypeStruct((batch, shards * WIDTH), jnp.bfloat16),
         ],
-        compiler_params=params(),
+        compiler_params=params(8),
         name="pool",
     )(code, embed_tables)
 
 
-def table_grad_kernel(hits_ref, grad_ref, out_ref):
-    total = dot(hits_ref[0], grad_ref[...], TN).astype(jnp.bfloat16)
+def table_grad_kernel(hits_ref, grad_ref, out_ref, turned):
+    @pl.when(pl.program_id(0) == 0)
+    def _():
+        turned[...] = grad_ref[...].T
+
+    total = dot(turned[...], hits_ref[0, 0]).T.astype(jnp.bfloat16)
     out_ref[...] = total.reshape(out_ref.shape)
 
 
-def table_grads(hits, grads, parts):
-    shards, batch, rows = hits.shape
-    each = rows // parts
-    step = BLOCK // each
+def table_grads(hits, grads, shard, parts, extra=()):
+    shards, blocks, batch, low = hits.shape
+    each = blocks * low // parts
+    step = low // each
+    hbm = pl.BlockSpec(memory_space=pl.ANY)
+
+    def kernel(hits_ref, grad_ref, *rest):
+        table_grad_kernel(hits_ref, grad_ref, rest[-2], rest[-1])
+
     return pl.pallas_call(
-        table_grad_kernel,
-        grid=(shards, rows // BLOCK),
+        kernel,
+        grid=(blocks,),
         in_specs=[
-            pl.BlockSpec((1, batch, BLOCK), lambda s, r: (s, 0, r)),
-            pl.BlockSpec((batch, WIDTH), lambda s, r: (0, s)),
-        ],
-        out_specs=pl.BlockSpec((step, 1, each, WIDTH), lambda s, r: (r, s, 0, 0)),
+            pl.BlockSpec((1, 1, batch, low), lambda r: (shard, r, 0, 0)),
+            pl.BlockSpec((batch, WIDTH), lambda r: (0, shard)),
+        ]
+        + [hbm] * len(extra),
+        out_specs=pl.BlockSpec((step, 1, each, WIDTH), lambda r: (r, shard, 0, 0)),
         out_shape=jax.ShapeDtypeStruct((parts, shards, each, WIDTH), jnp.bfloat16),
-        compiler_params=params(),
+        scratch_shapes=[pltpu.VMEM((WIDTH, batch), jnp.bfloat16)],
+        input_output_aliases={2: 0} if shard else {},
+        compiler_params=params(46),
+        cost_estimate=pl.CostEstimate(
+            flops=2 * batch * blocks * low * WIDTH, bytes_accessed=2 * batch * (blocks * low + 2 * WIDTH), transcendentals=0
+        ),
         name="table_grads",
-    )(hits, grads)
+    )(hits, grads, *extra)
 
 
 def silu(value):
@@ -155,13 +171,35 @@
     out_ref[1392:1536, :] = jnp.zeros((144, 128), jnp.bfloat16)
 
 
+def unpack_kernel(whole, first_grad, second_grad, third_grad, first_sum, second_sum, third_sum, bias_sum):
+    second_grad[:, 0:128] = whole[0:512].astype(jnp.float32)
+    second_grad[:, 128:256] = whole[512:1024].astype(jnp.float32)
+    third_grad[...] = whole[1024:1280].astype(jnp.float32)
+    for part in range(4):
+        block = whole[1280 + 16 * part : 1296 + 16 * part].astype(jnp.float32)
+        first_grad[:, part * 128 : part * 128 + 128] = block[0:13]
+    sums = whole[1344:1360].astype(jnp.float32)
+    for part in range(4):
+        first_sum[:, part * 128 : part * 128 + 128] = sums[part : part + 1]
+    for part in range(2):
+        second_sum[:, part * 128 : part * 128 + 128] = sums[4 + part : 5 + part]
+    third_sum[...] = sums[6:7]
+    biases = whole[1360:1392].astype(jnp.float32)
+    for part in range(27):
+        bias_sum[:, part * 128 : part * 128 + 128] = biases[part : part + 1]
+
+
 def cross_kernel(
     owner_ref, arrived_ref, bottom_ref, weights_ref, bias_ref, cot_ref,
-    send_ref, bottom_grad_ref, bias_grad_ref, total, inputs, mixed, grads,
+    send_ref, bottom_grad_ref, bias_grad_ref, total, inputs, mixed, grads, up, down, arrived_at,
 ):
     blocks = total.shape[0]
     wide = blocks * WIDTH
     shards = owner_ref.shape[0]
+    fetch_down = pltpu.make_async_copy(weights_ref.at[:, wide : 2 * wide], down, arrived_at.at[0])
+    fetch_up = pltpu.make_async_copy(weights_ref.at[:, 0:wide], up, arrived_at.at[1])
+    fetch_down.start()
+    fetch_up.start()
     total[1:] = jnp.zeros_like(total[1:])
     total[0] = bottom_ref[...].astype(jnp.float32)
     for shard in range(shards):
@@ -176,13 +214,15 @@
         mix_grad = cot_ref[:, columns].astype(jnp.float32) * piece.astype(jnp.float32)
         mixed[:, columns] = mix_grad.astype(jnp.bfloat16)
         bias_grad_ref[block : block + 1, :] = jnp.sum(mix_grad, axis=0, keepdims=True)
-    low_rank = dot(inputs[...], weights_ref[:, wide:], NT).astype(jnp.bfloat16)
-    rank_grad = dot(mixed[...], weights_ref[:, :wide], NT).astype(jnp.bfloat16)
+    fetch_down.wait()
+    low_rank = dot(inputs[...], down[...], NT).astype(jnp.bfloat16)
+    fetch_up.wait()
+    rank_grad = dot(mixed[...], up[...], NT).astype(jnp.bfloat16)
     step = 3 * WIDTH
     for part in range(wide // step):
         columns = slice(part * step, part * step + step)
-        mixing = dot(low_rank, weights_ref[:, columns]) + bias_ref[:, columns]
-        back = dot(rank_grad, weights_ref[:, wide + part * step : wide + part * step + step])
+        mixing = dot(low_rank, up[:, columns]) + bias_ref[:, columns]
+        back = dot(rank_grad, down[:, columns])
         grad = (cot_ref[:, columns].astype(jnp.float32) * (mixing + 1.0) + back).astype(jnp.bfloat16)
         for inner in range(3):
             grads[part * 3 + inner] = grad[:, inner * WIDTH : inner * WIDTH + WIDTH]
@@ -197,7 +237,7 @@
     vmem = pl.BlockSpec(memory_space=pltpu.VMEM)
     return pl.pallas_call(
         cross_kernel,
-        in_specs=[pl.BlockSpec(memory_space=pltpu.SMEM)] + [vmem] * 5,
+        in_specs=[pl.BlockSpec(memory_space=pltpu.SMEM), vmem, vmem, pl.BlockSpec(memory_space=pltpu.HBM), vmem, vmem],
         out_specs=[vmem] * 3,
         out_shape=[
             jax.ShapeDtypeStruct(arrived.shape, jnp.bfloat16),
@@ -209,10 +249,58 @@
             pltpu.VMEM((examples, wide), jnp.bfloat16),
             pltpu.VMEM((examples, wide), jnp.bfloat16),
             pltpu.VMEM((blocks, examples, WIDTH), jnp.bfloat16),
-        ],
-        compiler_params=params(),
+            pltpu.VMEM((weights.shape[0], wide), jnp.bfloat16),
+            pltpu.VMEM((weights.shape[0], wide), jnp.bfloat16),
+            pltpu.SemaphoreType.DMA((2,)),
+        ],
+        compiler_params=params(55),
         name="cross",
     )(shard_table, arrived, bottom_out, weights, cross_bias, cotangent)
+
+
+def spread_sum(value, axis, distances, after=None):
+    size = lax.axis_size(axis)
+    for distance in distances:
+        sent = value.astype(jnp.bfloat16)
+        came = lax.ppermute(sent, axis, [(place, place ^ distance) for place in range(size)])
+        if after is None:
+            value = sent.astype(jnp.float32) + came.astype(jnp.float32)
+        else:
+            value = add_after(sent, came, after)
+    return value
+
+
+def add_kernel(one_ref, other_ref, after_ref, out_ref):
+    out_ref[...] = (one_ref[...].astype(jnp.float32) + other_ref[...].astype(jnp.float32)).astype(jnp.bfloat16)
+
+
+def add_after(one, other, after):
+    vmem = pl.BlockSpec(memory_space=pltpu.VMEM)
+    return pl.pallas_call(
+        add_kernel,
+        in_specs=[vmem, vmem, pl.BlockSpec(memory_space=pl.ANY)],
+        out_specs=vmem,
+        out_shape=jax.ShapeDtypeStruct(one.shape, jnp.bfloat16),
+        compiler_params=params(4),
+        name="add_after",
+    )(one, other, after)
+
+
+def hold(value, after):
+    anywhere = pl.BlockSpec(memory_space=pl.ANY)
+
+    def kernel(value_ref, after_ref, out_ref):
+        pass
+
+    return pl.pallas_call(
+        kernel,
+        in_specs=[anywhere, anywhere],
+        out_specs=anywhere,
+        out_shape=jax.ShapeDtypeStruct(value.shape, value.dtype),
+        input_output_aliases={0: 0},
+        compiler_params=params(4),
+        name="hold",
+    )(value, after)
 
 
 def local(
@@ -235,40 +323,66 @@
         in_specs=[vmem] * 7,
         out_specs=vmem,
         out_shape=jax.ShapeDtypeStruct((examples, WIDTH), jnp.bfloat16),
-        compiler_params=params(),
+        compiler_params=params(8),
         name="bottom",
     )(*bottom_args)
     send, bottom_grad, bias_part = cross(shard_table, arrived, bottom_out, weights, cross_bias[None], cotangent)
     returned = lax.all_to_all(send, TABLE, split_axis=0, concat_axis=0, tiled=True)
     parts = lax.axis_size("x") * lax.axis_size("z")
-    table_parts = table_grads(hits, returned.reshape(-1, returned.shape[2]), parts)
-    table_parts = lax.all_to_all(table_parts, DP, split_axis=0, concat_axis=0, tiled=True)
-    table_grad = jnp.sum(table_parts.astype(jnp.float32), axis=0)
-
     packed = pl.pallas_call(
         bottom_back_kernel,
         in_specs=[vmem] * 9,
         out_specs=vmem,
-        out_shape=jax.ShapeDtypeStruct((devices * CHUNK, 128), jnp.bfloat16),
-        compiler_params=params(),
+        out_shape=jax.ShapeDtypeStruct((8 * CHUNK, 128), jnp.bfloat16),
+        compiler_params=params(8),
         name="bottom_back",
     )(*bottom_args, bottom_grad, bias_part)
-    packed = lax.all_to_all(packed.reshape(devices, CHUNK, 128), TABLE, split_axis=0, concat_axis=0, tiled=True)
-    summed = jnp.sum(packed.astype(jnp.float32), axis=0)
-    summed = lax.psum(lax.psum(summed, "x"), "z").astype(jnp.bfloat16)
-    summed = lax.all_gather(summed, TABLE, axis=0, tiled=True)
-    whole = summed.astype(jnp.float32)
-    second_grad = jnp.concatenate([whole[0:512], whole[512:1024]], axis=1)
-    first_grad = jnp.concatenate([whole[1280 + 16 * part : 1293 + 16 * part] for part in range(4)], axis=1)
+    core, column = lax.axis_index("c"), lax.axis_index("x")
+    length = lax.axis_size("x")
+    packed = packed.reshape(length, 2, CHUNK, 128)
+    theirs = lax.dynamic_index_in_dim(packed, 1 - core, axis=1, keepdims=False)
+    came = lax.ppermute(theirs, "c", [(0, 1), (1, 0)])
+    mine = lax.dynamic_index_in_dim(packed, core, axis=1, keepdims=False)
+    both = mine.astype(jnp.float32) + came.astype(jnp.float32)
+    part = lax.dynamic_index_in_dim(both, column, axis=0, keepdims=False)
+    narrow = both.astype(jnp.bfloat16)
+    for shift in range(1, length):
+        piece = lax.dynamic_index_in_dim(narrow, (column + shift) % length, axis=0, keepdims=False)
+        piece = lax.ppermute(piece, "x", [(place, (place + shift) % length) for place in range(length)])
+        part = part + piece.astype(jnp.float32)
+    part = spread_sum(part, "z", (1,))
+    part = spread_sum(part, "z", (2,), returned)
+    part = spread_sum(part, "z", (4,))
+
+    returned = returned.reshape(-1, returned.shape[2])
+    table_parts = table_grads(hits, returned, 0, parts)
+    for shard in range(1, hits.shape[0]):
+        table_parts = table_grads(hits, returned, shard, parts, (table_parts, part))
+    part = spread_sum(part, "y", (1,))
+    table_parts = hold(table_parts, part)
+    table_parts = lax.all_to_all(table_parts, DP, split_axis=0, concat_axis=0, tiled=True)
+    table_grad = jnp.sum(table_parts.astype(jnp.float32), axis=0)
+
+    part = spread_sum(part, "y", (2, 4)).astype(jnp.bfloat16)
+    other = lax.ppermute(part, "c", [(0, 1), (1, 0)])
+    pair = jnp.where(core == 0, jnp.stack([part, other]), jnp.stack([other, part]))
+    whole = lax.all_gather(pair.reshape(2 * CHUNK, 128), "x", axis=0, tiled=True)
+    first_grad, second_grad, third_grad, first_sum, second_sum, third_sum, bias_sum = pl.pallas_call(
+        unpack_kernel,
+        in_specs=[vmem],
+        out_specs=[vmem] * 7,
+        out_shape=[
+            jax.ShapeDtypeStruct(shape, jnp.float32)
+            for shape in (
+                first_layer.shape, second_layer.shape, third_layer.shape, (1, first_layer.shape[1]),
+                (1, second_layer.shape[1]), (1, third_layer.shape[1]), (1, cross_bias.shape[0]),
+            )
+        ],
+        compiler_params=params(8),
+        name="unpack",
+    )(whole)
     return (
-        table_grad,
-        first_grad,
-        whole[1344:1348].reshape(-1),
-        second_grad,
-        whole[1348:1350].reshape(-1),
-        whole[1024:1280],
-        whole[1350],
-        whole[1360:1387].reshape(-1),
+        table_grad, first_grad, first_sum[0], second_grad, second_sum[0], third_grad, third_sum[0], bias_sum[0],
     )
 
 

time: 242 us -> 214 us (0.88)
  blocking collectives: 67.5 us -> 11.1 us
  starting transfers between devices: 28.7 us -> 67.5 us
  waiting for transfers between devices: 75.1 us -> 60.6 us
  Pallas kernels: 39.5 us -> 42.5 us
    ppermute x0 -> x11, starting transfers between devices: none -> 48.3 us  [the longest x6 28.9 us: spread_sum(): lax.ppermute(sent, axis, [(place, place ^ distance) for place in range(si...]
    psum x2 -> x0, blocking collectives: 42.3 us -> none  [local(): summed = lax.psum(lax.psum(summed, 'x'), 'z').astype(jnp.bfloat16)]
    all_to_all x1, waiting for transfers between devices: 26.2 us -> 0.01 us  [local(): lax.all_to_all(send, TABLE, split_axis=0, concat_axis=0, tiled=True)]
    ppermute x0 -> x11, waiting for transfers between devices: none -> 14.6 us  [the longest x6 8.61 us: spread_sum(): lax.ppermute(sent, axis, [(place, place ^ distance) for place in range(si...]
    all_gather x1, blocking collectives: 25.2 us -> 11.1 us  [local(): lax.all_gather(pair.reshape(2 * CHUNK, 128), 'x', axis=0, tiled=True)]
    all_to_all x1, starting transfers between devices: 9.92 us -> 3.94 us  [local(): lax.all_to_all(table_parts, DP, split_axis=0, concat_axis=0, tiled=True)]
    all_to_all x1 -> x0, starting transfers between devices: 3.53 us -> none  [local(): lax.all_to_all(packed.reshape(devices, CHUNK, 128), TABLE, split_axis=0,...]
    unnamed x31 -> x35, local copies, waits for them, and re-layouts: 6.6 us -> 8.66 us
  transfers between devices with their start and end apart: 5 -> 15, of which waited for: 3 -> 10; matrix products, arithmetic and copies ran while one was open for 3% -> 2% of each run, Pallas kernels for 13% -> 16%
where the time goes in v2:
time: 214 us; the launch traced here: 211 us
  starting transfers between devices  67.5 us (32%)
  waiting for transfers between devices  60.6 us (28%)
  Pallas kernels  42.5 us (20%)
  between operations  14.4 us (7%)
  blocking collectives  11.1 us (5%)
  local copies, waits for them, and re-layouts  10.5 us (5%)
  other arithmetic  4.37 us (2%)
    all_to_all x1, waiting for transfers between devices, local(): lax.all_to_all(pooled, TABLE, split_axis=0, concat_axis=0, tiled=True)  29.9 us
    ppermute x6, starting transfers between devices, spread_sum(): lax.ppermute(sent, axis, [(place, place ^ distance) for place in range(si...  28.9 us
    pallas_call x2, Pallas kernels, table_grads(): pl.pallas_call(kernel, grid=(blocks,), in_specs=[pl.BlockSpec((1, 1, batc...  16.4 us
    all_gather x1, waiting for transfers between devices, local(): lax.all_gather(jnp.concatenate([cross_up, cross_down.T], axis=1), TABLE,...  16.1 us
    pallas_call x1, Pallas kernels, pool(): pl.pallas_call(pool_kernel, grid=(shards, batch // BLOCK), in_specs=[pl.B...  15.1 us
    all_gather x1, blocking collectives, local(): lax.all_gather(pair.reshape(2 * CHUNK, 128), 'x', axis=0, tiled=True)  11.1 us
    all_to_all x1, starting transfers between devices, local(): lax.all_to_all(pooled, TABLE, split_axis=0, concat_axis=0, tiled=True)  10.5 us
    ppermute x3, starting transfers between devices, local(): lax.ppermute(piece, 'x', [(place, (place + shift) % length) for place in...  9.27 us
  transfers between devices with their start and end apart: 15, of which 10 were waited for; matrix products, arithmetic and copies ran while one was open for 2% of the time, Pallas kernels for 16%

profile of v2, /device:TPU:1, one launch (start us, length us, event | category | flops | bytes accessed | tf_op | source)
XLA Modules:
  0.0 210.9 jit_solution(14625656571278562992)
XLA Ops:
  11.7 15.1 %pool.1 = (bf16[2,8,2048,256]{3,2,1,0:T(8,128)(2,1)}, bf16[2048,256]{1,0:T(8,128)(2,1)}) custom-call(s32[2,64,256]{2,1,0:T(8,128)S(1)} %copy.30.code_ref, bf16[2,2048,128]{2,1,0:T(8,128)(2,1)S(1)} %copy-done), custom_call_target="tpu_custom_call" | custom-call | tf_op jit(solution)/shard_map/pool/pallas_call | solution.py:67
  26.9 10.5 %all-to-all-start = ((bf16[16,128,256]{2,1,0:T(8,128)(2,1)}), bf16[16,128,256]{2,1,0:T(8,128)(2,1)S(1)}, u32[]{:S(2)}, u32[]{:S(2)}) async-start(bf16[16,128,256]{2,1,0:T(8,128)(2,1)} %bitcast.2), calls=%async_computation | async-start | bytes 2097152 | tf_op jit(solution)/shard_map/all_to_all | solution.py:315
  45.2 29.9 %all-to-all-done.arrived_ref = bf16[16,128,256]{2,1,0:T(8,128)(2,1)S(1)} async-done(((bf16[16,128,256]{2,1,0:T(8,128)(2,1)}), bf16[16,128,256]{2,1,0:T(8,128)(2,1)S(1)}, u32[]{:S(2)}, u32[]{:S(2)}) %all-to-all-start) | async-done | bytes 1048608 | tf_op jit(solution)/shard_map/all_to_all | solution.py:315
  75.1 16.1 %all-gather.2.cloned.1.call-done.weights_ref = bf16[512,6912]{1,0:T(8,128)(2,1)} async-done(((bf16[32,6912]{1,0:T(8,128)(2,1)}), bf16[512,6912]{1,0:T(8,128)(2,1)}) %all-gather.2.cloned.1.call-update) | async-done | bytes 7077904 | tf_op jit(solution)/shard_map/all_gather | solution.py:312
  91.2 8.6 %cross.1 = (bf16[16,128,256]{2,1,0:T(8,128)(2,1)}, bf16[128,128]{1,0:T(8,128)(2,1)}, f32[32,128]{1,0:T(8,128)}) custom-call(s32[32]{0:T(128)} %owner_ref.1, bf16[16,128,256]{2,1,0:T(8,128)(2,1)} %copy-done.16, bf16[128,128]{1,0:T(8,128)(2,1)} %copy-done.5, bf16[512,6912]{1,0:T(8,128)(2,1)} %all-gather.2.cloned.1.call-done.weights_ref, ...), custom_call_target="tpu_custom_call" | custom-call | tf_op jit(solution)/shard_map/cross/pallas_call | solution.py:238
  99.8 4.7 %all-to-all-start.1 = ((bf16[16,128,256]{2,1,0:T(8,128)(2,1)}), bf16[16,128,256]{2,1,0:T(8,128)(2,1)S(1)}, u32[]{:S(2)}, u32[]{:S(2)}) async-start(bf16[16,128,256]{2,1,0:T(8,128)(2,1)} %get-tuple-element.22), calls=%async_computation.1 | async-start | bytes 2097152 | tf_op jit(solution)/shard_map/all_to_all | solution.py:330
  107.0 2.0 collective-permute-start
  110.4 4.3 %collective-permute-start.3 = (bf16[192,128]{1,0:T(8,128)(2,1)S(1)}, bf16[192,128]{1,0:T(8,128)(2,1)S(1)}, u32[]{:S(2)}, u32[]{:S(2)}) collective-permute-start(bf16[192,128]{1,0:T(8,128)(2,1)S(1)} %get-tuple-element.35), channel_id=1, source_target_pairs={{0,384},{128,0},{256,128},{384,256},{1,385},{129,1},{257,129},{385... | collective-permute-start | bytes 147464 | tf_op jit(solution)/shard_map/ppermute | solution.py:351
  114.8 2.5 %collective-permute-start.2 = (bf16[192,128]{1,0:T(8,128)(2,1)S(1)}, bf16[192,128]{1,0:T(8,128)(2,1)S(1)}, u32[]{:S(2)}, u32[]{:S(2)}) collective-permute-start(bf16[192,128]{1,0:T(8,128)(2,1)S(1)} %get-tuple-element.36), channel_id=1, source_target_pairs={{0,256},{128,384},{256,0},{384,128},{1,257},{129,385},{257,1},{385... | collective-permute-start | bytes 147464 | tf_op jit(solution)/shard_map/ppermute | solution.py:351
  117.3 2.5 %collective-permute-start.1 = (bf16[192,128]{1,0:T(8,128)(2,1)S(1)}, bf16[192,128]{1,0:T(8,128)(2,1)S(1)}, u32[]{:S(2)}, u32[]{:S(2)}) collective-permute-start(bf16[192,128]{1,0:T(8,128)(2,1)S(1)} %get-tuple-element.34), channel_id=1, source_target_pairs={{0,128},{128,256},{256,384},{384,0},{1,129},{129,257},{257,385},{3... | collective-permute-start | bytes 147464 | tf_op jit(solution)/shard_map/ppermute | solution.py:351
  121.4 2.2 %collective-permute-done.1 = bf16[192,128]{1,0:T(8,128)(2,1)S(1)} collective-permute-done((bf16[192,128]{1,0:T(8,128)(2,1)S(1)}, bf16[192,128]{1,0:T(8,128)(2,1)S(1)}, u32[]{:S(2)}, u32[]{:S(2)}) %collective-permute-start.1) | collective-permute-done | bytes 49184 | tf_op jit(solution)/shard_map/ppermute | solution.py:351
  123.6 3.3 %collective-permute-start.4 = (bf16[192,128]{1,0:T(8,128)(2,1)S(1)}, bf16[192,128]{1,0:T(8,128)(2,1)S(1)}, u32[]{:S(2)}, u32[]{:S(2)}) collective-permute-start(bf16[192,128]{1,0:T(8,128)(2,1)S(1)} %fusion.3), channel_id=1, source_target_pairs={{0,16},{16,0},{32,48},{48,32},{64,80},{80,64},{96,112},{112,96},{1... | collective-permute-start | bytes 147464 | tf_op jit(solution)/shard_map/ppermute | solution.py:265
  128.8 4.3 %collective-permute-start.5 = (bf16[192,128]{1,0:T(8,128)(2,1)S(1)}, bf16[192,128]{1,0:T(8,128)(2,1)S(1)}, u32[]{:S(2)}, u32[]{:S(2)}) collective-permute-start(bf16[192,128]{1,0:T(8,128)(2,1)S(1)} %add_convert_fusion.2.one_ref), channel_id=1, source_target_pairs={{0,32},{16,48},{32,0},{48,16},{64,96},{80,112},{96,64},{112,80},{1... | collective-permute-start | bytes 147464 | tf_op jit(solution)/shard_map/ppermute | solution.py:265
  134.6 8.2 %collective-permute-start.6 = (bf16[192,128]{1,0:T(8,128)(2,1)S(1)}, bf16[192,128]{1,0:T(8,128)(2,1)S(1)}, u32[]{:S(2)}, u32[]{:S(2)}) collective-permute-start(bf16[192,128]{1,0:T(8,128)(2,1)S(1)} %add_after.1), channel_id=1, source_target_pairs={{0,64},{16,80},{32,96},{48,112},{64,0},{80,16},{96,32},{112,48},{1... | collective-permute-start | bytes 147464 | tf_op jit(solution)/shard_map/ppermute | solution.py:265
  142.8 8.2 %table_grads.2.rest_0_ = bf16[32,2,64,128]{3,2,1,0:T(8,128)(2,1)} custom-call(bf16[2,8,2048,256]{3,2,1,0:T(8,128)(2,1)} %get-tuple-element.20.hits_ref, bf16[2048,256]{1,0:T(8,128)(2,1)S(1)} %bitcast.37), custom_call_target="tpu_custom_call" | custom-call | flops 1073741824 | bytes 9437184 | tf_op jit(solution)/shard_map/table_grads/pallas_call | solution.py:105
  151.0 3.3 %collective-permute-start.7 = (bf16[192,128]{1,0:T(8,128)(2,1)S(1)}, bf16[192,128]{1,0:T(8,128)(2,1)S(1)}, u32[]{:S(2)}, u32[]{:S(2)}) collective-permute-start(bf16[192,128]{1,0:T(8,128)(2,1)S(1)} %get-tuple-element.39), channel_id=1, source_target_pairs={{0,2},{2,0},{4,6},{6,4},{8,10},{10,8},{12,14},{14,12},{1,3},{3,1},... | collective-permute-start | bytes 147464 | tf_op jit(solution)/shard_map/ppermute | solution.py:265
  154.3 8.2 %table_grads.3.value_ref = bf16[32,2,64,128]{3,2,1,0:T(8,128)(2,1)} custom-call(bf16[2,8,2048,256]{3,2,1,0:T(8,128)(2,1)} %get-tuple-element.20.hits_ref, bf16[2048,256]{1,0:T(8,128)(2,1)S(1)} %bitcast.38, bf16[32,2,64,128]{3,2,1,0:T(8,128)(2,1)} %table_grads.2.rest_0_, f32[192,128]{1,0:T(8,128)S(1)} %get-tuple-element.40.rest_1_), custom_call_target="tpu_custom_call", output_to_operand_aliasing={{}: (2, {})} | custom-call | flops 1073741824 | bytes 9437184 | tf_op jit(solution)/shard_map/table_grads/pallas_call | solution.py:105
  162.5 3.9 %all-to-all-start.2 = ((bf16[32,2,64,128]{3,2,1,0:T(8,128)(2,1)}), bf16[32,2,64,128]{3,2,1,0:T(8,128)(2,1)S(1)}, u32[]{:S(2)}, u32[]{:S(2)}) async-start(bf16[32,2,64,128]{3,2,1,0:T(8,128)(2,1)} %hold.1), calls=%async_computation.2 | async-start | bytes 2097152 | tf_op jit(solution)/shard_map/all_to_all | solution.py:363
  166.5 4.0 %collective-permute-start.8 = (bf16[192,128]{1,0:T(8,128)(2,1)S(1)}, bf16[192,128]{1,0:T(8,128)(2,1)S(1)}, u32[]{:S(2)}, u32[]{:S(2)}) collective-permute-start(bf16[192,128]{1,0:T(8,128)(2,1)S(1)} %get-tuple-element.37), channel_id=1, source_target_pairs={{0,4},{2,6},{4,0},{6,2},{8,12},{10,14},{12,8},{14,10},{1,5},{3,7},... | collective-permute-start | bytes 147464 | tf_op jit(solution)/shard_map/ppermute | solution.py:265
  170.5 2.1 collective-permute-done.8
  172.6 5.8 %collective-permute-start.9 = (bf16[192,128]{1,0:T(8,128)(2,1)S(1)}, bf16[192,128]{1,0:T(8,128)(2,1)S(1)}, u32[]{:S(2)}, u32[]{:S(2)}) collective-permute-start(bf16[192,128]{1,0:T(8,128)(2,1)S(1)} %add_convert_fusion.1), channel_id=1, source_target_pairs={{0,8},{2,10},{4,12},{6,14},{8,0},{10,2},{12,4},{14,6},{1,9},{3,11}... | collective-permute-start | bytes 147464 | tf_op jit(solution)/shard_map/ppermute | solution.py:265
  178.3 3.2 %collective-permute-done.9 = bf16[192,128]{1,0:T(8,128)(2,1)S(1)} collective-permute-done((bf16[192,128]{1,0:T(8,128)(2,1)S(1)}, bf16[192,128]{1,0:T(8,128)(2,1)S(1)}, u32[]{:S(2)}, u32[]{:S(2)}) %collective-permute-start.9) | collective-permute-done | bytes 49184 | tf_op jit(solution)/shard_map/ppermute | solution.py:265
  181.6 8.2 %collective-permute-start.10 = (bf16[192,128]{1,0:T(8,128)(2,1)S(1)}, bf16[192,128]{1,0:T(8,128)(2,1)S(1)}, u32[]{:S(2)}, u32[]{:S(2)}) collective-permute-start(bf16[192,128]{1,0:T(8,128)(2,1)S(1)} %add_convert_fusion), channel_id=1, source_target_pairs={{0,1},{1,0},{2,3},{3,2},{4,5},{5,4},{6,7},{7,6},{8,9},{9,8},{10,11... | collective-permute-start | bytes 147464 | tf_op jit(solution)/shard_map/ppermute | solution.py:367
  190.6 11.1 %all_gather.7.whole = bf16[1536,128]{1,0:T(8,128)(2,1)S(1)} all-gather(bf16[384,128]{1,0:T(8,128)(2,1)S(1)} %bitcast.49), channel_id=1, replica_groups=mesh['x'=4,'z'=8,'y'=8,'c'=2] {'x'}, dimensions={0}, use_global_device_ids=true | all-gather | bytes 491520 | tf_op jit(solution)/shard_map/all_gather | solution.py:369
  (70 shorter events, 24.4 us)
Async XLA Ops:
  7.2 84.0 %all-gather.2.cloned.1.call-start = ((), (), s32[]{:S(2)}) async-start(), calls=%async_computation.3 | async-start | bytes 7520256 | tf_op jit(solution)/shard_map/all_gather | solution.py:312
  10.5 1.2 copy-start
  26.9 77.7 %copy-start.2 = (bf16[512,256]{1,0:T(8,128)(2,1)S(1)}, bf16[512,256]{1,0:T(8,128)(2,1)}, u32[]{:S(2)}) copy-start(bf16[512,256]{1,0:T(8,128)(2,1)} %w2.3) | copy-start | bytes 786436
  26.9 77.7 %copy-start.4 = (bf16[256,128]{1,0:T(8,128)(2,1)S(1)}, bf16[256,128]{1,0:T(8,128)(2,1)}, u32[]{:S(2)}) copy-start(bf16[256,128]{1,0:T(8,128)(2,1)} %w3.3) | copy-start | bytes 196612
  26.9 77.7 %copy-start.7 = (bf16[13,512]{1,0:T(8,128)(2,1)S(1)}, bf16[13,512]{1,0:T(8,128)(2,1)}, u32[]{:S(2)}) copy-start(bf16[13,512]{1,0:T(8,128)(2,1)} %w1.3) | copy-start | bytes 39940
  26.9 77.7 %copy-start.11 = (f32[512]{0:T(512)S(1)}, f32[512]{0:T(512)}, u32[]{:S(2)}) copy-start(f32[512]{0:T(512)} %param.21) | copy-start | bytes 6148
  26.9 77.7 %copy-start.13 = (f32[256]{0:T(256)S(1)}, f32[256]{0:T(256)}, u32[]{:S(2)}) copy-start(f32[256]{0:T(256)} %param.23) | copy-start | bytes 3076
  26.9 77.7 %copy-start.15 = (f32[128]{0:T(128)S(1)}, f32[128]{0:T(128)}, u32[]{:S(2)}) copy-start(f32[128]{0:T(128)} %param.25) | copy-start | bytes 1540
  26.9 48.2 %all-to-all-start = ((bf16[16,128,256]{2,1,0:T(8,128)(2,1)}), bf16[16,128,256]{2,1,0:T(8,128)(2,1)S(1)}, u32[]{:S(2)}, u32[]{:S(2)}) async-start(bf16[16,128,256]{2,1,0:T(8,128)(2,1)} %bitcast.2), calls=%async_computation | async-start | bytes 2097152 | tf_op jit(solution)/shard_map/all_to_all | solution.py:315
  39.5 0.9 copy-start.1
  75.1 16.1 %copy-start.16 = (bf16[16,128,256]{2,1,0:T(8,128)(2,1)}, bf16[16,128,256]{2,1,0:T(8,128)(2,1)S(1)}, u32[]{:S(2)}) copy-start(bf16[16,128,256]{2,1,0:T(8,128)(2,1)S(1)} %all-to-all-done.arrived_ref) | copy-start | bytes 3145732
  99.8 34.8 %all-to-all-start.1 = ((bf16[16,128,256]{2,1,0:T(8,128)(2,1)}), bf16[16,128,256]{2,1,0:T(8,128)(2,1)S(1)}, u32[]{:S(2)}, u32[]{:S(2)}) async-start(bf16[16,128,256]{2,1,0:T(8,128)(2,1)} %get-tuple-element.22), calls=%async_computation.1 | async-start | bytes 2097152 | tf_op jit(solution)/shard_map/all_to_all | solution.py:330
  107.0 3.3 %collective-permute-start = (bf16[4,192,128]{2,1,0:T(8,128)(2,1)S(1)}, bf16[4,192,128]{2,1,0:T(8,128)(2,1)S(1)}, u32[]{:S(2)}, u32[]{:S(2)}) collective-permute-start(bf16[4,192,128]{2,1,0:T(8,128)(2,1)S(1)} %dynamic-slice_bitcast_fusion), channel_id=1, source_target_pairs={{0,1},{1,0},{2,3},{3,2},{4,5},{5,4},{6,7},{7,6},{8,9},{9,8},{10,11... | collective-permute-start | bytes 589832 | tf_op jit(solution)/shard_map/ppermute | solution.py:344
  110.4 9.3 %collective-permute-start.3 = (bf16[192,128]{1,0:T(8,128)(2,1)S(1)}, bf16[192,128]{1,0:T(8,128)(2,1)S(1)}, u32[]{:S(2)}, u32[]{:S(2)}) collective-permute-start(bf16[192,128]{1,0:T(8,128)(2,1)S(1)} %get-tuple-element.35), channel_id=1, source_target_pairs={{0,384},{128,0},{256,128},{384,256},{1,385},{129,1},{257,129},{385... | collective-permute-start | bytes 147464 | tf_op jit(solution)/shard_map/ppermute | solution.py:351
  114.8 6.6 %collective-permute-start.2 = (bf16[192,128]{1,0:T(8,128)(2,1)S(1)}, bf16[192,128]{1,0:T(8,128)(2,1)S(1)}, u32[]{:S(2)}, u32[]{:S(2)}) collective-permute-start(bf16[192,128]{1,0:T(8,128)(2,1)S(1)} %get-tuple-element.36), channel_id=1, source_target_pairs={{0,256},{128,384},{256,0},{384,128},{1,257},{129,385},{257,1},{385... | collective-permute-start | bytes 147464 | tf_op jit(solution)/shard_map/ppermute | solution.py:351
  117.3 6.3 %collective-permute-start.1 = (bf16[192,128]{1,0:T(8,128)(2,1)S(1)}, bf16[192,128]{1,0:T(8,128)(2,1)S(1)}, u32[]{:S(2)}, u32[]{:S(2)}) collective-permute-start(bf16[192,128]{1,0:T(8,128)(2,1)S(1)} %get-tuple-element.34), channel_id=1, source_target_pairs={{0,128},{128,256},{256,384},{384,0},{1,129},{129,257},{257,385},{3... | collective-permute-start | bytes 147464 | tf_op jit(solution)/shard_map/ppermute | solution.py:351
  123.6 5.1 %collective-permute-start.4 = (bf16[192,128]{1,0:T(8,128)(2,1)S(1)}, bf16[192,128]{1,0:T(8,128)(2,1)S(1)}, u32[]{:S(2)}, u32[]{:S(2)}) collective-permute-start(bf16[192,128]{1,0:T(8,128)(2,1)S(1)} %fusion.3), channel_id=1, source_target_pairs={{0,16},{16,0},{32,48},{48,32},{64,80},{80,64},{96,112},{112,96},{1... | collective-permute-start | bytes 147464 | tf_op jit(solution)/shard_map/ppermute | solution.py:265
  128.8 5.8 %collective-permute-start.5 = (bf16[192,128]{1,0:T(8,128)(2,1)S(1)}, bf16[192,128]{1,0:T(8,128)(2,1)S(1)}, u32[]{:S(2)}, u32[]{:S(2)}) collective-permute-start(bf16[192,128]{1,0:T(8,128)(2,1)S(1)} %add_convert_fusion.2.one_ref), channel_id=1, source_target_pairs={{0,32},{16,48},{32,0},{48,16},{64,96},{80,112},{96,64},{112,80},{1... | collective-permute-start | bytes 147464 | tf_op jit(solution)/shard_map/ppermute | solution.py:265
  134.6 16.4 %collective-permute-start.6 = (bf16[192,128]{1,0:T(8,128)(2,1)S(1)}, bf16[192,128]{1,0:T(8,128)(2,1)S(1)}, u32[]{:S(2)}, u32[]{:S(2)}) collective-permute-start(bf16[192,128]{1,0:T(8,128)(2,1)S(1)} %add_after.1), channel_id=1, source_target_pairs={{0,64},{16,80},{32,96},{48,112},{64,0},{80,16},{96,32},{112,48},{1... | collective-permute-start | bytes 147464 | tf_op jit(solution)/shard_map/ppermute | solution.py:265
  151.0 11.5 %collective-permute-start.7 = (bf16[192,128]{1,0:T(8,128)(2,1)S(1)}, bf16[192,128]{1,0:T(8,128)(2,1)S(1)}, u32[]{:S(2)}, u32[]{:S(2)}) collective-permute-start(bf16[192,128]{1,0:T(8,128)(2,1)S(1)} %get-tuple-element.39), channel_id=1, source_target_pairs={{0,2},{2,0},{4,6},{6,4},{8,10},{10,8},{12,14},{14,12},{1,3},{3,1},... | collective-permute-start | bytes 147464 | tf_op jit(solution)/shard_map/ppermute | solution.py:265
  162.5 40.7 %all-to-all-start.2 = ((bf16[32,2,64,128]{3,2,1,0:T(8,128)(2,1)}), bf16[32,2,64,128]{3,2,1,0:T(8,128)(2,1)S(1)}, u32[]{:S(2)}, u32[]{:S(2)}) async-start(bf16[32,2,64,128]{3,2,1,0:T(8,128)(2,1)} %hold.1), calls=%async_computation.2 | async-start | bytes 2097152 | tf_op jit(solution)/shard_map/all_to_all | solution.py:363
  166.5 6.1 %collective-permute-start.8 = (bf16[192,128]{1,0:T(8,128)(2,1)S(1)}, bf16[192,128]{1,0:T(8,128)(2,1)S(1)}, u32[]{:S(2)}, u32[]{:S(2)}) collective-permute-start(bf16[192,128]{1,0:T(8,128)(2,1)S(1)} %get-tuple-element.37), channel_id=1, source_target_pairs={{0,4},{2,6},{4,0},{6,2},{8,12},{10,14},{12,8},{14,10},{1,5},{3,7},... | collective-permute-start | bytes 147464 | tf_op jit(solution)/shard_map/ppermute | solution.py:265
  172.6 9.0 %collective-permute-start.9 = (bf16[192,128]{1,0:T(8,128)(2,1)S(1)}, bf16[192,128]{1,0:T(8,128)(2,1)S(1)}, u32[]{:S(2)}, u32[]{:S(2)}) collective-permute-start(bf16[192,128]{1,0:T(8,128)(2,1)S(1)} %add_convert_fusion.1), channel_id=1, source_target_pairs={{0,8},{2,10},{4,12},{6,14},{8,0},{10,2},{12,4},{14,6},{1,9},{3,11}... | collective-permute-start | bytes 147464 | tf_op jit(solution)/shard_map/ppermute | solution.py:265
  181.6 9.0 %collective-permute-start.10 = (bf16[192,128]{1,0:T(8,128)(2,1)S(1)}, bf16[192,128]{1,0:T(8,128)(2,1)S(1)}, u32[]{:S(2)}, u32[]{:S(2)}) collective-permute-start(bf16[192,128]{1,0:T(8,128)(2,1)S(1)} %add_convert_fusion), channel_id=1, source_target_pairs={{0,1},{1,0},{2,3},{3,2},{4,5},{5,4},{6,7},{7,6},{8,9},{9,8},{10,11... | collective-permute-start | bytes 147464 | tf_op jit(solution)/shard_map/ppermute | solution.py:367
  (8 other events, 5.7 us)
Sparse Core Ops, SparseCore 0:
  10.7 80.4 all-gather.1

commit v3 on v2

--- a/solution.py
+++ b/solution.py
@@ -1,8 +1,7 @@
-import functools
+import math
 
 import jax
 import jax.numpy as jnp
-import numpy as np
 from jax import lax
 from jax.experimental import pallas as pl
 from jax.experimental.pallas import tpu as pltpu
@@ -14,9 +13,9 @@
 GROUP = 32
 BLOCK = 256
 LOW = 256
-TABLE = ("y", "c")
-DP = ("x", "z")
-EVERY = ("x", "z", "y", "c")
+TABLE = ("yh", "yl", "c")
+DP = ("x", "zh", "zl")
+EVERY = ("x", "zh", "zl", "yh", "yl", "c")
 CHUNK = 192
 
 NT = (((1,), (1,)), ((), ()))
@@ -85,41 +84,40 @@
 
 
 def table_grad_kernel(hits_ref, grad_ref, out_ref, turned):
-    @pl.when(pl.program_id(0) == 0)
+    @pl.when(pl.program_id(1) == 0)
     def _():
         turned[...] = grad_ref[...].T
 
-    total = dot(turned[...], hits_ref[0, 0]).T.astype(jnp.bfloat16)
-    out_ref[...] = total.reshape(out_ref.shape)
-
-
-def table_grads(hits, grads, shard, parts, extra=()):
+    blocks = hits_ref.shape[1]
+    step = out_ref.shape[0] // blocks
+    for block in range(blocks):
+        total = dot(turned[...], hits_ref[0, block]).T.astype(jnp.bfloat16)
+        out_ref[block * step : block * step + step] = total.reshape(step, *out_ref.shape[1:])
+
+
+def table_grads(hits, grads, parts):
     shards, blocks, batch, low = hits.shape
     each = blocks * low // parts
-    step = low // each
-    hbm = pl.BlockSpec(memory_space=pl.ANY)
-
-    def kernel(hits_ref, grad_ref, *rest):
-        table_grad_kernel(hits_ref, grad_ref, rest[-2], rest[-1])
-
+    wide = math.gcd(blocks, 4)
+    step = wide * low // each
     return pl.pallas_call(
-        kernel,
-        grid=(blocks,),
+        table_grad_kernel,
+        grid=(shards, blocks // wide),
         in_specs=[
-            pl.BlockSpec((1, 1, batch, low), lambda r: (shard, r, 0, 0)),
-            pl.BlockSpec((batch, WIDTH), lambda r: (0, shard)),
-        ]
-        + [hbm] * len(extra),
-        out_specs=pl.BlockSpec((step, 1, each, WIDTH), lambda r: (r, shard, 0, 0)),
+            pl.BlockSpec((1, wide, batch, low), lambda s, r: (s, r, 0, 0)),
+            pl.BlockSpec((batch, WIDTH), lambda s, r: (0, s)),
+        ],
+        out_specs=pl.BlockSpec((step, 1, each, WIDTH), lambda s, r: (r, s, 0, 0)),
         out_shape=jax.ShapeDtypeStruct((parts, shards, each, WIDTH), jnp.bfloat16),
         scratch_shapes=[pltpu.VMEM((WIDTH, batch), jnp.bfloat16)],
-        input_output_aliases={2: 0} if shard else {},
         compiler_params=params(46),
         cost_estimate=pl.CostEstimate(
-            flops=2 * batch * blocks * low * WIDTH, bytes_accessed=2 * batch * (blocks * low + 2 * WIDTH), transcendentals=0
+            flops=2 * shards * batch * blocks * low * WIDTH,
+            bytes_accessed=2 * shards * batch * (blocks * low + 2 * WIDTH),
+            transcendentals=0,
         ),
         name="table_grads",
-    )(hits, grads, *extra)
+    )(hits, grads)
 
 
 def silu(value):
@@ -328,7 +326,7 @@
     )(*bottom_args)
     send, bottom_grad, bias_part = cross(shard_table, arrived, bottom_out, weights, cross_bias[None], cotangent)
     returned = lax.all_to_all(send, TABLE, split_axis=0, concat_axis=0, tiled=True)
-    parts = lax.axis_size("x") * lax.axis_size("z")
+    parts = lax.axis_size(DP)
     packed = pl.pallas_call(
         bottom_back_kernel,
         in_specs=[vmem] * 9,
@@ -350,20 +348,18 @@
         piece = lax.dynamic_index_in_dim(narrow, (column + shift) % length, axis=0, keepdims=False)
         piece = lax.ppermute(piece, "x", [(place, (place + shift) % length) for place in range(length)])
         part = part + piece.astype(jnp.float32)
-    part = spread_sum(part, "z", (1,))
-    part = spread_sum(part, "z", (2,), returned)
-    part = spread_sum(part, "z", (4,))
-
-    returned = returned.reshape(-1, returned.shape[2])
-    table_parts = table_grads(hits, returned, 0, parts)
-    for shard in range(1, hits.shape[0]):
-        table_parts = table_grads(hits, returned, shard, parts, (table_parts, part))
-    part = spread_sum(part, "y", (1,))
+    part = spread_sum(part, "zl", (1,), returned)
+    group = ("zh", "yl")
+    part = jnp.broadcast_to(part.astype(jnp.bfloat16), (lax.axis_size(group), CHUNK, 128))
+    part = lax.all_to_all(part, group, split_axis=0, concat_axis=0, tiled=True)
+    part = jnp.sum(part.astype(jnp.float32), axis=0)
+
+    table_parts = table_grads(hits, returned.reshape(-1, returned.shape[2]), parts)
     table_parts = hold(table_parts, part)
     table_parts = lax.all_to_all(table_parts, DP, split_axis=0, concat_axis=0, tiled=True)
     table_grad = jnp.sum(table_parts.astype(jnp.float32), axis=0)
 
-    part = spread_sum(part, "y", (2, 4)).astype(jnp.bfloat16)
+    part = spread_sum(part, "yh", (1, 2)).astype(jnp.bfloat16)
     other = lax.ppermute(part, "c", [(0, 1), (1, 0)])
     pair = jnp.where(core == 0, jnp.stack([part, other]), jnp.stack([other, part]))
     whole = lax.all_gather(pair.reshape(2 * CHUNK, 128), "x", axis=0, tiled=True)
@@ -387,7 +383,7 @@
 
 
 def solution(mesh):
-    fine = Mesh(mesh.devices.reshape(4, 8, 8, 2), EVERY)
+    fine = Mesh(mesh.devices.reshape(4, 4, 2, 4, 2, 2), EVERY)
     placed = (
         P(EVERY, None),
         P(TABLE, None, DP),

time: 214 us -> 203 us (0.949)
  starting transfers between devices: 67.5 us -> 55.3 us
  waiting for transfers between devices: 60.6 us -> 70 us
  Pallas kernels: 42.5 us -> 34.5 us
    ppermute x6 -> x3, starting transfers between devices: 28.9 us -> 8.87 us  [spread_sum(): lax.ppermute(sent, axis, [(place, place ^ distance) for place in range(si...]
    pallas_call x2 -> x1, Pallas kernels: 16.4 us -> 8.49 us  [table_grads(): pl.pallas_call(table_grad_kernel, grid=(shards, blocks // wide), in_specs...]
    all_to_all x0 -> x1, starting transfers between devices: none -> 7.1 us  [local(): part = lax.all_to_all(part, group, split_axis=0, concat_axis=0, tiled=True)]
    all_to_all x1, waiting for transfers between devices: 0.01 us -> 3.7 us  [local(): lax.all_to_all(send, TABLE, split_axis=0, concat_axis=0, tiled=True)]
    all_to_all x1, starting transfers between devices: 3.94 us -> 7.5 us  [local(): lax.all_to_all(table_parts, DP, split_axis=0, concat_axis=0, tiled=True)]
    all_to_all x0 -> x1, waiting for transfers between devices: none -> 3.29 us  [local(): part = lax.all_to_all(part, group, split_axis=0, concat_axis=0, tiled=True)]
    ppermute x1, starting transfers between devices: 8.16 us -> 5.3 us  [local(): other = lax.ppermute(part, 'c', [(0, 1), (1, 0)])]
    ppermute x6 -> x3, waiting for transfers between devices: 8.61 us -> 11 us  [spread_sum(): lax.ppermute(sent, axis, [(place, place ^ distance) for place in range(si...]
  transfers between devices with their start and end apart: 15 -> 13, of which waited for: 10 -> 11; matrix products, arithmetic and copies ran while one was open for 2% -> 2% of each run, Pallas kernels for 16% -> 13%
where the time goes in v3:
time: 203 us; the launch traced here: 200 us
  waiting for transfers between devices  70 us (34%)
  starting transfers between devices  55.3 us (27%)
  Pallas kernels  34.5 us (17%)
  between operations  14.4 us (7%)
  local copies, waits for them, and re-layouts  11.3 us (6%)
  blocking collectives  10.3 us (5%)
  other arithmetic  4.38 us (2%)
    all_to_all x1, waiting for transfers between devices, local(): lax.all_to_all(pooled, TABLE, split_axis=0, concat_axis=0, tiled=True)  29.9 us
    all_gather x1, waiting for transfers between devices, local(): lax.all_gather(jnp.concatenate([cross_up, cross_down.T], axis=1), TABLE,...  16.1 us
    pallas_call x1, Pallas kernels, pool(): pl.pallas_call(pool_kernel, grid=(shards, batch // BLOCK), in_specs=[pl.B...  15.1 us
    ppermute x3, waiting for transfers between devices, spread_sum(): lax.ppermute(sent, axis, [(place, place ^ distance) for place in range(si...  11 us
    all_to_all x1, starting transfers between devices, local(): lax.all_to_all(pooled, TABLE, split_axis=0, concat_axis=0, tiled=True)  10.5 us
    all_gather x1, blocking collectives, local(): lax.all_gather(pair.reshape(2 * CHUNK, 128), 'x', axis=0, tiled=True)  10.3 us
    ppermute x3, starting transfers between devices, local(): lax.ppermute(piece, 'x', [(place, (place + shift) % length) for place in...  9.28 us
    ppermute x3, starting transfers between devices, spread_sum(): lax.ppermute(sent, axis, [(place, place ^ distance) for place in range(si...  8.87 us
  transfers between devices with their start and end apart: 13, of which 11 were waited for; matrix products, arithmetic and copies ran while one was open for 2% of the time, Pallas kernels for 13%

profile of v3, /device:TPU:1, one launch (start us, length us, event | category | flops | bytes accessed | tf_op | source)
XLA Modules:
  0.0 200.2 jit_solution(8879548387974261919)
XLA Ops:
  11.7 15.1 %pool.1 = (bf16[2,8,2048,256]{3,2,1,0:T(8,128)(2,1)}, bf16[2048,256]{1,0:T(8,128)(2,1)}) custom-call(s32[2,64,256]{2,1,0:T(8,128)S(1)} %copy.34.code_ref, bf16[2,2048,128]{2,1,0:T(8,128)(2,1)S(1)} %copy-done), custom_call_target="tpu_custom_call" | custom-call | tf_op jit(solution)/shard_map/pool/pallas_call | solution.py:66
  26.8 10.5 %all-to-all-start = ((bf16[16,128,256]{2,1,0:T(8,128)(2,1)}), bf16[16,128,256]{2,1,0:T(8,128)(2,1)S(1)}, u32[]{:S(2)}, u32[]{:S(2)}) async-start(bf16[16,128,256]{2,1,0:T(8,128)(2,1)} %bitcast.2), calls=%async_computation | async-start | bytes 2097152 | tf_op jit(solution)/shard_map/all_to_all | solution.py:313
  45.1 29.9 %all-to-all-done.arrived_ref = bf16[16,128,256]{2,1,0:T(8,128)(2,1)S(1)} async-done(((bf16[16,128,256]{2,1,0:T(8,128)(2,1)}), bf16[16,128,256]{2,1,0:T(8,128)(2,1)S(1)}, u32[]{:S(2)}, u32[]{:S(2)}) %all-to-all-start) | async-done | bytes 1048608 | tf_op jit(solution)/shard_map/all_to_all | solution.py:313
  75.0 16.1 %all-gather.2.cloned.1.call-done.weights_ref = bf16[512,6912]{1,0:T(8,128)(2,1)} async-done(((bf16[32,6912]{1,0:T(8,128)(2,1)}), bf16[512,6912]{1,0:T(8,128)(2,1)}) %all-gather.2.cloned.1.call-update) | async-done | bytes 7077904 | tf_op jit(solution)/shard_map/all_gather | solution.py:310
  91.2 8.6 %cross.1 = (bf16[16,128,256]{2,1,0:T(8,128)(2,1)}, bf16[128,128]{1,0:T(8,128)(2,1)}, f32[32,128]{1,0:T(8,128)}) custom-call(s32[32]{0:T(128)} %owner_ref.1, bf16[16,128,256]{2,1,0:T(8,128)(2,1)} %copy-done.16, bf16[128,128]{1,0:T(8,128)(2,1)} %copy-done.5, bf16[512,6912]{1,0:T(8,128)(2,1)} %all-gather.2.cloned.1.call-done.weights_ref, ...), custom_call_target="tpu_custom_call" | custom-call | tf_op jit(solution)/shard_map/cross/pallas_call | solution.py:236
  99.8 4.7 %all-to-all-start.1 = ((bf16[16,128,256]{2,1,0:T(8,128)(2,1)}), bf16[16,128,256]{2,1,0:T(8,128)(2,1)S(1)}, u32[]{:S(2)}, u32[]{:S(2)}) async-start(bf16[16,128,256]{2,1,0:T(8,128)(2,1)} %get-tuple-element.22), calls=%async_computation.1 | async-start | bytes 2097152 | tf_op jit(solution)/shard_map/all_to_all | solution.py:328
  107.0 2.0 %collective-permute-start = (bf16[4,192,128]{2,1,0:T(8,128)(2,1)S(1)}, bf16[4,192,128]{2,1,0:T(8,128)(2,1)S(1)}, u32[]{:S(2)}, u32[]{:S(2)}) collective-permute-start(bf16[4,192,128]{2,1,0:T(8,128)(2,1)S(1)} %dynamic-slice_bitcast_fusion), channel_id=1, source_target_pairs={{0,1},{1,0},{2,3},{3,2},{4,5},{5,4},{6,7},{7,6},{8,9},{9,8},{10,11... | collective-permute-start | bytes 589832 | tf_op jit(solution)/shard_map/ppermute | solution.py:342
  110.4 4.3 %collective-permute-start.3 = (bf16[192,128]{1,0:T(8,128)(2,1)S(1)}, bf16[192,128]{1,0:T(8,128)(2,1)S(1)}, u32[]{:S(2)}, u32[]{:S(2)}) collective-permute-start(bf16[192,128]{1,0:T(8,128)(2,1)S(1)} %get-tuple-element.35), channel_id=1, source_target_pairs={{0,384},{128,0},{256,128},{384,256},{1,385},{129,1},{257,129},{385... | collective-permute-start | bytes 147464 | tf_op jit(solution)/shard_map/ppermute | solution.py:349
  114.8 2.5 %collective-permute-start.2 = (bf16[192,128]{1,0:T(8,128)(2,1)S(1)}, bf16[192,128]{1,0:T(8,128)(2,1)S(1)}, u32[]{:S(2)}, u32[]{:S(2)}) collective-permute-start(bf16[192,128]{1,0:T(8,128)(2,1)S(1)} %get-tuple-element.36), channel_id=1, source_target_pairs={{0,256},{128,384},{256,0},{384,128},{1,257},{129,385},{257,1},{385... | collective-permute-start | bytes 147464 | tf_op jit(solution)/shard_map/ppermute | solution.py:349
  117.3 2.5 %collective-permute-start.1 = (bf16[192,128]{1,0:T(8,128)(2,1)S(1)}, bf16[192,128]{1,0:T(8,128)(2,1)S(1)}, u32[]{:S(2)}, u32[]{:S(2)}) collective-permute-start(bf16[192,128]{1,0:T(8,128)(2,1)S(1)} %get-tuple-element.34), channel_id=1, source_target_pairs={{0,128},{128,256},{256,384},{384,0},{1,129},{129,257},{257,385},{3... | collective-permute-start | bytes 147464 | tf_op jit(solution)/shard_map/ppermute | solution.py:349
  121.4 2.2 %collective-permute-done.1 = bf16[192,128]{1,0:T(8,128)(2,1)S(1)} collective-permute-done((bf16[192,128]{1,0:T(8,128)(2,1)S(1)}, bf16[192,128]{1,0:T(8,128)(2,1)S(1)}, u32[]{:S(2)}, u32[]{:S(2)}) %collective-permute-start.1) | collective-permute-done | bytes 49184 | tf_op jit(solution)/shard_map/ppermute | solution.py:349
  123.6 3.3 %collective-permute-start.4 = (bf16[192,128]{1,0:T(8,128)(2,1)S(1)}, bf16[192,128]{1,0:T(8,128)(2,1)S(1)}, u32[]{:S(2)}, u32[]{:S(2)}) collective-permute-start(bf16[192,128]{1,0:T(8,128)(2,1)S(1)} %fusion.3.one_ref), channel_id=1, source_target_pairs={{0,16},{16,0},{1,17},{17,1},{2,18},{18,2},{3,19},{19,3},{4,20},{20... | collective-permute-start | bytes 147464 | tf_op jit(solution)/shard_map/ppermute | solution.py:263
  126.9 1.8 collective-permute-done.4.other_ref
  128.8 3.7 %all-to-all-done.1.after_ref = bf16[16,128,256]{2,1,0:T(8,128)(2,1)S(1)} async-done(((bf16[16,128,256]{2,1,0:T(8,128)(2,1)}), bf16[16,128,256]{2,1,0:T(8,128)(2,1)S(1)}, u32[]{:S(2)}, u32[]{:S(2)}) %all-to-all-start.1) | async-done | bytes 1048608 | tf_op jit(solution)/shard_map/all_to_all | solution.py:328
  133.3 7.1 %all-to-all-start.2 = ((bf16[8,192,128]{2,1,0:T(8,128)(2,1)}), bf16[8,192,128]{2,1,0:T(8,128)(2,1)S(1)}, u32[]{:S(2)}, u32[]{:S(2)}) async-start(bf16[8,192,128]{2,1,0:T(8,128)(2,1)} %broadcast_in_dim.25), calls=%async_computation.2 | async-start | bytes 786432 | tf_op jit(solution)/shard_map/all_to_all | solution.py:354
  140.4 8.5 %table_grads.1.value_ref = bf16[32,2,64,128]{3,2,1,0:T(8,128)(2,1)} custom-call(bf16[2,8,2048,256]{3,2,1,0:T(8,128)(2,1)} %get-tuple-element.20.hits_ref, bf16[2048,256]{1,0:T(8,128)(2,1)S(1)} %bitcast.37), custom_call_target="tpu_custom_call" | custom-call | flops 2147483648 | bytes 18874368 | tf_op jit(solution)/shard_map/table_grads/pallas_call | solution.py:103
  148.9 3.3 %all-to-all-done.2 = bf16[8,192,128]{2,1,0:T(8,128)(2,1)S(1)} async-done(((bf16[8,192,128]{2,1,0:T(8,128)(2,1)}), bf16[8,192,128]{2,1,0:T(8,128)(2,1)S(1)}, u32[]{:S(2)}, u32[]{:S(2)}) %all-to-all-start.2) | async-done | bytes 393248 | tf_op jit(solution)/shard_map/all_to_all | solution.py:354
  152.2 7.5 %all-to-all-start.3 = ((bf16[32,2,64,128]{3,2,1,0:T(8,128)(2,1)}), bf16[32,2,64,128]{3,2,1,0:T(8,128)(2,1)S(1)}, u32[]{:S(2)}, u32[]{:S(2)}) async-start(bf16[32,2,64,128]{3,2,1,0:T(8,128)(2,1)} %hold.1), calls=%async_computation.3 | async-start | bytes 2097152 | tf_op jit(solution)/shard_map/all_to_all | solution.py:359
  159.7 3.1 %collective-permute-start.5 = (bf16[192,128]{1,0:T(8,128)(2,1)S(1)}, bf16[192,128]{1,0:T(8,128)(2,1)S(1)}, u32[]{:S(2)}, u32[]{:S(2)}) collective-permute-start(bf16[192,128]{1,0:T(8,128)(2,1)S(1)} %convert_element_type.61), channel_id=1, source_target_pairs={{0,4},{4,0},{8,12},{12,8},{1,5},{5,1},{9,13},{13,9},{2,6},{6,2},{1... | collective-permute-start | bytes 147464 | tf_op jit(solution)/shard_map/ppermute | solution.py:263
  162.9 2.9 %collective-permute-done.5 = bf16[192,128]{1,0:T(8,128)(2,1)S(1)} collective-permute-done((bf16[192,128]{1,0:T(8,128)(2,1)S(1)}, bf16[192,128]{1,0:T(8,128)(2,1)S(1)}, u32[]{:S(2)}, u32[]{:S(2)}) %collective-permute-start.5) | collective-permute-done | bytes 49184 | tf_op jit(solution)/shard_map/ppermute | solution.py:263
  165.7 2.5 %collective-permute-start.6 = (bf16[192,128]{1,0:T(8,128)(2,1)S(1)}, bf16[192,128]{1,0:T(8,128)(2,1)S(1)}, u32[]{:S(2)}, u32[]{:S(2)}) collective-permute-start(bf16[192,128]{1,0:T(8,128)(2,1)S(1)} %add_convert_fusion.1), channel_id=1, source_target_pairs={{0,8},{4,12},{8,0},{12,4},{1,9},{5,13},{9,1},{13,5},{2,10},{6,14},... | collective-permute-start | bytes 147464 | tf_op jit(solution)/shard_map/ppermute | solution.py:263
  168.2 6.3 %collective-permute-done.6 = bf16[192,128]{1,0:T(8,128)(2,1)S(1)} collective-permute-done((bf16[192,128]{1,0:T(8,128)(2,1)S(1)}, bf16[192,128]{1,0:T(8,128)(2,1)S(1)}, u32[]{:S(2)}, u32[]{:S(2)}) %collective-permute-start.6) | collective-permute-done | bytes 49184 | tf_op jit(solution)/shard_map/ppermute | solution.py:263
  174.5 5.3 %collective-permute-start.7 = (bf16[192,128]{1,0:T(8,128)(2,1)S(1)}, bf16[192,128]{1,0:T(8,128)(2,1)S(1)}, u32[]{:S(2)}, u32[]{:S(2)}) collective-permute-start(bf16[192,128]{1,0:T(8,128)(2,1)S(1)} %add_convert_fusion), channel_id=1, source_target_pairs={{0,1},{1,0},{2,3},{3,2},{4,5},{5,4},{6,7},{7,6},{8,9},{9,8},{10,11... | collective-permute-start | bytes 147464 | tf_op jit(solution)/shard_map/ppermute | solution.py:363
  180.7 10.3 %all_gather.7.whole = bf16[1536,128]{1,0:T(8,128)(2,1)S(1)} all-gather(bf16[384,128]{1,0:T(8,128)(2,1)S(1)} %bitcast.48), channel_id=1, replica_groups=mesh['x'=4,'zh'=4,'zl'=2,'yh'=4,'yl'=2,'c'=2] {'x'}, dimensions={0}, use_global_device_ids=true | all-gather | bytes 491520 | tf_op jit(solution)/shard_map/all_gather | solution.py:365
  (65 shorter events, 21.8 us)
Async XLA Ops:
  7.2 84.0 %all-gather.2.cloned.1.call-start = ((), (), s32[]{:S(2)}) async-start(), calls=%async_computation.4 | async-start | bytes 7520256 | tf_op jit(solution)/shard_map/all_gather | solution.py:310
  10.5 1.2 copy-start
  26.8 77.7 %copy-start.2 = (bf16[512,256]{1,0:T(8,128)(2,1)S(1)}, bf16[512,256]{1,0:T(8,128)(2,1)}, u32[]{:S(2)}) copy-start(bf16[512,256]{1,0:T(8,128)(2,1)} %w2.3) | copy-start | bytes 786436
  26.8 77.7 %copy-start.4 = (bf16[256,128]{1,0:T(8,128)(2,1)S(1)}, bf16[256,128]{1,0:T(8,128)(2,1)}, u32[]{:S(2)}) copy-start(bf16[256,128]{1,0:T(8,128)(2,1)} %w3.3) | copy-start | bytes 196612
  26.8 77.7 %copy-start.7 = (bf16[13,512]{1,0:T(8,128)(2,1)S(1)}, bf16[13,512]{1,0:T(8,128)(2,1)}, u32[]{:S(2)}) copy-start(bf16[13,512]{1,0:T(8,128)(2,1)} %w1.3) | copy-start | bytes 39940
  26.8 77.7 %copy-start.11 = (f32[512]{0:T(512)S(1)}, f32[512]{0:T(512)}, u32[]{:S(2)}) copy-start(f32[512]{0:T(512)} %param.21) | copy-start | bytes 6148
  26.8 77.7 %copy-start.13 = (f32[256]{0:T(256)S(1)}, f32[256]{0:T(256)}, u32[]{:S(2)}) copy-start(f32[256]{0:T(256)} %param.23) | copy-start | bytes 3076
  26.8 77.7 %copy-start.15 = (f32[128]{0:T(128)S(1)}, f32[128]{0:T(128)}, u32[]{:S(2)}) copy-start(f32[128]{0:T(128)} %param.25) | copy-start | bytes 1540
  26.8 48.2 %all-to-all-start = ((bf16[16,128,256]{2,1,0:T(8,128)(2,1)}), bf16[16,128,256]{2,1,0:T(8,128)(2,1)S(1)}, u32[]{:S(2)}, u32[]{:S(2)}) async-start(bf16[16,128,256]{2,1,0:T(8,128)(2,1)} %bitcast.2), calls=%async_computation | async-start | bytes 2097152 | tf_op jit(solution)/shard_map/all_to_all | solution.py:313
  39.4 0.9 copy-start.1
  40.4 0.8 copy-start.3
  75.0 16.1 %copy-start.16 = (bf16[16,128,256]{2,1,0:T(8,128)(2,1)}, bf16[16,128,256]{2,1,0:T(8,128)(2,1)S(1)}, u32[]{:S(2)}) copy-start(bf16[16,128,256]{2,1,0:T(8,128)(2,1)S(1)} %all-to-all-done.arrived_ref) | copy-start | bytes 3145732
  99.8 32.7 %all-to-all-start.1 = ((bf16[16,128,256]{2,1,0:T(8,128)(2,1)}), bf16[16,128,256]{2,1,0:T(8,128)(2,1)S(1)}, u32[]{:S(2)}, u32[]{:S(2)}) async-start(bf16[16,128,256]{2,1,0:T(8,128)(2,1)} %get-tuple-element.22), calls=%async_computation.1 | async-start | bytes 2097152 | tf_op jit(solution)/shard_map/all_to_all | solution.py:328
  104.6 0.8 copy-start.8
  107.0 3.3 %collective-permute-start = (bf16[4,192,128]{2,1,0:T(8,128)(2,1)S(1)}, bf16[4,192,128]{2,1,0:T(8,128)(2,1)S(1)}, u32[]{:S(2)}, u32[]{:S(2)}) collective-permute-start(bf16[4,192,128]{2,1,0:T(8,128)(2,1)S(1)} %dynamic-slice_bitcast_fusion), channel_id=1, source_target_pairs={{0,1},{1,0},{2,3},{3,2},{4,5},{5,4},{6,7},{7,6},{8,9},{9,8},{10,11... | collective-permute-start | bytes 589832 | tf_op jit(solution)/shard_map/ppermute | solution.py:342
  110.4 9.3 %collective-permute-start.3 = (bf16[192,128]{1,0:T(8,128)(2,1)S(1)}, bf16[192,128]{1,0:T(8,128)(2,1)S(1)}, u32[]{:S(2)}, u32[]{:S(2)}) collective-permute-start(bf16[192,128]{1,0:T(8,128)(2,1)S(1)} %get-tuple-element.35), channel_id=1, source_target_pairs={{0,384},{128,0},{256,128},{384,256},{1,385},{129,1},{257,129},{385... | collective-permute-start | bytes 147464 | tf_op jit(solution)/shard_map/ppermute | solution.py:349
  114.8 6.6 %collective-permute-start.2 = (bf16[192,128]{1,0:T(8,128)(2,1)S(1)}, bf16[192,128]{1,0:T(8,128)(2,1)S(1)}, u32[]{:S(2)}, u32[]{:S(2)}) collective-permute-start(bf16[192,128]{1,0:T(8,128)(2,1)S(1)} %get-tuple-element.36), channel_id=1, source_target_pairs={{0,256},{128,384},{256,0},{384,128},{1,257},{129,385},{257,1},{385... | collective-permute-start | bytes 147464 | tf_op jit(solution)/shard_map/ppermute | solution.py:349
  117.3 6.3 %collective-permute-start.1 = (bf16[192,128]{1,0:T(8,128)(2,1)S(1)}, bf16[192,128]{1,0:T(8,128)(2,1)S(1)}, u32[]{:S(2)}, u32[]{:S(2)}) collective-permute-start(bf16[192,128]{1,0:T(8,128)(2,1)S(1)} %get-tuple-element.34), channel_id=1, source_target_pairs={{0,128},{128,256},{256,384},{384,0},{1,129},{129,257},{257,385},{3... | collective-permute-start | bytes 147464 | tf_op jit(solution)/shard_map/ppermute | solution.py:349
  123.6 5.1 %collective-permute-start.4 = (bf16[192,128]{1,0:T(8,128)(2,1)S(1)}, bf16[192,128]{1,0:T(8,128)(2,1)S(1)}, u32[]{:S(2)}, u32[]{:S(2)}) collective-permute-start(bf16[192,128]{1,0:T(8,128)(2,1)S(1)} %fusion.3.one_ref), channel_id=1, source_target_pairs={{0,16},{16,0},{1,17},{17,1},{2,18},{18,2},{3,19},{19,3},{4,20},{20... | collective-permute-start | bytes 147464 | tf_op jit(solution)/shard_map/ppermute | solution.py:263
  133.3 18.9 %all-to-all-start.2 = ((bf16[8,192,128]{2,1,0:T(8,128)(2,1)}), bf16[8,192,128]{2,1,0:T(8,128)(2,1)S(1)}, u32[]{:S(2)}, u32[]{:S(2)}) async-start(bf16[8,192,128]{2,1,0:T(8,128)(2,1)} %broadcast_in_dim.25), calls=%async_computation.2 | async-start | bytes 786432 | tf_op jit(solution)/shard_map/all_to_all | solution.py:354
  152.2 40.3 %all-to-all-start.3 = ((bf16[32,2,64,128]{3,2,1,0:T(8,128)(2,1)}), bf16[32,2,64,128]{3,2,1,0:T(8,128)(2,1)S(1)}, u32[]{:S(2)}, u32[]{:S(2)}) async-start(bf16[32,2,64,128]{3,2,1,0:T(8,128)(2,1)} %hold.1), calls=%async_computation.3 | async-start | bytes 2097152 | tf_op jit(solution)/shard_map/all_to_all | solution.py:359
  159.7 6.0 %collective-permute-start.5 = (bf16[192,128]{1,0:T(8,128)(2,1)S(1)}, bf16[192,128]{1,0:T(8,128)(2,1)S(1)}, u32[]{:S(2)}, u32[]{:S(2)}) collective-permute-start(bf16[192,128]{1,0:T(8,128)(2,1)S(1)} %convert_element_type.61), channel_id=1, source_target_pairs={{0,4},{4,0},{8,12},{12,8},{1,5},{5,1},{9,13},{13,9},{2,6},{6,2},{1... | collective-permute-start | bytes 147464 | tf_op jit(solution)/shard_map/ppermute | solution.py:263
  165.7 8.8 %collective-permute-start.6 = (bf16[192,128]{1,0:T(8,128)(2,1)S(1)}, bf16[192,128]{1,0:T(8,128)(2,1)S(1)}, u32[]{:S(2)}, u32[]{:S(2)}) collective-permute-start(bf16[192,128]{1,0:T(8,128)(2,1)S(1)} %add_convert_fusion.1), channel_id=1, source_target_pairs={{0,8},{4,12},{8,0},{12,4},{1,9},{5,13},{9,1},{13,5},{2,10},{6,14},... | collective-permute-start | bytes 147464 | tf_op jit(solution)/shard_map/ppermute | solution.py:263
  174.5 6.2 %collective-permute-start.7 = (bf16[192,128]{1,0:T(8,128)(2,1)S(1)}, bf16[192,128]{1,0:T(8,128)(2,1)S(1)}, u32[]{:S(2)}, u32[]{:S(2)}) collective-permute-start(bf16[192,128]{1,0:T(8,128)(2,1)S(1)} %add_convert_fusion), channel_id=1, source_target_pairs={{0,1},{1,0},{2,3},{3,2},{4,5},{5,4},{6,7},{7,6},{8,9},{9,8},{10,11... | collective-permute-start | bytes 147464 | tf_op jit(solution)/shard_map/ppermute | solution.py:363
  (6 other events, 4.1 us)
Sparse Core Ops, SparseCore 0:
  10.7 80.4 all-gather.1

commit v4 on v3

--- a/solution.py
+++ b/solution.py
@@ -16,7 +16,7 @@
 TABLE = ("yh", "yl", "c")
 DP = ("x", "zh", "zl")
 EVERY = ("x", "zh", "zl", "yh", "yl", "c")
-CHUNK = 192
+CHUNK = 176
 
 NT = (((1,), (1,)), ((), ()))
 TN = (((0,), (0,)), ((), ()))
@@ -166,7 +166,7 @@
     rows += [third_sum, jnp.zeros((9, 128), jnp.float32)]
     out_ref[1344:1360, :] = jnp.concatenate(rows, axis=0).astype(jnp.bfloat16)
     out_ref[1360:1392, :] = bias_ref[...].astype(jnp.bfloat16)
-    out_ref[1392:1536, :] = jnp.zeros((144, 128), jnp.bfloat16)
+    out_ref[1392:1408, :] = jnp.zeros((16, 128), jnp.bfloat16)
 
 
 def unpack_kernel(whole, first_grad, second_grad, third_grad, first_sum, second_sum, third_sum, bias_sum):
@@ -187,20 +187,11 @@
         bias_sum[:, part * 128 : part * 128 + 128] = biases[part : part + 1]
 
 
-def cross_kernel(
-    owner_ref, arrived_ref, bottom_ref, weights_ref, bias_ref, cot_ref,
-    send_ref, bottom_grad_ref, bias_grad_ref, total, inputs, mixed, grads, up, down, arrived_at,
-):
+def mix_kernel(owner_ref, arrived_ref, bottom_ref, cot_ref, inputs, mixed, bias_grad_ref, total):
     blocks = total.shape[0]
-    wide = blocks * WIDTH
-    shards = owner_ref.shape[0]
-    fetch_down = pltpu.make_async_copy(weights_ref.at[:, wide : 2 * wide], down, arrived_at.at[0])
-    fetch_up = pltpu.make_async_copy(weights_ref.at[:, 0:wide], up, arrived_at.at[1])
-    fetch_down.start()
-    fetch_up.start()
     total[1:] = jnp.zeros_like(total[1:])
     total[0] = bottom_ref[...].astype(jnp.float32)
-    for shard in range(shards):
+    for shard in range(owner_ref.shape[0]):
         place = owner_ref[shard] + 1
         piece = arrived_ref[shard // 2, :, (shard % 2) * WIDTH : (shard % 2) * WIDTH + WIDTH]
         total[place] = total[place] + piece.astype(jnp.float32)
@@ -212,15 +203,36 @@
         mix_grad = cot_ref[:, columns].astype(jnp.float32) * piece.astype(jnp.float32)
         mixed[:, columns] = mix_grad.astype(jnp.bfloat16)
         bias_grad_ref[block : block + 1, :] = jnp.sum(mix_grad, axis=0, keepdims=True)
-    fetch_down.wait()
-    low_rank = dot(inputs[...], down[...], NT).astype(jnp.bfloat16)
-    fetch_up.wait()
-    rank_grad = dot(mixed[...], up[...], NT).astype(jnp.bfloat16)
+
+
+def cross_kernel(
+    owner_ref, inputs, mixed, weights_ref, bias_ref, cot_ref, send_ref, bottom_grad_ref, grads, up, down, low_rank,
+    rank_grad, landed,
+):
+    wide = inputs.shape[1]
+    shards = owner_ref.shape[0]
+    parts = landed.shape[0] // 2
+    ranks = up.shape[0] // parts
+    copies = []
+    for part in range(parts):
+        rows = pl.ds(part * ranks, ranks)
+        for place, (held, first) in enumerate(((down, wide), (up, 0))):
+            copy = pltpu.make_async_copy(
+                weights_ref.at[rows, first : first + wide], held.at[rows, :], landed.at[part * 2 + place]
+            )
+            copy.start()
+            copies.append(copy)
+    for part in range(parts):
+        rows = slice(part * ranks, part * ranks + ranks)
+        copies[2 * part].wait()
+        low_rank[:, rows] = dot(inputs[...], down[rows, :], NT).astype(jnp.bfloat16)
+        copies[2 * part + 1].wait()
+        rank_grad[:, rows] = dot(mixed[...], up[rows, :], NT).astype(jnp.bfloat16)
     step = 3 * WIDTH
     for part in range(wide // step):
         columns = slice(part * step, part * step + step)
-        mixing = dot(low_rank, up[:, columns]) + bias_ref[:, columns]
-        back = dot(rank_grad, down[:, columns])
+        mixing = dot(low_rank[...], up[:, columns]) + bias_ref[:, columns]
+        back = dot(rank_grad[...], down[:, columns])
         grad = (cot_ref[:, columns].astype(jnp.float32) * (mixing + 1.0) + back).astype(jnp.bfloat16)
         for inner in range(3):
             grads[part * 3 + inner] = grad[:, inner * WIDTH : inner * WIDTH + WIDTH]
@@ -232,28 +244,42 @@
 def cross(shard_table, arrived, bottom_out, weights, cross_bias, cotangent):
     examples, wide = cotangent.shape
     blocks = wide // WIDTH
+    ranks = weights.shape[0]
     vmem = pl.BlockSpec(memory_space=pltpu.VMEM)
-    return pl.pallas_call(
+    smem = pl.BlockSpec(memory_space=pltpu.SMEM)
+    inputs, mixed, bias_part = pl.pallas_call(
+        mix_kernel,
+        in_specs=[smem] + [vmem] * 3,
+        out_specs=[vmem] * 3,
+        out_shape=[
+            jax.ShapeDtypeStruct((examples, wide), jnp.bfloat16),
+            jax.ShapeDtypeStruct((examples, wide), jnp.bfloat16),
+            jax.ShapeDtypeStruct((32, WIDTH), jnp.float32),
+        ],
+        scratch_shapes=[pltpu.VMEM((blocks, examples, WIDTH), jnp.float32)],
+        compiler_params=params(16),
+        name="mix",
+    )(shard_table, arrived, bottom_out, cotangent)
+    send, bottom_grad = pl.pallas_call(
         cross_kernel,
-        in_specs=[pl.BlockSpec(memory_space=pltpu.SMEM), vmem, vmem, pl.BlockSpec(memory_space=pltpu.HBM), vmem, vmem],
-        out_specs=[vmem] * 3,
+        in_specs=[smem, vmem, vmem, pl.BlockSpec(memory_space=pltpu.HBM), vmem, vmem],
+        out_specs=[vmem] * 2,
         out_shape=[
             jax.ShapeDtypeStruct(arrived.shape, jnp.bfloat16),
             jax.ShapeDtypeStruct((examples, WIDTH), jnp.bfloat16),
-            jax.ShapeDtypeStruct((32, WIDTH), jnp.float32),
         ],
         scratch_shapes=[
-            pltpu.VMEM((blocks, examples, WIDTH), jnp.float32),
-            pltpu.VMEM((examples, wide), jnp.bfloat16),
-            pltpu.VMEM((examples, wide), jnp.bfloat16),
             pltpu.VMEM((blocks, examples, WIDTH), jnp.bfloat16),
-            pltpu.VMEM((weights.shape[0], wide), jnp.bfloat16),
-            pltpu.VMEM((weights.shape[0], wide), jnp.bfloat16),
-            pltpu.SemaphoreType.DMA((2,)),
-        ],
-        compiler_params=params(55),
+            pltpu.VMEM((ranks, wide), jnp.bfloat16),
+            pltpu.VMEM((ranks, wide), jnp.bfloat16),
+            pltpu.VMEM((examples, ranks), jnp.bfloat16),
+            pltpu.VMEM((examples, ranks), jnp.bfloat16),
+            pltpu.SemaphoreType.DMA((4,)),
+        ],
+        compiler_params=params(50),
         name="cross",
-    )(shard_table, arrived, bottom_out, weights, cross_bias, cotangent)
+    )(shard_table, inputs, mixed, weights, cross_bias, cotangent)
+    return send, bottom_grad, bias_part
 
 
 def spread_sum(value, axis, distances, after=None):

time: 203 us -> 203 us (level)
    all_gather x1, waiting for transfers between devices: 16.1 us -> 14.1 us  [local(): lax.all_gather(jnp.concatenate([cross_up, cross_down.T], axis=1), TABLE,...]
    pallas_call x1 -> x2, Pallas kernels: 8.62 us -> 10.2 us  [the longest x1 8.88 us: cross(): pl.pallas_call(cross_kernel, in_specs=[smem, vmem, vmem, pl.BlockSpec(mem...]
where the time goes in v4:
time: 203 us; the launch traced here: 201 us
  waiting for transfers between devices  70.6 us (35%)
  starting transfers between devices  54.3 us (27%)
  Pallas kernels  36 us (18%)
  between operations  14.4 us (7%)
  local copies, waits for them, and re-layouts  10.8 us (5%)
  blocking collectives  10.6 us (5%)
  other arithmetic  4.44 us (2%)
    all_to_all x1, waiting for transfers between devices, local(): lax.all_to_all(pooled, TABLE, split_axis=0, concat_axis=0, tiled=True)  31.1 us
    pallas_call x1, Pallas kernels, pool(): pl.pallas_call(pool_kernel, grid=(shards, batch // BLOCK), in_specs=[pl.B...  15 us
    all_gather x1, waiting for transfers between devices, local(): lax.all_gather(jnp.concatenate([cross_up, cross_down.T], axis=1), TABLE,...  14.1 us
    ppermute x3, waiting for transfers between devices, spread_sum(): lax.ppermute(sent, axis, [(place, place ^ distance) for place in range(si...  10.6 us
    all_gather x1, blocking collectives, local(): lax.all_gather(pair.reshape(2 * CHUNK, 128), 'x', axis=0, tiled=True)  10.6 us
    all_to_all x1, starting transfers between devices, local(): lax.all_to_all(pooled, TABLE, split_axis=0, concat_axis=0, tiled=True)  10.3 us
    ppermute x3, starting transfers between devices, local(): lax.ppermute(piece, 'x', [(place, (place + shift) % length) for place in...  9.28 us
    ppermute x3, starting transfers between devices, spread_sum(): lax.ppermute(sent, axis, [(place, place ^ distance) for place in range(si...  9.19 us
  transfers between devices with their start and end apart: 13, of which 11 were waited for; matrix products, arithmetic and copies ran while one was open for 2% of the time, Pallas kernels for 13%

profile of v4, /device:TPU:1, one launch (start us, length us, event | category | flops | bytes accessed | tf_op | source)
XLA Modules:
  0.0 201.0 jit_solution(11808306166173327989)
XLA Ops:
  7.2 1.9 pad_maximum_fusion
  11.8 15.0 %pool.1 = (bf16[2,8,2048,256]{3,2,1,0:T(8,128)(2,1)}, bf16[2048,256]{1,0:T(8,128)(2,1)}) custom-call(s32[2,64,256]{2,1,0:T(8,128)S(1)} %copy.34.code_ref, bf16[2,2048,128]{2,1,0:T(8,128)(2,1)S(1)} %copy-done.1), custom_call_target="tpu_custom_call" | custom-call | tf_op jit(solution)/shard_map/pool/pallas_call | solution.py:66
  26.8 10.3 %all-to-all-start = ((bf16[16,128,256]{2,1,0:T(8,128)(2,1)}), bf16[16,128,256]{2,1,0:T(8,128)(2,1)S(1)}, u32[]{:S(2)}, u32[]{:S(2)}) async-start(bf16[16,128,256]{2,1,0:T(8,128)(2,1)} %bitcast.2), calls=%async_computation | async-start | bytes 2097152 | tf_op jit(solution)/shard_map/all_to_all | solution.py:339
  43.8 31.1 %all-to-all-done.arrived_ref = bf16[16,128,256]{2,1,0:T(8,128)(2,1)S(1)} async-done(((bf16[16,128,256]{2,1,0:T(8,128)(2,1)}), bf16[16,128,256]{2,1,0:T(8,128)(2,1)S(1)}, u32[]{:S(2)}, u32[]{:S(2)}) %all-to-all-start) | async-done | bytes 1048608 | tf_op jit(solution)/shard_map/all_to_all | solution.py:339
  77.1 14.1 %all-gather.2.cloned.1.call-done.weights_ref = bf16[512,6912]{1,0:T(8,128)(2,1)} async-done(((bf16[32,6912]{1,0:T(8,128)(2,1)}), bf16[512,6912]{1,0:T(8,128)(2,1)}) %all-gather.2.cloned.1.call-update) | async-done | bytes 7077904 | tf_op jit(solution)/shard_map/all_gather | solution.py:336
  92.4 8.9 %cross.1 = (bf16[16,128,256]{2,1,0:T(8,128)(2,1)}, bf16[128,128]{1,0:T(8,128)(2,1)S(1)}) custom-call(s32[32]{0:T(128)S(1)} %copy-done.14, bf16[128,3456]{1,0:T(8,128)(2,1)S(1)} %get-tuple-element.24.inputs, bf16[128,3456]{1,0:T(8,128)(2,1)S(1)} %copy-done.5, bf16[512,6912]{1,0:T(8,128)(2,1)} %all-gather.2.cloned.1.call-done.weights_ref, ...), custom_call_target="tpu_custom_call" | custom-call | tf_op jit(solution)/shard_map/cross/pallas_call | solution.py:263
  101.2 4.8 %all-to-all-start.1 = ((bf16[16,128,256]{2,1,0:T(8,128)(2,1)}), bf16[16,128,256]{2,1,0:T(8,128)(2,1)S(1)}, u32[]{:S(2)}, u32[]{:S(2)}) async-start(bf16[16,128,256]{2,1,0:T(8,128)(2,1)} %get-tuple-element.26), calls=%async_computation.1 | async-start | bytes 2097152 | tf_op jit(solution)/shard_map/all_to_all | solution.py:354
  107.0 2.0 %collective-permute-start = (bf16[4,176,128]{2,1,0:T(8,128)(2,1)S(1)}, bf16[4,176,128]{2,1,0:T(8,128)(2,1)S(1)}, u32[]{:S(2)}, u32[]{:S(2)}) collective-permute-start(bf16[4,176,128]{2,1,0:T(8,128)(2,1)S(1)} %dynamic-slice_bitcast_fusion), channel_id=1, source_target_pairs={{0,1},{1,0},{2,3},{3,2},{4,5},{5,4},{6,7},{7,6},{8,9},{9,8},{10,11... | collective-permute-start | bytes 540680 | tf_op jit(solution)/shard_map/ppermute | solution.py:368
  110.4 4.3 %collective-permute-start.3 = (bf16[176,128]{1,0:T(8,128)(2,1)S(1)}, bf16[176,128]{1,0:T(8,128)(2,1)S(1)}, u32[]{:S(2)}, u32[]{:S(2)}) collective-permute-start(bf16[176,128]{1,0:T(8,128)(2,1)S(1)} %get-tuple-element.39), channel_id=1, source_target_pairs={{0,384},{128,0},{256,128},{384,256},{1,385},{129,1},{257,129},{385... | collective-permute-start | bytes 135176 | tf_op jit(solution)/shard_map/ppermute | solution.py:375
  114.7 2.5 %collective-permute-start.2 = (bf16[176,128]{1,0:T(8,128)(2,1)S(1)}, bf16[176,128]{1,0:T(8,128)(2,1)S(1)}, u32[]{:S(2)}, u32[]{:S(2)}) collective-permute-start(bf16[176,128]{1,0:T(8,128)(2,1)S(1)} %get-tuple-element.40), channel_id=1, source_target_pairs={{0,256},{128,384},{256,0},{384,128},{1,257},{129,385},{257,1},{385... | collective-permute-start | bytes 135176 | tf_op jit(solution)/shard_map/ppermute | solution.py:375
  117.2 2.5 %collective-permute-start.1 = (bf16[176,128]{1,0:T(8,128)(2,1)S(1)}, bf16[176,128]{1,0:T(8,128)(2,1)S(1)}, u32[]{:S(2)}, u32[]{:S(2)}) collective-permute-start(bf16[176,128]{1,0:T(8,128)(2,1)S(1)} %get-tuple-element.38), channel_id=1, source_target_pairs={{0,128},{128,256},{256,384},{384,0},{1,129},{129,257},{257,385},{3... | collective-permute-start | bytes 135176 | tf_op jit(solution)/shard_map/ppermute | solution.py:375
  121.3 2.2 %collective-permute-done.1 = bf16[176,128]{1,0:T(8,128)(2,1)S(1)} collective-permute-done((bf16[176,128]{1,0:T(8,128)(2,1)S(1)}, bf16[176,128]{1,0:T(8,128)(2,1)S(1)}, u32[]{:S(2)}, u32[]{:S(2)}) %collective-permute-start.1) | collective-permute-done | bytes 45088 | tf_op jit(solution)/shard_map/ppermute | solution.py:375
  123.5 3.3 %collective-permute-start.4 = (bf16[176,128]{1,0:T(8,128)(2,1)S(1)}, bf16[176,128]{1,0:T(8,128)(2,1)S(1)}, u32[]{:S(2)}, u32[]{:S(2)}) collective-permute-start(bf16[176,128]{1,0:T(8,128)(2,1)S(1)} %fusion.3.one_ref), channel_id=1, source_target_pairs={{0,16},{16,0},{1,17},{17,1},{2,18},{18,2},{3,19},{19,3},{4,20},{20... | collective-permute-start | bytes 135176 | tf_op jit(solution)/shard_map/ppermute | solution.py:289
  128.6 5.3 %all-to-all-done.1.after_ref = bf16[16,128,256]{2,1,0:T(8,128)(2,1)S(1)} async-done(((bf16[16,128,256]{2,1,0:T(8,128)(2,1)}), bf16[16,128,256]{2,1,0:T(8,128)(2,1)S(1)}, u32[]{:S(2)}, u32[]{:S(2)}) %all-to-all-start.1) | async-done | bytes 1048608 | tf_op jit(solution)/shard_map/all_to_all | solution.py:354
  134.7 7.1 %all-to-all-start.2 = ((bf16[8,176,128]{2,1,0:T(8,128)(2,1)}), bf16[8,176,128]{2,1,0:T(8,128)(2,1)S(1)}, u32[]{:S(2)}, u32[]{:S(2)}) async-start(bf16[8,176,128]{2,1,0:T(8,128)(2,1)} %broadcast_in_dim.25), calls=%async_computation.2 | async-start | bytes 720896 | tf_op jit(solution)/shard_map/all_to_all | solution.py:380
  141.8 8.5 %table_grads.1.value_ref = bf16[32,2,64,128]{3,2,1,0:T(8,128)(2,1)} custom-call(bf16[2,8,2048,256]{3,2,1,0:T(8,128)(2,1)} %get-tuple-element.22.hits_ref, bf16[2048,256]{1,0:T(8,128)(2,1)S(1)} %bitcast.37), custom_call_target="tpu_custom_call" | custom-call | flops 2147483648 | bytes 18874368 | tf_op jit(solution)/shard_map/table_grads/pallas_call | solution.py:103
  150.3 3.7 %all-to-all-done.2 = bf16[8,176,128]{2,1,0:T(8,128)(2,1)S(1)} async-done(((bf16[8,176,128]{2,1,0:T(8,128)(2,1)}), bf16[8,176,128]{2,1,0:T(8,128)(2,1)S(1)}, u32[]{:S(2)}, u32[]{:S(2)}) %all-to-all-start.2) | async-done | bytes 360480 | tf_op jit(solution)/shard_map/all_to_all | solution.py:380
  154.0 6.6 %all-to-all-start.3 = ((bf16[32,2,64,128]{3,2,1,0:T(8,128)(2,1)}), bf16[32,2,64,128]{3,2,1,0:T(8,128)(2,1)S(1)}, u32[]{:S(2)}, u32[]{:S(2)}) async-start(bf16[32,2,64,128]{3,2,1,0:T(8,128)(2,1)} %hold.1), calls=%async_computation.3 | async-start | bytes 2097152 | tf_op jit(solution)/shard_map/all_to_all | solution.py:385
  160.6 3.0 %collective-permute-start.5 = (bf16[176,128]{1,0:T(8,128)(2,1)S(1)}, bf16[176,128]{1,0:T(8,128)(2,1)S(1)}, u32[]{:S(2)}, u32[]{:S(2)}) collective-permute-start(bf16[176,128]{1,0:T(8,128)(2,1)S(1)} %convert_element_type.61), channel_id=1, source_target_pairs={{0,4},{4,0},{8,12},{12,8},{1,5},{5,1},{9,13},{13,9},{2,6},{6,2},{1... | collective-permute-start | bytes 135176 | tf_op jit(solution)/shard_map/ppermute | solution.py:289
  163.6 2.9 %collective-permute-done.5 = bf16[176,128]{1,0:T(8,128)(2,1)S(1)} collective-permute-done((bf16[176,128]{1,0:T(8,128)(2,1)S(1)}, bf16[176,128]{1,0:T(8,128)(2,1)S(1)}, u32[]{:S(2)}, u32[]{:S(2)}) %collective-permute-start.5) | collective-permute-done | bytes 45088 | tf_op jit(solution)/shard_map/ppermute | solution.py:289
  166.5 2.9 %collective-permute-start.6 = (bf16[176,128]{1,0:T(8,128)(2,1)S(1)}, bf16[176,128]{1,0:T(8,128)(2,1)S(1)}, u32[]{:S(2)}, u32[]{:S(2)}) collective-permute-start(bf16[176,128]{1,0:T(8,128)(2,1)S(1)} %add_convert_fusion.1), channel_id=1, source_target_pairs={{0,8},{4,12},{8,0},{12,4},{1,9},{5,13},{9,1},{13,5},{2,10},{6,14},... | collective-permute-start | bytes 135176 | tf_op jit(solution)/shard_map/ppermute | solution.py:289
  169.5 5.9 %collective-permute-done.6 = bf16[176,128]{1,0:T(8,128)(2,1)S(1)} collective-permute-done((bf16[176,128]{1,0:T(8,128)(2,1)S(1)}, bf16[176,128]{1,0:T(8,128)(2,1)S(1)}, u32[]{:S(2)}, u32[]{:S(2)}) %collective-permute-start.6) | collective-permute-done | bytes 45088 | tf_op jit(solution)/shard_map/ppermute | solution.py:289
  175.4 5.0 %collective-permute-start.7 = (bf16[176,128]{1,0:T(8,128)(2,1)S(1)}, bf16[176,128]{1,0:T(8,128)(2,1)S(1)}, u32[]{:S(2)}, u32[]{:S(2)}) collective-permute-start(bf16[176,128]{1,0:T(8,128)(2,1)S(1)} %add_convert_fusion), channel_id=1, source_target_pairs={{0,1},{1,0},{2,3},{3,2},{4,5},{5,4},{6,7},{7,6},{8,9},{9,8},{10,11... | collective-permute-start | bytes 135176 | tf_op jit(solution)/shard_map/ppermute | solution.py:389
  181.3 10.6 %all_gather.7.whole = bf16[1408,128]{1,0:T(8,128)(2,1)S(1)} all-gather(bf16[352,128]{1,0:T(8,128)(2,1)S(1)} %bitcast.48), channel_id=1, replica_groups=mesh['x'=4,'zh'=4,'zl'=2,'yh'=4,'yl'=2,'c'=2] {'x'}, dimensions={0}, use_global_device_ids=true | all-gather | bytes 450560 | tf_op jit(solution)/shard_map/all_gather | solution.py:391
  (66 shorter events, 22.5 us)
Async XLA Ops:
  7.2 67.7 %copy-start.14 = (s32[32]{0:T(128)S(1)}, s32[32]{0:T(128)}, u32[]{:S(2)}) copy-start(s32[32]{0:T(128)} %owner_ref.3) | copy-start | bytes 388
  7.2 67.7 %copy-start = (bf16[128,3456]{1,0:T(8,128)(2,1)S(1)}, bf16[128,3456]{1,0:T(8,128)(2,1)}, u32[]{:S(2)}) copy-start(bf16[128,3456]{1,0:T(8,128)(2,1)} %cot_ref.3) | copy-start | bytes 2654212
  7.2 84.0 %all-gather.2.cloned.1.call-start = ((), (), s32[]{:S(2)}) async-start(), calls=%async_computation.4 | async-start | bytes 7520256 | tf_op jit(solution)/shard_map/all_gather | solution.py:336
  10.6 1.2 copy-start.1
  26.8 48.0 %all-to-all-start = ((bf16[16,128,256]{2,1,0:T(8,128)(2,1)}), bf16[16,128,256]{2,1,0:T(8,128)(2,1)S(1)}, u32[]{:S(2)}, u32[]{:S(2)}) async-start(bf16[16,128,256]{2,1,0:T(8,128)(2,1)} %bitcast.2), calls=%async_computation | async-start | bytes 2097152 | tf_op jit(solution)/shard_map/all_to_all | solution.py:339
  38.6 1.0 copy-start.2
  43.2 62.8 %copy-start.3 = (bf16[512,256]{1,0:T(8,128)(2,1)S(1)}, bf16[512,256]{1,0:T(8,128)(2,1)}, u32[]{:S(2)}) copy-start(bf16[512,256]{1,0:T(8,128)(2,1)} %w2.3) | copy-start | bytes 786436
  43.2 62.8 %copy-start.7 = (bf16[256,128]{1,0:T(8,128)(2,1)S(1)}, bf16[256,128]{1,0:T(8,128)(2,1)}, u32[]{:S(2)}) copy-start(bf16[256,128]{1,0:T(8,128)(2,1)} %w3.3) | copy-start | bytes 196612
  43.2 62.8 %copy-start.9 = (bf16[13,512]{1,0:T(8,128)(2,1)S(1)}, bf16[13,512]{1,0:T(8,128)(2,1)}, u32[]{:S(2)}) copy-start(bf16[13,512]{1,0:T(8,128)(2,1)} %w1.3) | copy-start | bytes 39940
  43.2 62.8 %copy-start.11 = (f32[512]{0:T(512)S(1)}, f32[512]{0:T(512)}, u32[]{:S(2)}) copy-start(f32[512]{0:T(512)} %param.21) | copy-start | bytes 6148
  43.2 62.8 %copy-start.13 = (f32[256]{0:T(256)S(1)}, f32[256]{0:T(256)}, u32[]{:S(2)}) copy-start(f32[256]{0:T(256)} %param.23) | copy-start | bytes 3076
  43.2 62.8 %copy-start.16 = (f32[128]{0:T(128)S(1)}, f32[128]{0:T(128)}, u32[]{:S(2)}) copy-start(f32[128]{0:T(128)} %param.25) | copy-start | bytes 1540
  91.2 1.2 copy-start.5
  101.2 32.7 %all-to-all-start.1 = ((bf16[16,128,256]{2,1,0:T(8,128)(2,1)}), bf16[16,128,256]{2,1,0:T(8,128)(2,1)S(1)}, u32[]{:S(2)}, u32[]{:S(2)}) async-start(bf16[16,128,256]{2,1,0:T(8,128)(2,1)} %get-tuple-element.26), calls=%async_computation.1 | async-start | bytes 2097152 | tf_op jit(solution)/shard_map/all_to_all | solution.py:354
  107.0 3.3 %collective-permute-start = (bf16[4,176,128]{2,1,0:T(8,128)(2,1)S(1)}, bf16[4,176,128]{2,1,0:T(8,128)(2,1)S(1)}, u32[]{:S(2)}, u32[]{:S(2)}) collective-permute-start(bf16[4,176,128]{2,1,0:T(8,128)(2,1)S(1)} %dynamic-slice_bitcast_fusion), channel_id=1, source_target_pairs={{0,1},{1,0},{2,3},{3,2},{4,5},{5,4},{6,7},{7,6},{8,9},{9,8},{10,11... | collective-permute-start | bytes 540680 | tf_op jit(solution)/shard_map/ppermute | solution.py:368
  110.4 9.3 %collective-permute-start.3 = (bf16[176,128]{1,0:T(8,128)(2,1)S(1)}, bf16[176,128]{1,0:T(8,128)(2,1)S(1)}, u32[]{:S(2)}, u32[]{:S(2)}) collective-permute-start(bf16[176,128]{1,0:T(8,128)(2,1)S(1)} %get-tuple-element.39), channel_id=1, source_target_pairs={{0,384},{128,0},{256,128},{384,256},{1,385},{129,1},{257,129},{385... | collective-permute-start | bytes 135176 | tf_op jit(solution)/shard_map/ppermute | solution.py:375
  114.7 6.6 %collective-permute-start.2 = (bf16[176,128]{1,0:T(8,128)(2,1)S(1)}, bf16[176,128]{1,0:T(8,128)(2,1)S(1)}, u32[]{:S(2)}, u32[]{:S(2)}) collective-permute-start(bf16[176,128]{1,0:T(8,128)(2,1)S(1)} %get-tuple-element.40), channel_id=1, source_target_pairs={{0,256},{128,384},{256,0},{384,128},{1,257},{129,385},{257,1},{385... | collective-permute-start | bytes 135176 | tf_op jit(solution)/shard_map/ppermute | solution.py:375
  117.2 6.3 %collective-permute-start.1 = (bf16[176,128]{1,0:T(8,128)(2,1)S(1)}, bf16[176,128]{1,0:T(8,128)(2,1)S(1)}, u32[]{:S(2)}, u32[]{:S(2)}) collective-permute-start(bf16[176,128]{1,0:T(8,128)(2,1)S(1)} %get-tuple-element.38), channel_id=1, source_target_pairs={{0,128},{128,256},{256,384},{384,0},{1,129},{129,257},{257,385},{3... | collective-permute-start | bytes 135176 | tf_op jit(solution)/shard_map/ppermute | solution.py:375
  123.5 5.1 %collective-permute-start.4 = (bf16[176,128]{1,0:T(8,128)(2,1)S(1)}, bf16[176,128]{1,0:T(8,128)(2,1)S(1)}, u32[]{:S(2)}, u32[]{:S(2)}) collective-permute-start(bf16[176,128]{1,0:T(8,128)(2,1)S(1)} %fusion.3.one_ref), channel_id=1, source_target_pairs={{0,16},{16,0},{1,17},{17,1},{2,18},{18,2},{3,19},{19,3},{4,20},{20... | collective-permute-start | bytes 135176 | tf_op jit(solution)/shard_map/ppermute | solution.py:289
  134.7 19.2 %all-to-all-start.2 = ((bf16[8,176,128]{2,1,0:T(8,128)(2,1)}), bf16[8,176,128]{2,1,0:T(8,128)(2,1)S(1)}, u32[]{:S(2)}, u32[]{:S(2)}) async-start(bf16[8,176,128]{2,1,0:T(8,128)(2,1)} %broadcast_in_dim.25), calls=%async_computation.2 | async-start | bytes 720896 | tf_op jit(solution)/shard_map/all_to_all | solution.py:380
  154.0 39.3 %all-to-all-start.3 = ((bf16[32,2,64,128]{3,2,1,0:T(8,128)(2,1)}), bf16[32,2,64,128]{3,2,1,0:T(8,128)(2,1)S(1)}, u32[]{:S(2)}, u32[]{:S(2)}) async-start(bf16[32,2,64,128]{3,2,1,0:T(8,128)(2,1)} %hold.1), calls=%async_computation.3 | async-start | bytes 2097152 | tf_op jit(solution)/shard_map/all_to_all | solution.py:385
  160.6 5.9 %collective-permute-start.5 = (bf16[176,128]{1,0:T(8,128)(2,1)S(1)}, bf16[176,128]{1,0:T(8,128)(2,1)S(1)}, u32[]{:S(2)}, u32[]{:S(2)}) collective-permute-start(bf16[176,128]{1,0:T(8,128)(2,1)S(1)} %convert_element_type.61), channel_id=1, source_target_pairs={{0,4},{4,0},{8,12},{12,8},{1,5},{5,1},{9,13},{13,9},{2,6},{6,2},{1... | collective-permute-start | bytes 135176 | tf_op jit(solution)/shard_map/ppermute | solution.py:289
  166.5 8.8 %collective-permute-start.6 = (bf16[176,128]{1,0:T(8,128)(2,1)S(1)}, bf16[176,128]{1,0:T(8,128)(2,1)S(1)}, u32[]{:S(2)}, u32[]{:S(2)}) collective-permute-start(bf16[176,128]{1,0:T(8,128)(2,1)S(1)} %add_convert_fusion.1), channel_id=1, source_target_pairs={{0,8},{4,12},{8,0},{12,4},{1,9},{5,13},{9,1},{13,5},{2,10},{6,14},... | collective-permute-start | bytes 135176 | tf_op jit(solution)/shard_map/ppermute | solution.py:289
  175.4 5.9 %collective-permute-start.7 = (bf16[176,128]{1,0:T(8,128)(2,1)S(1)}, bf16[176,128]{1,0:T(8,128)(2,1)S(1)}, u32[]{:S(2)}, u32[]{:S(2)}) collective-permute-start(bf16[176,128]{1,0:T(8,128)(2,1)S(1)} %add_convert_fusion), channel_id=1, source_target_pairs={{0,1},{1,0},{2,3},{3,2},{4,5},{5,4},{6,7},{7,6},{8,9},{9,8},{10,11... | collective-permute-start | bytes 135176 | tf_op jit(solution)/shard_map/ppermute | solution.py:389
  (6 other events, 4.5 us)
Sparse Core Ops, SparseCore 0:
  10.7 80.4 all-gather.1

commit v5 on v3

--- a/solution.py
+++ b/solution.py
@@ -16,7 +16,7 @@
 TABLE = ("yh", "yl", "c")
 DP = ("x", "zh", "zl")
 EVERY = ("x", "zh", "zl", "yh", "yl", "c")
-CHUNK = 192
+CHUNK = 176
 
 NT = (((1,), (1,)), ((), ()))
 TN = (((0,), (0,)), ((), ()))
@@ -166,7 +166,7 @@
     rows += [third_sum, jnp.zeros((9, 128), jnp.float32)]
     out_ref[1344:1360, :] = jnp.concatenate(rows, axis=0).astype(jnp.bfloat16)
     out_ref[1360:1392, :] = bias_ref[...].astype(jnp.bfloat16)
-    out_ref[1392:1536, :] = jnp.zeros((144, 128), jnp.bfloat16)
+    out_ref[1392:1408, :] = jnp.zeros((16, 128), jnp.bfloat16)
 
 
 def unpack_kernel(whole, first_grad, second_grad, third_grad, first_sum, second_sum, third_sum, bias_sum):
@@ -359,7 +359,12 @@
     table_parts = lax.all_to_all(table_parts, DP, split_axis=0, concat_axis=0, tiled=True)
     table_grad = jnp.sum(table_parts.astype(jnp.float32), axis=0)
 
-    part = spread_sum(part, "yh", (1, 2)).astype(jnp.bfloat16)
+    sent = part.astype(jnp.bfloat16)
+    four = [
+        lax.ppermute(sent, "yh", [(place, place ^ distance) for place in range(4)]).astype(jnp.float32)
+        for distance in (1, 2, 3)
+    ]
+    part = ((sent.astype(jnp.float32) + four[0]) + (four[1] + four[2])).astype(jnp.bfloat16)
     other = lax.ppermute(part, "c", [(0, 1), (1, 0)])
     pair = jnp.where(core == 0, jnp.stack([part, other]), jnp.stack([other, part]))
     whole = lax.all_gather(pair.reshape(2 * CHUNK, 128), "x", axis=0, tiled=True)

time: 203 us -> 201 us (level)
  waiting for transfers between devices: 70 us -> 64.9 us
  starting transfers between devices: 55.3 us -> 58.7 us
    ppermute x0 -> x3, starting transfers between devices: none -> 11.4 us  [local(): lax.ppermute(sent, 'yh', [(place, place ^ distance) for place in range(4)])]
    ppermute x3 -> x1, waiting for transfers between devices: 11 us -> 1.8 us  [spread_sum(): lax.ppermute(sent, axis, [(place, place ^ distance) for place in range(si...]
    ppermute x3 -> x1, starting transfers between devices: 8.87 us -> 3.27 us  [spread_sum(): lax.ppermute(sent, axis, [(place, place ^ distance) for place in range(si...]
    ppermute x0 -> x3, waiting for transfers between devices: none -> 3.18 us  [local(): lax.ppermute(sent, 'yh', [(place, place ^ distance) for place in range(4)])]
  transfers between devices with their start and end apart: 13 -> 14, of which waited for: 11 -> 10; matrix products, arithmetic and copies ran while one was open for 2% -> 2% of each run, Pallas kernels for 13% -> 13%
where the time goes in v5:
time: 201 us; the launch traced here: 199 us
  waiting for transfers between devices  64.9 us (32%)
  starting transfers between devices  58.7 us (29%)
  Pallas kernels  34.4 us (17%)
  between operations  14.4 us (7%)
  local copies, waits for them, and re-layouts  11.3 us (6%)
  blocking collectives  11.1 us (6%)
  other arithmetic  4.37 us (2%)
    all_to_all x1, waiting for transfers between devices, local(): lax.all_to_all(pooled, TABLE, split_axis=0, concat_axis=0, tiled=True)  29.9 us
    all_gather x1, waiting for transfers between devices, local(): lax.all_gather(jnp.concatenate([cross_up, cross_down.T], axis=1), TABLE,...  16.2 us
    pallas_call x1, Pallas kernels, pool(): pl.pallas_call(pool_kernel, grid=(shards, batch // BLOCK), in_specs=[pl.B...  15 us
    ppermute x3, starting transfers between devices, local(): lax.ppermute(sent, 'yh', [(place, place ^ distance) for place in range(4)])  11.4 us
    all_gather x1, blocking collectives, local(): lax.all_gather(pair.reshape(2 * CHUNK, 128), 'x', axis=0, tiled=True)  11.1 us
    all_to_all x1, starting transfers between devices, local(): lax.all_to_all(pooled, TABLE, split_axis=0, concat_axis=0, tiled=True)  10.4 us
    ppermute x3, starting transfers between devices, local(): lax.ppermute(piece, 'x', [(place, (place + shift) % length) for place in...  9.28 us
    unnamed x35, local copies, waits for them, and re-layouts  8.67 us
  transfers between devices with their start and end apart: 14, of which 10 were waited for; matrix products, arithmetic and copies ran while one was open for 2% of the time, Pallas kernels for 13%

profile of v5, /device:TPU:1, one launch (start us, length us, event | category | flops | bytes accessed | tf_op | source)
XLA Modules:
  0.0 199.1 jit_solution(5544303121299143209)
XLA Ops:
  7.2 1.8 pad_maximum_fusion
  11.7 15.0 %pool.1 = (bf16[2,8,2048,256]{3,2,1,0:T(8,128)(2,1)}, bf16[2048,256]{1,0:T(8,128)(2,1)}) custom-call(s32[2,64,256]{2,1,0:T(8,128)S(1)} %copy.34.code_ref, bf16[2,2048,128]{2,1,0:T(8,128)(2,1)S(1)} %copy-done), custom_call_target="tpu_custom_call" | custom-call | tf_op jit(solution)/shard_map/pool/pallas_call | solution.py:66
  26.7 10.4 %all-to-all-start = ((bf16[16,128,256]{2,1,0:T(8,128)(2,1)}), bf16[16,128,256]{2,1,0:T(8,128)(2,1)S(1)}, u32[]{:S(2)}, u32[]{:S(2)}) async-start(bf16[16,128,256]{2,1,0:T(8,128)(2,1)} %bitcast.2), calls=%async_computation | async-start | bytes 2097152 | tf_op jit(solution)/shard_map/all_to_all | solution.py:313
  45.0 29.9 %all-to-all-done.arrived_ref = bf16[16,128,256]{2,1,0:T(8,128)(2,1)S(1)} async-done(((bf16[16,128,256]{2,1,0:T(8,128)(2,1)}), bf16[16,128,256]{2,1,0:T(8,128)(2,1)S(1)}, u32[]{:S(2)}, u32[]{:S(2)}) %all-to-all-start) | async-done | bytes 1048608 | tf_op jit(solution)/shard_map/all_to_all | solution.py:313
  74.9 16.2 %all-gather.2.cloned.1.call-done.weights_ref = bf16[512,6912]{1,0:T(8,128)(2,1)} async-done(((bf16[32,6912]{1,0:T(8,128)(2,1)}), bf16[512,6912]{1,0:T(8,128)(2,1)}) %all-gather.2.cloned.1.call-update) | async-done | bytes 7077904 | tf_op jit(solution)/shard_map/all_gather | solution.py:310
  91.2 8.6 %cross.1 = (bf16[16,128,256]{2,1,0:T(8,128)(2,1)}, bf16[128,128]{1,0:T(8,128)(2,1)}, f32[32,128]{1,0:T(8,128)}) custom-call(s32[32]{0:T(128)} %owner_ref.1, bf16[16,128,256]{2,1,0:T(8,128)(2,1)} %copy-done.16, bf16[128,128]{1,0:T(8,128)(2,1)} %copy-done.5, bf16[512,6912]{1,0:T(8,128)(2,1)} %all-gather.2.cloned.1.call-done.weights_ref, ...), custom_call_target="tpu_custom_call" | custom-call | tf_op jit(solution)/shard_map/cross/pallas_call | solution.py:236
  99.8 4.8 %all-to-all-start.1 = ((bf16[16,128,256]{2,1,0:T(8,128)(2,1)}), bf16[16,128,256]{2,1,0:T(8,128)(2,1)S(1)}, u32[]{:S(2)}, u32[]{:S(2)}) async-start(bf16[16,128,256]{2,1,0:T(8,128)(2,1)} %get-tuple-element.22), calls=%async_computation.1 | async-start | bytes 2097152 | tf_op jit(solution)/shard_map/all_to_all | solution.py:328
  107.0 2.0 %collective-permute-start = (bf16[4,176,128]{2,1,0:T(8,128)(2,1)S(1)}, bf16[4,176,128]{2,1,0:T(8,128)(2,1)S(1)}, u32[]{:S(2)}, u32[]{:S(2)}) collective-permute-start(bf16[4,176,128]{2,1,0:T(8,128)(2,1)S(1)} %dynamic-slice_bitcast_fusion), channel_id=1, source_target_pairs={{0,1},{1,0},{2,3},{3,2},{4,5},{5,4},{6,7},{7,6},{8,9},{9,8},{10,11... | collective-permute-start | bytes 540680 | tf_op jit(solution)/shard_map/ppermute | solution.py:342
  110.4 4.3 %collective-permute-start.3 = (bf16[176,128]{1,0:T(8,128)(2,1)S(1)}, bf16[176,128]{1,0:T(8,128)(2,1)S(1)}, u32[]{:S(2)}, u32[]{:S(2)}) collective-permute-start(bf16[176,128]{1,0:T(8,128)(2,1)S(1)} %get-tuple-element.35), channel_id=1, source_target_pairs={{0,384},{128,0},{256,128},{384,256},{1,385},{129,1},{257,129},{385... | collective-permute-start | bytes 135176 | tf_op jit(solution)/shard_map/ppermute | solution.py:349
  114.7 2.5 %collective-permute-start.2 = (bf16[176,128]{1,0:T(8,128)(2,1)S(1)}, bf16[176,128]{1,0:T(8,128)(2,1)S(1)}, u32[]{:S(2)}, u32[]{:S(2)}) collective-permute-start(bf16[176,128]{1,0:T(8,128)(2,1)S(1)} %get-tuple-element.36), channel_id=1, source_target_pairs={{0,256},{128,384},{256,0},{384,128},{1,257},{129,385},{257,1},{385... | collective-permute-start | bytes 135176 | tf_op jit(solution)/shard_map/ppermute | solution.py:349
  117.2 2.5 %collective-permute-start.1 = (bf16[176,128]{1,0:T(8,128)(2,1)S(1)}, bf16[176,128]{1,0:T(8,128)(2,1)S(1)}, u32[]{:S(2)}, u32[]{:S(2)}) collective-permute-start(bf16[176,128]{1,0:T(8,128)(2,1)S(1)} %get-tuple-element.34), channel_id=1, source_target_pairs={{0,128},{128,256},{256,384},{384,0},{1,129},{129,257},{257,385},{3... | collective-permute-start | bytes 135176 | tf_op jit(solution)/shard_map/ppermute | solution.py:349
  121.3 2.2 %collective-permute-done.1 = bf16[176,128]{1,0:T(8,128)(2,1)S(1)} collective-permute-done((bf16[176,128]{1,0:T(8,128)(2,1)S(1)}, bf16[176,128]{1,0:T(8,128)(2,1)S(1)}, u32[]{:S(2)}, u32[]{:S(2)}) %collective-permute-start.1) | collective-permute-done | bytes 45088 | tf_op jit(solution)/shard_map/ppermute | solution.py:349
  123.5 3.3 %collective-permute-start.4 = (bf16[176,128]{1,0:T(8,128)(2,1)S(1)}, bf16[176,128]{1,0:T(8,128)(2,1)S(1)}, u32[]{:S(2)}, u32[]{:S(2)}) collective-permute-start(bf16[176,128]{1,0:T(8,128)(2,1)S(1)} %fusion.3.one_ref), channel_id=1, source_target_pairs={{0,16},{16,0},{1,17},{17,1},{2,18},{18,2},{3,19},{19,3},{4,20},{20... | collective-permute-start | bytes 135176 | tf_op jit(solution)/shard_map/ppermute | solution.py:263
  128.6 3.8 %all-to-all-done.1.after_ref = bf16[16,128,256]{2,1,0:T(8,128)(2,1)S(1)} async-done(((bf16[16,128,256]{2,1,0:T(8,128)(2,1)}), bf16[16,128,256]{2,1,0:T(8,128)(2,1)S(1)}, u32[]{:S(2)}, u32[]{:S(2)}) %all-to-all-start.1) | async-done | bytes 1048608 | tf_op jit(solution)/shard_map/all_to_all | solution.py:328
  133.3 7.1 %all-to-all-start.2 = ((bf16[8,176,128]{2,1,0:T(8,128)(2,1)}), bf16[8,176,128]{2,1,0:T(8,128)(2,1)S(1)}, u32[]{:S(2)}, u32[]{:S(2)}) async-start(bf16[8,176,128]{2,1,0:T(8,128)(2,1)} %broadcast_in_dim.25), calls=%async_computation.2 | async-start | bytes 720896 | tf_op jit(solution)/shard_map/all_to_all | solution.py:354
  140.4 8.5 %table_grads.1.value_ref = bf16[32,2,64,128]{3,2,1,0:T(8,128)(2,1)} custom-call(bf16[2,8,2048,256]{3,2,1,0:T(8,128)(2,1)} %get-tuple-element.20.hits_ref, bf16[2048,256]{1,0:T(8,128)(2,1)S(1)} %bitcast.37), custom_call_target="tpu_custom_call" | custom-call | flops 2147483648 | bytes 18874368 | tf_op jit(solution)/shard_map/table_grads/pallas_call | solution.py:103
  148.9 4.0 %all-to-all-done.2 = bf16[8,176,128]{2,1,0:T(8,128)(2,1)S(1)} async-done(((bf16[8,176,128]{2,1,0:T(8,128)(2,1)}), bf16[8,176,128]{2,1,0:T(8,128)(2,1)S(1)}, u32[]{:S(2)}, u32[]{:S(2)}) %all-to-all-start.2) | async-done | bytes 360480 | tf_op jit(solution)/shard_map/all_to_all | solution.py:354
  152.9 6.2 %all-to-all-start.3 = ((bf16[32,2,64,128]{3,2,1,0:T(8,128)(2,1)}), bf16[32,2,64,128]{3,2,1,0:T(8,128)(2,1)S(1)}, u32[]{:S(2)}, u32[]{:S(2)}) async-start(bf16[32,2,64,128]{3,2,1,0:T(8,128)(2,1)} %hold.1), calls=%async_computation.3 | async-start | bytes 2097152 | tf_op jit(solution)/shard_map/all_to_all | solution.py:359
  159.1 1.9 collective-permute-start.7
  161.1 6.2 %collective-permute-start.6 = (bf16[176,128]{1,0:T(8,128)(2,1)S(1)}, bf16[176,128]{1,0:T(8,128)(2,1)S(1)}, u32[]{:S(2)}, u32[]{:S(2)}) collective-permute-start(bf16[176,128]{1,0:T(8,128)(2,1)S(1)} %convert_element_type.58), channel_id=1, source_target_pairs={{0,8},{4,12},{8,0},{12,4},{1,9},{5,13},{9,1},{13,5},{2,10},{6,14},... | collective-permute-start | bytes 135176 | tf_op jit(solution)/shard_map/ppermute | solution.py:364
  167.3 3.2 %collective-permute-start.5 = (bf16[176,128]{1,0:T(8,128)(2,1)S(1)}, bf16[176,128]{1,0:T(8,128)(2,1)S(1)}, u32[]{:S(2)}, u32[]{:S(2)}) collective-permute-start(bf16[176,128]{1,0:T(8,128)(2,1)S(1)} %convert_element_type.58), channel_id=1, source_target_pairs={{0,4},{4,0},{8,12},{12,8},{1,5},{5,1},{9,13},{13,9},{2,6},{6,2},{1... | collective-permute-start | bytes 135176 | tf_op jit(solution)/shard_map/ppermute | solution.py:364
  170.6 3.2 %collective-permute-done.5 = bf16[176,128]{1,0:T(8,128)(2,1)S(1)} collective-permute-done((bf16[176,128]{1,0:T(8,128)(2,1)S(1)}, bf16[176,128]{1,0:T(8,128)(2,1)S(1)}, u32[]{:S(2)}, u32[]{:S(2)}) %collective-permute-start.5) | collective-permute-done | bytes 45088 | tf_op jit(solution)/shard_map/ppermute | solution.py:364
  173.8 4.2 %collective-permute-start.8 = (bf16[176,128]{1,0:T(8,128)(2,1)S(1)}, bf16[176,128]{1,0:T(8,128)(2,1)S(1)}, u32[]{:S(2)}, u32[]{:S(2)}) collective-permute-start(bf16[176,128]{1,0:T(8,128)(2,1)S(1)} %add_convert_fusion), channel_id=1, source_target_pairs={{0,1},{1,0},{2,3},{3,2},{4,5},{5,4},{6,7},{7,6},{8,9},{9,8},{10,11... | collective-permute-start | bytes 135176 | tf_op jit(solution)/shard_map/ppermute | solution.py:368
  178.8 11.1 %all_gather.7.whole = bf16[1408,128]{1,0:T(8,128)(2,1)S(1)} all-gather(bf16[352,128]{1,0:T(8,128)(2,1)S(1)} %bitcast.48), channel_id=1, replica_groups=mesh['x'=4,'zh'=4,'zl'=2,'yh'=4,'yl'=2,'c'=2] {'x'}, dimensions={0}, use_global_device_ids=true | all-gather | bytes 450560 | tf_op jit(solution)/shard_map/all_gather | solution.py:370
  (66 shorter events, 21.7 us)
Async XLA Ops:
  7.2 84.0 %all-gather.2.cloned.1.call-start = ((), (), s32[]{:S(2)}) async-start(), calls=%async_computation.4 | async-start | bytes 7520256 | tf_op jit(solution)/shard_map/all_gather | solution.py:310
  10.5 1.2 copy-start
  26.7 77.8 %copy-start.2 = (bf16[512,256]{1,0:T(8,128)(2,1)S(1)}, bf16[512,256]{1,0:T(8,128)(2,1)}, u32[]{:S(2)}) copy-start(bf16[512,256]{1,0:T(8,128)(2,1)} %w2.3) | copy-start | bytes 786436
  26.7 77.8 %copy-start.4 = (bf16[256,128]{1,0:T(8,128)(2,1)S(1)}, bf16[256,128]{1,0:T(8,128)(2,1)}, u32[]{:S(2)}) copy-start(bf16[256,128]{1,0:T(8,128)(2,1)} %w3.3) | copy-start | bytes 196612
  26.7 77.8 %copy-start.7 = (bf16[13,512]{1,0:T(8,128)(2,1)S(1)}, bf16[13,512]{1,0:T(8,128)(2,1)}, u32[]{:S(2)}) copy-start(bf16[13,512]{1,0:T(8,128)(2,1)} %w1.3) | copy-start | bytes 39940
  26.7 77.8 %copy-start.11 = (f32[512]{0:T(512)S(1)}, f32[512]{0:T(512)}, u32[]{:S(2)}) copy-start(f32[512]{0:T(512)} %param.21) | copy-start | bytes 6148
  26.7 77.8 %copy-start.13 = (f32[256]{0:T(256)S(1)}, f32[256]{0:T(256)}, u32[]{:S(2)}) copy-start(f32[256]{0:T(256)} %param.23) | copy-start | bytes 3076
  26.7 77.8 %copy-start.15 = (f32[128]{0:T(128)S(1)}, f32[128]{0:T(128)}, u32[]{:S(2)}) copy-start(f32[128]{0:T(128)} %param.25) | copy-start | bytes 1540
  26.7 48.2 %all-to-all-start = ((bf16[16,128,256]{2,1,0:T(8,128)(2,1)}), bf16[16,128,256]{2,1,0:T(8,128)(2,1)S(1)}, u32[]{:S(2)}, u32[]{:S(2)}) async-start(bf16[16,128,256]{2,1,0:T(8,128)(2,1)} %bitcast.2), calls=%async_computation | async-start | bytes 2097152 | tf_op jit(solution)/shard_map/all_to_all | solution.py:313
  39.3 0.9 copy-start.1
  40.3 0.8 copy-start.3
  74.9 16.2 %copy-start.16 = (bf16[16,128,256]{2,1,0:T(8,128)(2,1)}, bf16[16,128,256]{2,1,0:T(8,128)(2,1)S(1)}, u32[]{:S(2)}) copy-start(bf16[16,128,256]{2,1,0:T(8,128)(2,1)S(1)} %all-to-all-done.arrived_ref) | copy-start | bytes 3145732
  99.8 32.7 %all-to-all-start.1 = ((bf16[16,128,256]{2,1,0:T(8,128)(2,1)}), bf16[16,128,256]{2,1,0:T(8,128)(2,1)S(1)}, u32[]{:S(2)}, u32[]{:S(2)}) async-start(bf16[16,128,256]{2,1,0:T(8,128)(2,1)} %get-tuple-element.22), calls=%async_computation.1 | async-start | bytes 2097152 | tf_op jit(solution)/shard_map/all_to_all | solution.py:328
  107.0 3.3 %collective-permute-start = (bf16[4,176,128]{2,1,0:T(8,128)(2,1)S(1)}, bf16[4,176,128]{2,1,0:T(8,128)(2,1)S(1)}, u32[]{:S(2)}, u32[]{:S(2)}) collective-permute-start(bf16[4,176,128]{2,1,0:T(8,128)(2,1)S(1)} %dynamic-slice_bitcast_fusion), channel_id=1, source_target_pairs={{0,1},{1,0},{2,3},{3,2},{4,5},{5,4},{6,7},{7,6},{8,9},{9,8},{10,11... | collective-permute-start | bytes 540680 | tf_op jit(solution)/shard_map/ppermute | solution.py:342
  110.4 9.3 %collective-permute-start.3 = (bf16[176,128]{1,0:T(8,128)(2,1)S(1)}, bf16[176,128]{1,0:T(8,128)(2,1)S(1)}, u32[]{:S(2)}, u32[]{:S(2)}) collective-permute-start(bf16[176,128]{1,0:T(8,128)(2,1)S(1)} %get-tuple-element.35), channel_id=1, source_target_pairs={{0,384},{128,0},{256,128},{384,256},{1,385},{129,1},{257,129},{385... | collective-permute-start | bytes 135176 | tf_op jit(solution)/shard_map/ppermute | solution.py:349
  114.7 6.6 %collective-permute-start.2 = (bf16[176,128]{1,0:T(8,128)(2,1)S(1)}, bf16[176,128]{1,0:T(8,128)(2,1)S(1)}, u32[]{:S(2)}, u32[]{:S(2)}) collective-permute-start(bf16[176,128]{1,0:T(8,128)(2,1)S(1)} %get-tuple-element.36), channel_id=1, source_target_pairs={{0,256},{128,384},{256,0},{384,128},{1,257},{129,385},{257,1},{385... | collective-permute-start | bytes 135176 | tf_op jit(solution)/shard_map/ppermute | solution.py:349
  117.2 6.3 %collective-permute-start.1 = (bf16[176,128]{1,0:T(8,128)(2,1)S(1)}, bf16[176,128]{1,0:T(8,128)(2,1)S(1)}, u32[]{:S(2)}, u32[]{:S(2)}) collective-permute-start(bf16[176,128]{1,0:T(8,128)(2,1)S(1)} %get-tuple-element.34), channel_id=1, source_target_pairs={{0,128},{128,256},{256,384},{384,0},{1,129},{129,257},{257,385},{3... | collective-permute-start | bytes 135176 | tf_op jit(solution)/shard_map/ppermute | solution.py:349
  123.5 5.1 %collective-permute-start.4 = (bf16[176,128]{1,0:T(8,128)(2,1)S(1)}, bf16[176,128]{1,0:T(8,128)(2,1)S(1)}, u32[]{:S(2)}, u32[]{:S(2)}) collective-permute-start(bf16[176,128]{1,0:T(8,128)(2,1)S(1)} %fusion.3.one_ref), channel_id=1, source_target_pairs={{0,16},{16,0},{1,17},{17,1},{2,18},{18,2},{3,19},{19,3},{4,20},{20... | collective-permute-start | bytes 135176 | tf_op jit(solution)/shard_map/ppermute | solution.py:263
  133.3 19.6 %all-to-all-start.2 = ((bf16[8,176,128]{2,1,0:T(8,128)(2,1)}), bf16[8,176,128]{2,1,0:T(8,128)(2,1)S(1)}, u32[]{:S(2)}, u32[]{:S(2)}) async-start(bf16[8,176,128]{2,1,0:T(8,128)(2,1)} %broadcast_in_dim.25), calls=%async_computation.2 | async-start | bytes 720896 | tf_op jit(solution)/shard_map/all_to_all | solution.py:354
  152.9 38.5 %all-to-all-start.3 = ((bf16[32,2,64,128]{3,2,1,0:T(8,128)(2,1)}), bf16[32,2,64,128]{3,2,1,0:T(8,128)(2,1)S(1)}, u32[]{:S(2)}, u32[]{:S(2)}) async-start(bf16[32,2,64,128]{3,2,1,0:T(8,128)(2,1)} %hold.1), calls=%async_computation.3 | async-start | bytes 2097152 | tf_op jit(solution)/shard_map/all_to_all | solution.py:359
  159.1 11.4 %collective-permute-start.7 = (bf16[176,128]{1,0:T(8,128)(2,1)S(1)}, bf16[176,128]{1,0:T(8,128)(2,1)S(1)}, u32[]{:S(2)}, u32[]{:S(2)}) collective-permute-start(bf16[176,128]{1,0:T(8,128)(2,1)S(1)} %convert_element_type.58), channel_id=1, source_target_pairs={{0,12},{4,8},{8,4},{12,0},{1,13},{5,9},{9,5},{13,1},{2,14},{6,10},... | collective-permute-start | bytes 135176 | tf_op jit(solution)/shard_map/ppermute | solution.py:364
  161.1 9.5 %collective-permute-start.6 = (bf16[176,128]{1,0:T(8,128)(2,1)S(1)}, bf16[176,128]{1,0:T(8,128)(2,1)S(1)}, u32[]{:S(2)}, u32[]{:S(2)}) collective-permute-start(bf16[176,128]{1,0:T(8,128)(2,1)S(1)} %convert_element_type.58), channel_id=1, source_target_pairs={{0,8},{4,12},{8,0},{12,4},{1,9},{5,13},{9,1},{13,5},{2,10},{6,14},... | collective-permute-start | bytes 135176 | tf_op jit(solution)/shard_map/ppermute | solution.py:364
  167.3 6.4 %collective-permute-start.5 = (bf16[176,128]{1,0:T(8,128)(2,1)S(1)}, bf16[176,128]{1,0:T(8,128)(2,1)S(1)}, u32[]{:S(2)}, u32[]{:S(2)}) collective-permute-start(bf16[176,128]{1,0:T(8,128)(2,1)S(1)} %convert_element_type.58), channel_id=1, source_target_pairs={{0,4},{4,0},{8,12},{12,8},{1,5},{5,1},{9,13},{13,9},{2,6},{6,2},{1... | collective-permute-start | bytes 135176 | tf_op jit(solution)/shard_map/ppermute | solution.py:364
  173.8 5.0 %collective-permute-start.8 = (bf16[176,128]{1,0:T(8,128)(2,1)S(1)}, bf16[176,128]{1,0:T(8,128)(2,1)S(1)}, u32[]{:S(2)}, u32[]{:S(2)}) collective-permute-start(bf16[176,128]{1,0:T(8,128)(2,1)S(1)} %add_convert_fusion), channel_id=1, source_target_pairs={{0,1},{1,0},{2,3},{3,2},{4,5},{5,4},{6,7},{7,6},{8,9},{9,8},{10,11... | collective-permute-start | bytes 135176 | tf_op jit(solution)/shard_map/ppermute | solution.py:368
  (7 other events, 4.8 us)
Sparse Core Ops, SparseCore 0:
  10.7 80.4 all-gather.1

commit v6 on v5

--- a/solution.py
+++ b/solution.py
@@ -11,7 +11,7 @@
 TABLES = 26
 WIDTH = 128
 GROUP = 32
-BLOCK = 256
+BLOCK = 512
 LOW = 256
 TABLE = ("yh", "yl", "c")
 DP = ("x", "zh", "zl")
@@ -78,7 +78,7 @@
             pltpu.HBM((shards, rows // LOW, batch, LOW), jnp.bfloat16),
             jax.ShapeDtypeStruct((batch, shards * WIDTH), jnp.bfloat16),
         ],
-        compiler_params=params(8),
+        compiler_params=params(16),
         name="pool",
     )(code, embed_tables)
 

time: 201 us -> 201 us (level)
  Pallas kernels: 34.4 us -> 31.5 us
  waiting for transfers between devices: 64.9 us -> 67.8 us
    pallas_call x1, Pallas kernels: 15 us -> 12.1 us  [pool(): pl.pallas_call(pool_kernel, grid=(shards, batch // BLOCK), in_specs=[pl.B...]
    all_gather x1, waiting for transfers between devices: 16.2 us -> 19.1 us  [local(): lax.all_gather(jnp.concatenate([cross_up, cross_down.T], axis=1), TABLE,...]
  transfers between devices with their start and end apart: 14 -> 14, of which waited for: 10 -> 10; matrix products, arithmetic and copies ran while one was open for 2% -> 2% of each run, Pallas kernels for 13% -> 12%
where the time goes in v6:
time: 201 us; the launch traced here: 199 us
  waiting for transfers between devices  67.8 us (34%)
  starting transfers between devices  58.6 us (29%)
  Pallas kernels  31.5 us (16%)
  between operations  14.4 us (7%)
  local copies, waits for them, and re-layouts  11.3 us (6%)
  blocking collectives  11.1 us (6%)
  other arithmetic  4.37 us (2%)
    all_to_all x1, waiting for transfers between devices, local(): lax.all_to_all(pooled, TABLE, split_axis=0, concat_axis=0, tiled=True)  29.9 us
    all_gather x1, waiting for transfers between devices, local(): lax.all_gather(jnp.concatenate([cross_up, cross_down.T], axis=1), TABLE,...  19.1 us
    pallas_call x1, Pallas kernels, pool(): pl.pallas_call(pool_kernel, grid=(shards, batch // BLOCK), in_specs=[pl.B...  12.1 us
    ppermute x3, starting transfers between devices, local(): lax.ppermute(sent, 'yh', [(place, place ^ distance) for place in range(4)])  11.4 us
    all_gather x1, blocking collectives, local(): lax.all_gather(pair.reshape(2 * CHUNK, 128), 'x', axis=0, tiled=True)  11.1 us
    all_to_all x1, starting transfers between devices, local(): lax.all_to_all(pooled, TABLE, split_axis=0, concat_axis=0, tiled=True)  10.5 us
    ppermute x3, starting transfers between devices, local(): lax.ppermute(piece, 'x', [(place, (place + shift) % length) for place in...  9.28 us
    unnamed x35, local copies, waits for them, and re-layouts  8.7 us
  transfers between devices with their start and end apart: 14, of which 10 were waited for; matrix products, arithmetic and copies ran while one was open for 2% of the time, Pallas kernels for 12%

profile of v6, /device:TPU:1, one launch (start us, length us, event | category | flops | bytes accessed | tf_op | source)
XLA Modules:
  0.0 199.1 jit_solution(14650921869823960686)
XLA Ops:
  7.2 1.8 pad_maximum_fusion
  11.7 12.1 %pool.1 = (bf16[2,8,2048,256]{3,2,1,0:T(8,128)(2,1)}, bf16[2048,256]{1,0:T(8,128)(2,1)}) custom-call(s32[2,64,256]{2,1,0:T(8,128)S(1)} %copy.34.code_ref, bf16[2,2048,128]{2,1,0:T(8,128)(2,1)S(1)} %copy-done), custom_call_target="tpu_custom_call" | custom-call | tf_op jit(solution)/shard_map/pool/pallas_call | solution.py:66
  23.9 10.5 %all-to-all-start = ((bf16[16,128,256]{2,1,0:T(8,128)(2,1)}), bf16[16,128,256]{2,1,0:T(8,128)(2,1)S(1)}, u32[]{:S(2)}, u32[]{:S(2)}) async-start(bf16[16,128,256]{2,1,0:T(8,128)(2,1)} %bitcast.2), calls=%async_computation | async-start | bytes 2097152 | tf_op jit(solution)/shard_map/all_to_all | solution.py:313
  42.2 29.9 %all-to-all-done.arrived_ref = bf16[16,128,256]{2,1,0:T(8,128)(2,1)S(1)} async-done(((bf16[16,128,256]{2,1,0:T(8,128)(2,1)}), bf16[16,128,256]{2,1,0:T(8,128)(2,1)S(1)}, u32[]{:S(2)}, u32[]{:S(2)}) %all-to-all-start) | async-done | bytes 1048608 | tf_op jit(solution)/shard_map/all_to_all | solution.py:313
  72.1 19.1 %all-gather.2.cloned.1.call-done.weights_ref = bf16[512,6912]{1,0:T(8,128)(2,1)} async-done(((bf16[32,6912]{1,0:T(8,128)(2,1)}), bf16[512,6912]{1,0:T(8,128)(2,1)}) %all-gather.2.cloned.1.call-update) | async-done | bytes 7077904 | tf_op jit(solution)/shard_map/all_gather | solution.py:310
  91.2 8.6 %cross.1 = (bf16[16,128,256]{2,1,0:T(8,128)(2,1)}, bf16[128,128]{1,0:T(8,128)(2,1)}, f32[32,128]{1,0:T(8,128)}) custom-call(s32[32]{0:T(128)} %owner_ref.1, bf16[16,128,256]{2,1,0:T(8,128)(2,1)} %copy-done.16, bf16[128,128]{1,0:T(8,128)(2,1)} %copy-done.5, bf16[512,6912]{1,0:T(8,128)(2,1)} %all-gather.2.cloned.1.call-done.weights_ref, ...), custom_call_target="tpu_custom_call" | custom-call | tf_op jit(solution)/shard_map/cross/pallas_call | solution.py:236
  99.8 4.7 %all-to-all-start.1 = ((bf16[16,128,256]{2,1,0:T(8,128)(2,1)}), bf16[16,128,256]{2,1,0:T(8,128)(2,1)S(1)}, u32[]{:S(2)}, u32[]{:S(2)}) async-start(bf16[16,128,256]{2,1,0:T(8,128)(2,1)} %get-tuple-element.22), calls=%async_computation.1 | async-start | bytes 2097152 | tf_op jit(solution)/shard_map/all_to_all | solution.py:328
  107.0 2.0 %collective-permute-start = (bf16[4,176,128]{2,1,0:T(8,128)(2,1)S(1)}, bf16[4,176,128]{2,1,0:T(8,128)(2,1)S(1)}, u32[]{:S(2)}, u32[]{:S(2)}) collective-permute-start(bf16[4,176,128]{2,1,0:T(8,128)(2,1)S(1)} %dynamic-slice_bitcast_fusion), channel_id=1, source_target_pairs={{0,1},{1,0},{2,3},{3,2},{4,5},{5,4},{6,7},{7,6},{8,9},{9,8},{10,11... | collective-permute-start | bytes 540680 | tf_op jit(solution)/shard_map/ppermute | solution.py:342
  110.4 4.3 %collective-permute-start.3 = (bf16[176,128]{1,0:T(8,128)(2,1)S(1)}, bf16[176,128]{1,0:T(8,128)(2,1)S(1)}, u32[]{:S(2)}, u32[]{:S(2)}) collective-permute-start(bf16[176,128]{1,0:T(8,128)(2,1)S(1)} %get-tuple-element.35), channel_id=1, source_target_pairs={{0,384},{128,0},{256,128},{384,256},{1,385},{129,1},{257,129},{385... | collective-permute-start | bytes 135176 | tf_op jit(solution)/shard_map/ppermute | solution.py:349
  114.7 2.5 %collective-permute-start.2 = (bf16[176,128]{1,0:T(8,128)(2,1)S(1)}, bf16[176,128]{1,0:T(8,128)(2,1)S(1)}, u32[]{:S(2)}, u32[]{:S(2)}) collective-permute-start(bf16[176,128]{1,0:T(8,128)(2,1)S(1)} %get-tuple-element.36), channel_id=1, source_target_pairs={{0,256},{128,384},{256,0},{384,128},{1,257},{129,385},{257,1},{385... | collective-permute-start | bytes 135176 | tf_op jit(solution)/shard_map/ppermute | solution.py:349
  117.2 2.5 %collective-permute-start.1 = (bf16[176,128]{1,0:T(8,128)(2,1)S(1)}, bf16[176,128]{1,0:T(8,128)(2,1)S(1)}, u32[]{:S(2)}, u32[]{:S(2)}) collective-permute-start(bf16[176,128]{1,0:T(8,128)(2,1)S(1)} %get-tuple-element.34), channel_id=1, source_target_pairs={{0,128},{128,256},{256,384},{384,0},{1,129},{129,257},{257,385},{3... | collective-permute-start | bytes 135176 | tf_op jit(solution)/shard_map/ppermute | solution.py:349
  121.3 2.2 %collective-permute-done.1 = bf16[176,128]{1,0:T(8,128)(2,1)S(1)} collective-permute-done((bf16[176,128]{1,0:T(8,128)(2,1)S(1)}, bf16[176,128]{1,0:T(8,128)(2,1)S(1)}, u32[]{:S(2)}, u32[]{:S(2)}) %collective-permute-start.1) | collective-permute-done | bytes 45088 | tf_op jit(solution)/shard_map/ppermute | solution.py:349
  123.5 3.3 %collective-permute-start.4 = (bf16[176,128]{1,0:T(8,128)(2,1)S(1)}, bf16[176,128]{1,0:T(8,128)(2,1)S(1)}, u32[]{:S(2)}, u32[]{:S(2)}) collective-permute-start(bf16[176,128]{1,0:T(8,128)(2,1)S(1)} %fusion.3.one_ref), channel_id=1, source_target_pairs={{0,16},{16,0},{1,17},{17,1},{2,18},{18,2},{3,19},{19,3},{4,20},{20... | collective-permute-start | bytes 135176 | tf_op jit(solution)/shard_map/ppermute | solution.py:263
  128.6 3.8 %all-to-all-done.1.after_ref = bf16[16,128,256]{2,1,0:T(8,128)(2,1)S(1)} async-done(((bf16[16,128,256]{2,1,0:T(8,128)(2,1)}), bf16[16,128,256]{2,1,0:T(8,128)(2,1)S(1)}, u32[]{:S(2)}, u32[]{:S(2)}) %all-to-all-start.1) | async-done | bytes 1048608 | tf_op jit(solution)/shard_map/all_to_all | solution.py:328
  133.3 7.1 %all-to-all-start.2 = ((bf16[8,176,128]{2,1,0:T(8,128)(2,1)}), bf16[8,176,128]{2,1,0:T(8,128)(2,1)S(1)}, u32[]{:S(2)}, u32[]{:S(2)}) async-start(bf16[8,176,128]{2,1,0:T(8,128)(2,1)} %broadcast_in_dim.25), calls=%async_computation.2 | async-start | bytes 720896 | tf_op jit(solution)/shard_map/all_to_all | solution.py:354
  140.4 8.5 %table_grads.1.value_ref = bf16[32,2,64,128]{3,2,1,0:T(8,128)(2,1)} custom-call(bf16[2,8,2048,256]{3,2,1,0:T(8,128)(2,1)} %get-tuple-element.20.hits_ref, bf16[2048,256]{1,0:T(8,128)(2,1)S(1)} %bitcast.37), custom_call_target="tpu_custom_call" | custom-call | flops 2147483648 | bytes 18874368 | tf_op jit(solution)/shard_map/table_grads/pallas_call | solution.py:103
  148.8 4.1 %all-to-all-done.2 = bf16[8,176,128]{2,1,0:T(8,128)(2,1)S(1)} async-done(((bf16[8,176,128]{2,1,0:T(8,128)(2,1)}), bf16[8,176,128]{2,1,0:T(8,128)(2,1)S(1)}, u32[]{:S(2)}, u32[]{:S(2)}) %all-to-all-start.2) | async-done | bytes 360480 | tf_op jit(solution)/shard_map/all_to_all | solution.py:354
  153.0 6.2 %all-to-all-start.3 = ((bf16[32,2,64,128]{3,2,1,0:T(8,128)(2,1)}), bf16[32,2,64,128]{3,2,1,0:T(8,128)(2,1)S(1)}, u32[]{:S(2)}, u32[]{:S(2)}) async-start(bf16[32,2,64,128]{3,2,1,0:T(8,128)(2,1)} %hold.1), calls=%async_computation.3 | async-start | bytes 2097152 | tf_op jit(solution)/shard_map/all_to_all | solution.py:359
  159.2 1.9 collective-permute-start.7
  161.1 6.3 %collective-permute-start.6 = (bf16[176,128]{1,0:T(8,128)(2,1)S(1)}, bf16[176,128]{1,0:T(8,128)(2,1)S(1)}, u32[]{:S(2)}, u32[]{:S(2)}) collective-permute-start(bf16[176,128]{1,0:T(8,128)(2,1)S(1)} %convert_element_type.58), channel_id=1, source_target_pairs={{0,8},{4,12},{8,0},{12,4},{1,9},{5,13},{9,1},{13,5},{2,10},{6,14},... | collective-permute-start | bytes 135176 | tf_op jit(solution)/shard_map/ppermute | solution.py:364
  167.4 3.2 %collective-permute-start.5 = (bf16[176,128]{1,0:T(8,128)(2,1)S(1)}, bf16[176,128]{1,0:T(8,128)(2,1)S(1)}, u32[]{:S(2)}, u32[]{:S(2)}) collective-permute-start(bf16[176,128]{1,0:T(8,128)(2,1)S(1)} %convert_element_type.58), channel_id=1, source_target_pairs={{0,4},{4,0},{8,12},{12,8},{1,5},{5,1},{9,13},{13,9},{2,6},{6,2},{1... | collective-permute-start | bytes 135176 | tf_op jit(solution)/shard_map/ppermute | solution.py:364
  170.6 3.2 %collective-permute-done.5 = bf16[176,128]{1,0:T(8,128)(2,1)S(1)} collective-permute-done((bf16[176,128]{1,0:T(8,128)(2,1)S(1)}, bf16[176,128]{1,0:T(8,128)(2,1)S(1)}, u32[]{:S(2)}, u32[]{:S(2)}) %collective-permute-start.5) | collective-permute-done | bytes 45088 | tf_op jit(solution)/shard_map/ppermute | solution.py:364
  173.9 4.1 %collective-permute-start.8 = (bf16[176,128]{1,0:T(8,128)(2,1)S(1)}, bf16[176,128]{1,0:T(8,128)(2,1)S(1)}, u32[]{:S(2)}, u32[]{:S(2)}) collective-permute-start(bf16[176,128]{1,0:T(8,128)(2,1)S(1)} %add_convert_fusion), channel_id=1, source_target_pairs={{0,1},{1,0},{2,3},{3,2},{4,5},{5,4},{6,7},{7,6},{8,9},{9,8},{10,11... | collective-permute-start | bytes 135176 | tf_op jit(solution)/shard_map/ppermute | solution.py:368
  178.8 11.1 %all_gather.7.whole = bf16[1408,128]{1,0:T(8,128)(2,1)S(1)} all-gather(bf16[352,128]{1,0:T(8,128)(2,1)S(1)} %bitcast.48), channel_id=1, replica_groups=mesh['x'=4,'zh'=4,'zl'=2,'yh'=4,'yl'=2,'c'=2] {'x'}, dimensions={0}, use_global_device_ids=true | all-gather | bytes 450560 | tf_op jit(solution)/shard_map/all_gather | solution.py:370
  (66 shorter events, 21.7 us)
Async XLA Ops:
  7.2 84.0 %all-gather.2.cloned.1.call-start = ((), (), s32[]{:S(2)}) async-start(), calls=%async_computation.4 | async-start | bytes 7520256 | tf_op jit(solution)/shard_map/all_gather | solution.py:310
  10.5 1.2 copy-start
  23.8 80.7 %copy-start.2 = (bf16[512,256]{1,0:T(8,128)(2,1)S(1)}, bf16[512,256]{1,0:T(8,128)(2,1)}, u32[]{:S(2)}) copy-start(bf16[512,256]{1,0:T(8,128)(2,1)} %w2.3) | copy-start | bytes 786436
  23.8 80.7 %copy-start.4 = (bf16[256,128]{1,0:T(8,128)(2,1)S(1)}, bf16[256,128]{1,0:T(8,128)(2,1)}, u32[]{:S(2)}) copy-start(bf16[256,128]{1,0:T(8,128)(2,1)} %w3.3) | copy-start | bytes 196612
  23.8 80.7 %copy-start.7 = (bf16[13,512]{1,0:T(8,128)(2,1)S(1)}, bf16[13,512]{1,0:T(8,128)(2,1)}, u32[]{:S(2)}) copy-start(bf16[13,512]{1,0:T(8,128)(2,1)} %w1.3) | copy-start | bytes 39940
  23.8 80.7 %copy-start.11 = (f32[512]{0:T(512)S(1)}, f32[512]{0:T(512)}, u32[]{:S(2)}) copy-start(f32[512]{0:T(512)} %param.21) | copy-start | bytes 6148
  23.9 80.7 %copy-start.13 = (f32[256]{0:T(256)S(1)}, f32[256]{0:T(256)}, u32[]{:S(2)}) copy-start(f32[256]{0:T(256)} %param.23) | copy-start | bytes 3076
  23.9 80.7 %copy-start.15 = (f32[128]{0:T(128)S(1)}, f32[128]{0:T(128)}, u32[]{:S(2)}) copy-start(f32[128]{0:T(128)} %param.25) | copy-start | bytes 1540
  23.9 48.2 %all-to-all-start = ((bf16[16,128,256]{2,1,0:T(8,128)(2,1)}), bf16[16,128,256]{2,1,0:T(8,128)(2,1)S(1)}, u32[]{:S(2)}, u32[]{:S(2)}) async-start(bf16[16,128,256]{2,1,0:T(8,128)(2,1)} %bitcast.2), calls=%async_computation | async-start | bytes 2097152 | tf_op jit(solution)/shard_map/all_to_all | solution.py:313
  36.5 1.0 copy-start.1
  37.4 0.9 copy-start.3
  72.1 19.1 %copy-start.16 = (bf16[16,128,256]{2,1,0:T(8,128)(2,1)}, bf16[16,128,256]{2,1,0:T(8,128)(2,1)S(1)}, u32[]{:S(2)}) copy-start(bf16[16,128,256]{2,1,0:T(8,128)(2,1)S(1)} %all-to-all-done.arrived_ref) | copy-start | bytes 3145732
  99.8 32.7 %all-to-all-start.1 = ((bf16[16,128,256]{2,1,0:T(8,128)(2,1)}), bf16[16,128,256]{2,1,0:T(8,128)(2,1)S(1)}, u32[]{:S(2)}, u32[]{:S(2)}) async-start(bf16[16,128,256]{2,1,0:T(8,128)(2,1)} %get-tuple-element.22), calls=%async_computation.1 | async-start | bytes 2097152 | tf_op jit(solution)/shard_map/all_to_all | solution.py:328
  107.0 3.3 %collective-permute-start = (bf16[4,176,128]{2,1,0:T(8,128)(2,1)S(1)}, bf16[4,176,128]{2,1,0:T(8,128)(2,1)S(1)}, u32[]{:S(2)}, u32[]{:S(2)}) collective-permute-start(bf16[4,176,128]{2,1,0:T(8,128)(2,1)S(1)} %dynamic-slice_bitcast_fusion), channel_id=1, source_target_pairs={{0,1},{1,0},{2,3},{3,2},{4,5},{5,4},{6,7},{7,6},{8,9},{9,8},{10,11... | collective-permute-start | bytes 540680 | tf_op jit(solution)/shard_map/ppermute | solution.py:342
  110.4 9.3 %collective-permute-start.3 = (bf16[176,128]{1,0:T(8,128)(2,1)S(1)}, bf16[176,128]{1,0:T(8,128)(2,1)S(1)}, u32[]{:S(2)}, u32[]{:S(2)}) collective-permute-start(bf16[176,128]{1,0:T(8,128)(2,1)S(1)} %get-tuple-element.35), channel_id=1, source_target_pairs={{0,384},{128,0},{256,128},{384,256},{1,385},{129,1},{257,129},{385... | collective-permute-start | bytes 135176 | tf_op jit(solution)/shard_map/ppermute | solution.py:349
  114.7 6.6 %collective-permute-start.2 = (bf16[176,128]{1,0:T(8,128)(2,1)S(1)}, bf16[176,128]{1,0:T(8,128)(2,1)S(1)}, u32[]{:S(2)}, u32[]{:S(2)}) collective-permute-start(bf16[176,128]{1,0:T(8,128)(2,1)S(1)} %get-tuple-element.36), channel_id=1, source_target_pairs={{0,256},{128,384},{256,0},{384,128},{1,257},{129,385},{257,1},{385... | collective-permute-start | bytes 135176 | tf_op jit(solution)/shard_map/ppermute | solution.py:349
  117.2 6.3 %collective-permute-start.1 = (bf16[176,128]{1,0:T(8,128)(2,1)S(1)}, bf16[176,128]{1,0:T(8,128)(2,1)S(1)}, u32[]{:S(2)}, u32[]{:S(2)}) collective-permute-start(bf16[176,128]{1,0:T(8,128)(2,1)S(1)} %get-tuple-element.34), channel_id=1, source_target_pairs={{0,128},{128,256},{256,384},{384,0},{1,129},{129,257},{257,385},{3... | collective-permute-start | bytes 135176 | tf_op jit(solution)/shard_map/ppermute | solution.py:349
  123.5 5.1 %collective-permute-start.4 = (bf16[176,128]{1,0:T(8,128)(2,1)S(1)}, bf16[176,128]{1,0:T(8,128)(2,1)S(1)}, u32[]{:S(2)}, u32[]{:S(2)}) collective-permute-start(bf16[176,128]{1,0:T(8,128)(2,1)S(1)} %fusion.3.one_ref), channel_id=1, source_target_pairs={{0,16},{16,0},{1,17},{17,1},{2,18},{18,2},{3,19},{19,3},{4,20},{20... | collective-permute-start | bytes 135176 | tf_op jit(solution)/shard_map/ppermute | solution.py:263
  133.3 19.7 %all-to-all-start.2 = ((bf16[8,176,128]{2,1,0:T(8,128)(2,1)}), bf16[8,176,128]{2,1,0:T(8,128)(2,1)S(1)}, u32[]{:S(2)}, u32[]{:S(2)}) async-start(bf16[8,176,128]{2,1,0:T(8,128)(2,1)} %broadcast_in_dim.25), calls=%async_computation.2 | async-start | bytes 720896 | tf_op jit(solution)/shard_map/all_to_all | solution.py:354
  153.0 38.5 %all-to-all-start.3 = ((bf16[32,2,64,128]{3,2,1,0:T(8,128)(2,1)}), bf16[32,2,64,128]{3,2,1,0:T(8,128)(2,1)S(1)}, u32[]{:S(2)}, u32[]{:S(2)}) async-start(bf16[32,2,64,128]{3,2,1,0:T(8,128)(2,1)} %hold.1), calls=%async_computation.3 | async-start | bytes 2097152 | tf_op jit(solution)/shard_map/all_to_all | solution.py:359
  159.2 11.4 %collective-permute-start.7 = (bf16[176,128]{1,0:T(8,128)(2,1)S(1)}, bf16[176,128]{1,0:T(8,128)(2,1)S(1)}, u32[]{:S(2)}, u32[]{:S(2)}) collective-permute-start(bf16[176,128]{1,0:T(8,128)(2,1)S(1)} %convert_element_type.58), channel_id=1, source_target_pairs={{0,12},{4,8},{8,4},{12,0},{1,13},{5,9},{9,5},{13,1},{2,14},{6,10},... | collective-permute-start | bytes 135176 | tf_op jit(solution)/shard_map/ppermute | solution.py:364
  161.1 9.5 %collective-permute-start.6 = (bf16[176,128]{1,0:T(8,128)(2,1)S(1)}, bf16[176,128]{1,0:T(8,128)(2,1)S(1)}, u32[]{:S(2)}, u32[]{:S(2)}) collective-permute-start(bf16[176,128]{1,0:T(8,128)(2,1)S(1)} %convert_element_type.58), channel_id=1, source_target_pairs={{0,8},{4,12},{8,0},{12,4},{1,9},{5,13},{9,1},{13,5},{2,10},{6,14},... | collective-permute-start | bytes 135176 | tf_op jit(solution)/shard_map/ppermute | solution.py:364
  167.4 6.4 %collective-permute-start.5 = (bf16[176,128]{1,0:T(8,128)(2,1)S(1)}, bf16[176,128]{1,0:T(8,128)(2,1)S(1)}, u32[]{:S(2)}, u32[]{:S(2)}) collective-permute-start(bf16[176,128]{1,0:T(8,128)(2,1)S(1)} %convert_element_type.58), channel_id=1, source_target_pairs={{0,4},{4,0},{8,12},{12,8},{1,5},{5,1},{9,13},{13,9},{2,6},{6,2},{1... | collective-permute-start | bytes 135176 | tf_op jit(solution)/shard_map/ppermute | solution.py:364
  173.9 5.0 %collective-permute-start.8 = (bf16[176,128]{1,0:T(8,128)(2,1)S(1)}, bf16[176,128]{1,0:T(8,128)(2,1)S(1)}, u32[]{:S(2)}, u32[]{:S(2)}) collective-permute-start(bf16[176,128]{1,0:T(8,128)(2,1)S(1)} %add_convert_fusion), channel_id=1, source_target_pairs={{0,1},{1,0},{2,3},{3,2},{4,5},{5,4},{6,7},{7,6},{8,9},{9,8},{10,11... | collective-permute-start | bytes 135176 | tf_op jit(solution)/shard_map/ppermute | solution.py:368
  (7 other events, 4.8 us)
Sparse Core Ops, SparseCore 0:
  10.7 80.4 all-gather.1
